TPU v7x, 32 devices: a whole 2x2x4 slice. The times are simulated.
32 devices in a mesh: tm: 8 (over z, y), dom: 4 (over x, core).
Axes of the slice: x: 2, y: 2, z: 4, core: 2. Of those that a mesh axis runs over, the one named last changes fastest.
Arguments:
- starting_voltage_guess: float32 [128, 4, 128], P('tm', 'dom'), may hold values from -3 to 3
- injected_amperes: float32 [128, 4, 128], P('tm', 'dom'), may hold values from -6 to 6
- capacitance: float32 [4, 128], P('dom'), may hold values from 0.5 to 2
- conductance: float32 [4, 128, 128], P('dom'), may hold values from -0.5 to 0.5
- block_pattern: int32 [4, 1, 1], P('dom'), may hold values 0 or 1
- device_gain: float32 [4, 128], P('dom'), may hold values from 0.2 to 2
- link_weight: float32 [4, 128, 128], P('dom'), may hold values from -0.5 to 0.5
- boundary_vertex_list: int32 [4, 128], P('dom'), may hold values from 0 to 127, as said below
- diagonal_reciprocals: float32 [128, 4, 1, 128, 128], P('tm', 'dom')
- boundary_jacobian: float32 [4, 128, 128], P('dom'), may hold values from -6 to 6
- transfer: float32 [128, 4, 1, 128, 128], P('tm', 'dom')
Outputs:
- periodic_state: float32 [128, 4, 128], P('tm', 'dom')
Inputs may be any that keep to these rules, and one draw needn't show every extreme that they name: `boundary_vertex_list`: the 128 interface nodes of one partition are distinct.
All inputs are finite; a program needn't handle non-finite values. No bound on the sum of `block_pattern` on one device may be relied on, other than what follows from the above.
Results may differ from a plain program's by a relative error of at most 0.0003.
Values sent between devices are 32-bit elements; how exact they have to be, the bound alone decides.
No kernel may reach another device: no remote copies, remote signals or barrier semaphores. Data moves between devices by JAX's collectives and lax.ppermute only.
A program may use at most 64 MiB of HBM per device.

v0:
```python
import functools

import jax
import jax.numpy as jnp
from jax import lax
from jax.experimental import pallas as pl
from jax.experimental.pallas import tpu as pltpu
from jax.sharding import PartitionSpec as P

F32 = jnp.float32
BF16 = jnp.bfloat16
PAIR = 2


def halves(x):
    hi = x.astype(BF16)
    return hi, (x - hi.astype(F32)).astype(BF16)


def split_cols(matrix):
    return jnp.concatenate(halves(matrix), axis=1)


def split_rows(vectors):
    hi, lo = halves(vectors)
    hi, lo = hi.astype(F32), lo.astype(F32)
    top = jnp.concatenate([hi, hi], axis=1)
    low = jnp.concatenate([lo, jnp.zeros_like(lo)], axis=1)
    return jnp.concatenate([top, low], axis=0).astype(BF16)


def dot_nt(a, b):
    return lax.dot_general(a, b, (((1,), (1,)), ((), ())), preferred_element_type=F32)


def times(a, b):
    ah, al = halves(a)
    bh, bl = halves(b)
    left = jnp.concatenate([ah, al, ah], axis=1)
    right = jnp.concatenate([bh, bh, bl], axis=0)
    return jnp.dot(left, right, preferred_element_type=F32)


def mapped(matrix_split, vectors):
    count = vectors.shape[0]
    both = dot_nt(split_rows(vectors), matrix_split)
    return both[:count] + both[count:]


def mapped_each(matrices, vectors):
    rows = []
    for r in range(vectors.shape[0]):
        products = matrices[r] * vectors[r : r + 1, :]
        rows.append(jnp.sum(products.T, axis=0, keepdims=True))
    return jnp.concatenate(rows, axis=0)


def call(kernel, outs, *args, cost=None):
    vmem = pl.BlockSpec(memory_space=pltpu.VMEM)
    return pl.pallas_call(
        kernel,
        out_shape=[jax.ShapeDtypeStruct(s, d) for s, d in outs],
        in_specs=[vmem] * len(args),
        out_specs=[vmem] * len(outs),
        cost_estimate=cost,
        compiler_params=pltpu.CompilerParams(vmem_limit_bytes=24 * 2**20),
    )(*args)


def identity(width):
    return (
        lax.broadcasted_iota(jnp.int32, (width, width), 0)
        == lax.broadcasted_iota(jnp.int32, (width, width), 1)
    ).astype(F32)


def halo_kernel(s_ref, near_ref, msg_ref):
    points, width = s_ref.shape
    msg_ref[:4] = jnp.broadcast_to(near_ref[points - 1 :], (4, width))
    msg_ref[4:] = jnp.broadcast_to(s_ref[points - 1 :], (4, width))


def ones_kernel(one_ref):
    one_ref[...] = jnp.ones(one_ref.shape, F32)


def pack_kernel(one_ref, g_ref, mask_ref, k_ref, j_ref, inj_ref, cap_ref, gain_ref, bnd_ref, pack_ref):
    points, width = inj_ref.shape
    pack_ref[:width] = g_ref[...] * (mask_ref[...] * one_ref[...])
    pack_ref[width : 2 * width] = k_ref[...]
    pack_ref[2 * width : 3 * width] = j_ref[...]
    at = 3 * width
    pack_ref[at : at + points] = inj_ref[...]
    at += points
    for one in (cap_ref[...], gain_ref[...], bnd_ref[...].astype(F32)):
        pack_ref[at : at + 8] = jnp.broadcast_to(one, (8, width))
        at += 8


def unpacked(pack_ref, points):
    width = pack_ref.shape[1]
    at = 3 * width
    inj = pack_ref[at : at + points]
    at += points
    cap, gain, bnd = (pack_ref[at + 8 * i : at + 8 * i + 1] for i in range(3))
    return inj, cap, gain, bnd.astype(jnp.int32)


def suffix_kernel(lo_ref, hi_ref, s_ref, w_ref):
    points, width = lo_ref.shape[0], lo_ref.shape[1]
    for g, r_ref in enumerate((lo_ref, hi_ref)):
        u = [r_ref[i] for i in range(points)]
        span = 1
        while span < points:
            for base in range(0, points, 2 * span):
                prod = times(u[base + span], jnp.concatenate(u[base : base + span], axis=1))
                for i in range(span):
                    u[base + i] = prod[:, i * width : (i + 1) * width]
            span *= 2
        w_ref[g * width : (g + 1) * width] = u[0]
        for i in range(points - 1):
            s_ref[g * points + i] = u[i + 1]
        s_ref[(g + 1) * points - 1] = identity(width)


def prefix_kernel(lo_ref, hi_ref, p_ref, l_ref):
    points, width = lo_ref.shape[0], lo_ref.shape[1]
    slot = 0
    for g, r_ref in enumerate((lo_ref, hi_ref)):
        q = [r_ref[i] for i in range(points)]
        span = 1
        while span < points:
            for base in range(0, points, 2 * span):
                upper = q[base + span : base + 2 * span]
                for matrix in upper:
                    l_ref[slot] = matrix
                    slot += 1
                prod = times(jnp.concatenate(upper, axis=0), q[base + span - 1])
                for i in range(span):
                    q[base + span + i] = prod[i * width : (i + 1) * width]
            span *= 2
        for i in range(points):
            p_ref[g * points + i] = q[i]


def scanned(c, l_ref, slot):
    points = c.shape[0]
    x = [c[i : i + 1, :] for i in range(points)]
    span = 1
    while span < points:
        for base in range(0, points, 2 * span):
            head = x[base + span - 1]
            for i in range(base + span, base + 2 * span):
                x[i] = x[i] + mapped_each(l_ref[slot : slot + 1], head)
                slot += 1
        span *= 2
    return jnp.concatenate(x, axis=0)


def taken(rows, lanes):
    return jnp.take_along_axis(rows, jnp.broadcast_to(lanes, rows.shape), axis=1)


def negative_residual(s, halo, inj, cap, gain, gs):
    before = jnp.concatenate([halo, s[: s.shape[0] - 1]], axis=0)
    return inj - cap * (s - before) - mapped(gs, s) - gain * jnp.tanh(s)


def corrected(nr, c_before, s_before, d_ref, js, ks):
    return mapped_each(d_ref, nr + mapped(js, c_before) + mapped(ks, s_before))


def pair_corrected(nr, s_lo, c_lo, bnd_lo, d_hi_ref, js, ks):
    return corrected(nr, taken(c_lo, bnd_lo), taken(s_lo, bnd_lo), d_hi_ref, js, ks)


def correct_both(
    s_lo, s_hi, halo_lo, halo_hi, pack_lo, pack_hi, lo_maps, hi_maps, d_lo, d_hi, nr_ref, c_ref, msg_ref
):
    points = s_lo.shape[0]
    inj_lo, cap_lo, gain_lo, bnd_lo = unpacked(pack_lo, points)
    inj_hi, cap_hi, gain_hi, bnd_hi = unpacked(pack_hi, points)
    nr_lo = negative_residual(s_lo, halo_lo, inj_lo, cap_lo, gain_lo, lo_maps[0])
    nr_hi = negative_residual(s_hi, halo_hi, inj_hi, cap_hi, gain_hi, hi_maps[0])
    c_lo = mapped_each(d_lo, nr_lo)
    c_hi = pair_corrected(nr_hi, s_lo, c_lo, bnd_lo, d_hi, hi_maps[2], hi_maps[1])
    nr_ref[:points], nr_ref[points:] = nr_lo, nr_hi
    c_ref[:points], c_ref[points:] = c_lo, c_hi
    msg_ref[:points] = taken(c_hi, bnd_hi)
    msg_ref[points:] = taken(s_hi, bnd_hi)


def early_kernel(s_lo, s_hi, pack_lo, pack_hi, d_lo, d_hi, maps_ref, nr_ref, c_ref, msg_ref):
    points, width = s_lo.shape
    for i in range(3):
        rows = slice(i * width, (i + 1) * width)
        maps_ref[i] = split_cols(pack_lo[rows])
        maps_ref[3 + i] = split_cols(pack_hi[rows])
    none = jnp.zeros((1, width), F32)
    correct_both(
        s_lo[...], s_hi[...], none, none, pack_lo, pack_hi,
        [maps_ref[i] for i in range(3)], [maps_ref[i] for i in range(3, 6)],
        d_lo, d_hi, nr_ref, c_ref, msg_ref,
    )


def first_kernel(
    halo_ref, s_lo, s_hi, pack_lo, pack_hi, maps_ref, d_lo, d_hi, old_nr, old_c, old_msg,
    s_ref, nr_ref, c_ref, msg_ref,
):
    points = s_lo.shape[0]
    _, cap_lo, _, bnd_lo = unpacked(pack_lo, points)
    _, cap_hi, _, bnd_hi = unpacked(pack_hi, points)
    s_ref[:points], s_ref[points:] = s_lo[...], s_hi[...]
    nr_ref[...], c_ref[...], msg_ref[...] = old_nr[...], old_c[...], old_msg[...]
    nr_lo = old_nr[:1] + cap_lo * halo_ref[:1]
    nr_hi = old_nr[points : points + 1] + cap_hi * halo_ref[4:5]
    c_lo = mapped_each(d_lo, nr_lo)
    came = mapped(maps_ref[5], taken(jnp.broadcast_to(c_lo, (8, c_lo.shape[1])), bnd_lo))
    came = came + mapped(maps_ref[4], taken(s_lo[:8], bnd_lo))
    c_hi = mapped_each(d_hi, nr_hi + came[:1])
    nr_ref[:1], nr_ref[points : points + 1] = nr_lo, nr_hi
    c_ref[:1], c_ref[points : points + 1] = c_lo, c_hi
    msg_ref[:1] = taken(jnp.broadcast_to(c_hi, (8, c_hi.shape[1])), bnd_hi)[:1]


def second_kernel(
    got_ref, s_ref, nr_ref, c_ref, pack_lo, maps_ref, d_lo, d_hi, ss_ref, new_c_ref, tail_ref, f_ref
):
    points, width = got_ref.shape[0] // 2, got_ref.shape[1]
    second_pair = lax.axis_index("dom") >= PAIR

    @pl.when(second_pair)
    def _():
        bnd_lo = unpacked(pack_lo, points)[3]
        c_lo = corrected(
            nr_ref[:points], got_ref[:points], got_ref[points:], d_lo, maps_ref[2], maps_ref[1]
        )
        new_c_ref[:points] = c_lo
        new_c_ref[points:] = pair_corrected(
            nr_ref[points:], s_ref[:points], c_lo, bnd_lo, d_hi, maps_ref[5], maps_ref[4]
        )

    @pl.when(jnp.logical_not(second_pair))
    def _():
        new_c_ref[...] = c_ref[...]

    each = mapped_each(ss_ref, new_c_ref[...])
    for g in range(PAIR):
        total = each[g * points : (g + 1) * points]
        shift = 1
        while shift < points:
            total = total + jnp.concatenate(
                [total[shift:], jnp.zeros((shift, width), F32)], axis=0
            )
            shift *= 2
        at = g * (points + 8)
        tail_ref[at : at + points] = jnp.concatenate(
            [total[1:], jnp.zeros((1, width), F32)], axis=0
        )
        whole = jnp.broadcast_to(total[:1], (8, width))
        tail_ref[at + points : at + points + 8] = whole
        f_ref[8 * g : 8 * g + 8] = whole


def is_later(distance):
    return (lax.axis_index("tm") // distance) % 2 == 1


def sections(width):
    return [
        (slice(g * width, (g + 1) * width), slice(8 * g, 8 * g + 8)) for g in range(PAIR)
    ]


def first_level_kernel(
    distance, mw_ref, mf_ref, got_ref, tw_ref, tf_ref, a_ref, bw_ref, bf_ref, aw_ref, af_ref
):
    width = mw_ref.shape[1]
    later = is_later(distance)
    eye = identity(width)
    for wide, short in sections(width):
        mw, mf, gw = mw_ref[wide], mf_ref[short], got_ref[wide]
        gf = got_ref[PAIR * width + short.start : PAIR * width + short.stop]
        a = jnp.where(later, mw, gw)
        tw_ref[wide] = times(a, jnp.where(later, gw, mw))
        a_split = split_cols(a)
        a_ref[wide] = a_split
        tf_ref[short] = mapped(a_split, jnp.where(later, gf, mf)) + jnp.where(later, mf, gf)
        bw_ref[wide] = jnp.where(later, gw, eye)
        bf_ref[short] = jnp.where(later, gf, 0.0)
        aw_ref[wide] = jnp.where(later, eye, gw)
        af_ref[short] = jnp.where(later, 0.0, gf)


def next_level_kernel(
    distance, mw_ref, mf_ref, got_ref, bw_ref, bf_ref, aw_ref, af_ref,
    tw_ref, tf_ref, a_ref, x_ref, nbw_ref, nbf_ref, naw_ref, naf_ref,
):
    width = mw_ref.shape[1]
    later = is_later(distance)
    for wide, short in sections(width):
        mw, mf, gw = mw_ref[wide], mf_ref[short], got_ref[wide]
        gf = got_ref[PAIR * width + short.start : PAIR * width + short.stop]
        bw, bf, aw, af = bw_ref[wide], bf_ref[short], aw_ref[wide], af_ref[short]
        a = jnp.where(later, mw, gw)
        tw_ref[wide] = times(a, jnp.where(later, gw, mw))
        a_split = split_cols(a)
        a_ref[wide] = a_split
        tf_ref[short] = mapped(a_split, jnp.where(later, gf, mf)) + jnp.where(later, mf, gf)
        x = jnp.where(later, bw, gw)
        joined = times(x, jnp.where(later, gw, aw))
        x_split = split_cols(x)
        x_ref[wide] = x_split
        sums = mapped(x_split, jnp.where(later, gf, af)) + jnp.where(later, bf, gf)
        nbw_ref[wide] = jnp.where(later, joined, bw)
        nbf_ref[short] = jnp.where(later, sums, bf)
        naw_ref[wide] = jnp.where(later, aw, joined)
        naf_ref[short] = jnp.where(later, af, sums)


def again_first_kernel(distance, mf_ref, gf_ref, a_ref, tf_ref, bf_ref, af_ref):
    later = is_later(distance)
    for wide, short in sections(a_ref.shape[0] // PAIR):
        mf, gf = mf_ref[short], gf_ref[short]
        tf_ref[short] = mapped(a_ref[wide], jnp.where(later, gf, mf)) + jnp.where(later, mf, gf)
        bf_ref[short] = jnp.where(later, gf, 0.0)
        af_ref[short] = jnp.where(later, 0.0, gf)


def again_next_kernel(
    distance, mf_ref, gf_ref, bf_ref, af_ref, a_ref, x_ref, tf_ref, nbf_ref, naf_ref
):
    later = is_later(distance)
    for wide, short in sections(a_ref.shape[0] // PAIR):
        mf, gf, bf, af = mf_ref[short], gf_ref[short], bf_ref[short], af_ref[short]
        tf_ref[short] = mapped(a_ref[wide], jnp.where(later, gf, mf)) + jnp.where(later, mf, gf)
        sums = mapped(x_ref[wide], jnp.where(later, gf, af)) + jnp.where(later, bf, gf)
        nbf_ref[short] = jnp.where(later, sums, bf)
        naf_ref[short] = jnp.where(later, af, sums)


def local_kernel(c_ref, ls_ref, tail_ref, aw_ref, af_ref, s_ref, base_ref, v_ref):
    points, width = s_ref.shape[0] // PAIR, s_ref.shape[1]
    for g, (wide, short) in enumerate(sections(width)):
        rows = slice(g * points, (g + 1) * points)
        long = slice(g * (points + 8), (g + 1) * (points + 8))
        slot = g * (ls_ref.shape[0] // PAIR)
        base_ref[rows] = s_ref[rows] + scanned(c_ref[rows], ls_ref, slot)
        v_ref[long] = mapped(split_cols(aw_ref[wide]), tail_ref[long]) + af_ref[short][:1]


def turn_kernel(
    v_ref, got_ref, bw_ref, bf_ref, ps_ref, base_ref, halo_ref, pack_lo, pack_hi, maps_ref,
    d_lo, d_hi, s_ref, nr_ref, c_ref, msg_ref,
):
    points, width = s_ref.shape[0] // PAIR, s_ref.shape[1]
    came = []
    for g, (wide, short) in enumerate(sections(width)):
        long = slice(g * (points + 8), (g + 1) * (points + 8))
        gf = got_ref[PAIR * width + 8 * g : PAIR * width + 8 * g + 1]
        v = mapped(split_cols(got_ref[wide]), v_ref[long]) + gf
        came.append(mapped(split_cols(bw_ref[wide]), v) + bf_ref[short][:1])
    moved = mapped_each(ps_ref, jnp.concatenate([v[:points] for v in came], axis=0))
    s = base_ref[...] + moved
    s_ref[...] = s
    correct_both(
        s[:points], s[points:],
        halo_ref[:1] + came[0][points : points + 1],
        halo_ref[4:5] + came[1][points : points + 1],
        pack_lo, pack_hi, [maps_ref[i] for i in range(3)], [maps_ref[i] for i in range(3, 6)],
        d_lo, d_hi, nr_ref, c_ref, msg_ref,
    )


def last_local_kernel(
    c_ref, ls_ref, tail_ref, aw_ref, af_ref, gw_ref, bw_ref, bf_ref, ps_ref, s_ref, base_ref
):
    points, width = s_ref.shape[0] // PAIR, s_ref.shape[1]
    came = []
    for g, (wide, short) in enumerate(sections(width)):
        at = g * (points + 8)
        v = mapped(split_cols(aw_ref[wide]), tail_ref[at : at + points]) + af_ref[short][:1]
        v = mapped(split_cols(gw_ref[wide]), v)
        came.append(mapped(split_cols(bw_ref[wide]), v) + bf_ref[short][:1])
    moved = mapped_each(ps_ref, jnp.concatenate(came, axis=0))
    for g in range(PAIR):
        rows = slice(g * points, (g + 1) * points)
        slot = g * (ls_ref.shape[0] // PAIR)
        base_ref[rows] = s_ref[rows] + moved[rows] + scanned(c_ref[rows], ls_ref, slot)


def end_kernel(gf_ref, bw_ref, ps_ref, base_ref, s_ref):
    points, width = s_ref.shape[0] // PAIR, s_ref.shape[1]
    came = []
    for wide, short in sections(width):
        v = mapped(split_cols(bw_ref[wide]), gf_ref[short])[:1]
        came.append(jnp.broadcast_to(v, (points, width)))
    s_ref[...] = base_ref[...] + mapped_each(ps_ref, jnp.concatenate(came, axis=0))


def choose_kernel(both_ref, got_ref, s_ref):
    points = s_ref.shape[0]
    odd = lax.axis_index("dom") % 2 == 1
    s_ref[...] = jnp.where(odd, both_ref[points:], got_ref[:points])


def exchanged(value, distance):
    return lax.ppermute(
        value, "tm", [(i, i ^ distance) for i in range(lax.axis_size("tm"))]
    )


def swapped(value, distance):
    return lax.ppermute(value, "dom", [(i, i ^ distance) for i in range(lax.axis_size("dom"))])


def both_partitions(s, nr, c, msg, halo, maps, pack_lo, pack_hi, d_lo, d_hi, r_lo, r_hi):
    points, width = s.shape[0] // PAIR, s.shape[1]
    vec, square = ((PAIR * points, width), F32), ((PAIR * width, width), F32)
    square_split = ((PAIR * width, 2 * width), BF16)
    eight = ((PAIR * 8, width), F32)
    longer = ((PAIR * (points + 8), width), F32)
    many = ((PAIR * points, width, width), F32)
    steps = (points.bit_length() - 1) * points // 2
    distances = [2**k for k in range(lax.axis_size("tm").bit_length() - 1)]

    got = swapped(msg, 2)
    ss, w = call(suffix_kernel, [many, square], r_lo, r_hi)
    ps, ls = call(prefix_kernel, [many, ((PAIR * steps, width, width), F32)], r_lo, r_hi)
    c, tail, f = call(
        second_kernel, [vec, longer, eight], got, s, nr, c, pack_lo, maps, d_lo, d_hi, ss
    )
    kept = []
    for level, distance in enumerate(distances[:-1]):
        got = exchanged(jnp.concatenate([w, f], axis=0), distance)
        if level == 0:
            w, f, a, bw, bf, aw, af = call(
                functools.partial(first_level_kernel, distance),
                [square, eight, square_split, square, eight, square, eight], w, f, got,
            )
            kept.append((a,))
        else:
            w, f, a, x, bw, bf, aw, af = call(
                functools.partial(next_level_kernel, distance),
                [square, eight, square_split, square_split, square, eight, square, eight],
                w, f, got, bw, bf, aw, af,
            )
            kept.append((a, x))
    last = exchanged(jnp.concatenate([w, f], axis=0), distances[-1])
    base, v = call(local_kernel, [vec, longer], c, ls, tail, aw, af, s)
    s, nr, c, msg = call(
        turn_kernel, [vec] * 4,
        v, last, bw, bf, ps, base, halo, pack_lo, pack_hi, maps, d_lo, d_hi,
    )
    got = swapped(msg, 2)
    c, tail, f = call(
        second_kernel, [vec, longer, eight], got, s, nr, c, pack_lo, maps, d_lo, d_hi, ss
    )
    for level, distance in enumerate(distances[:-1]):
        got = exchanged(f, distance)
        if level == 0:
            f, bf, af = call(
                functools.partial(again_first_kernel, distance), [eight] * 3, f, got, *kept[0]
            )
        else:
            f, bf, af = call(
                functools.partial(again_next_kernel, distance), [eight] * 3,
                f, got, bf, af, *kept[level],
            )
    got = exchanged(f, distances[-1])
    (base,) = call(last_local_kernel, [vec], c, ls, tail, aw, af, last, bw, bf, ps, s)
    return call(end_kernel, [vec], got, bw, ps, base)[0]


def per_device(
    starting_voltage_guess,
    injected_amperes,
    capacitance,
    conductance,
    block_pattern,
    device_gain,
    link_weight,
    boundary_vertex_list,
    diagonal_reciprocals,
    boundary_jacobian,
    transfer,
):
    points, _, width = starting_voltage_guess.shape
    segments = lax.axis_size("tm")
    (one,) = call(
        ones_kernel, [((1, width), F32)],
        cost=pl.CostEstimate(flops=2**33, bytes_accessed=2**25, transcendentals=0),
    )
    mask = jnp.broadcast_to(block_pattern[0].astype(F32), (1, width))
    s = starting_voltage_guess[:, 0]
    near_s = swapped(starting_voltage_guess, 1)[:, 0]
    d, r, near_s, mask, one = lax.optimization_barrier(
        (diagonal_reciprocals, transfer, near_s, mask, one)
    )
    d, near_d = d[:, 0, 0], swapped(d, 1)[:, 0, 0]
    r, near_r = r[:, 0, 0], swapped(r, 1)[:, 0, 0]
    (rows,) = call(halo_kernel, [((8, width), F32)], s, near_s)
    halo = lax.ppermute(rows, "tm", [(i, (i + 1) % segments) for i in range(segments)])
    (pack,) = call(
        pack_kernel, [((3 * width + points + 24, width), F32)],
        one, conductance[0], mask, link_weight[0], boundary_jacobian[0],
        injected_amperes[:, 0], capacitance, device_gain, boundary_vertex_list,
    )
    near_pack = swapped(pack, 1)
    vec = ((PAIR * points, width), F32)
    maps, nr, c, msg = call(
        early_kernel, [((6, width, 2 * width), BF16), vec, vec, vec],
        near_s, s, near_pack, pack, near_d, d,
    )
    s, nr, c, msg = call(
        first_kernel, [vec] * 4,
        halo, near_s, s, near_pack, pack, maps, near_d, d, nr, c, msg,
    )
    odd = lax.axis_index("dom") % 2 == 1
    both = lax.cond(
        odd,
        both_partitions,
        lambda s, *rest: s,
        s, nr, c, msg, halo, maps, near_pack, pack, near_d, d, near_r, r,
    )
    (s,) = call(choose_kernel, [((points, width), F32)], both, swapped(both, 1))
    return s[:, None]


def solution(mesh):
    in_specs = (
        P("tm", "dom", None),
        P("tm", "dom", None),
        P("dom", None),
        P("dom", None, None),
        P("dom", None, None),
        P("dom", None),
        P("dom", None, None),
        P("dom", None),
        P("tm", "dom", None, None, None),
        P("dom", None, None),
        P("tm", "dom", None, None, None),
    )
    out_specs = P("tm", "dom", None)
    return jax.shard_map(
        per_device, mesh=mesh, in_specs=in_specs, out_specs=out_specs, check_vma=False
    )
```

profile of v0, /device:TPU:0, one launch (start us, length us, event | category | flops | bytes accessed | tf_op | source)
XLA Modules:
  0.0 46.2 jit_solution(5769779425142874327)
XLA Ops:
  0.0 0.0 copy-start.8
  0.0 0.0 copy-start.1
  0.0 0.0 copy-start.2
  0.0 0.0 copy-start.5
  0.0 0.0 copy-start.6
  0.0 0.0 copy-start.7
  0.0 0.0 copy-start
  0.1 0.5 %collective-permute-start.8 = (f32[16,1,128]{2,0,1:T(8,128)}, f32[16,1,128]{2,0,1:T(8,128)S(1)}, u32[]{:S(2)}, u32[]{:S(2)}) collective-permute-start(f32[16,1,128]{2,0,1:T(8,128)} %bitcast.19), channel_id=1, source_target_pairs={{0,1},{1,0},{2,3},{3,2},{4,5},{5,4},{6,7},{7,6},{8,9},{9,8},{10,11... | collective-permute-start | bytes 24584 | tf_op jit(solution)/shard_map/ppermute | solution.py:415
  1.2 0.4 collective-permute-done.8
  1.6 0.0 copy-done.8
  1.6 0.3 collective-permute-start.11
  2.0 0.2 collective-permute-start.12
  2.1 0.0 copy-done.1
  2.1 0.0 copy-done.2
  2.1 0.0 copy-done.3
  2.2 0.0 copy-done.4
  2.2 0.0 copy-done.5
  2.2 0.0 copy-done.6
  2.2 0.0 copy-done.7
  2.2 0.4 collective-permute-start.10
  2.6 0.0 copy-done
  2.6 2.7 %collective-permute-start.9 = (f32[8,128]{1,0:T(8,128)S(1)}, f32[8,128]{1,0:T(8,128)S(1)}, u32[]{:S(2)}, u32[]{:S(2)}) collective-permute-start(f32[8,128]{1,0:T(8,128)S(1)} %shard_map.110), channel_id=1, source_target_pairs={{0,4},{4,8},{8,12},{12,16},{16,20},{20,24},{24,28},{28,0},{1,5},{5... | collective-permute-start | bytes 12296 | tf_op jit(solution)/shard_map/ppermute | solution.py:504
  5.3 0.0 collective-permute-done.10.pack_lo
  5.3 0.0 collective-permute-done.11
  5.3 1.2 %shard_map.112 = (bf16[6,128,256]{2,1,0:T(8,128)(2,1)S(1)}, f32[32,128]{1,0:T(8,128)S(1)}, f32[32,128]{1,0:T(8,128)S(1)}, f32[32,128]{1,0:T(8,128)S(1)}) custom-call(f32[16,128]{1,0:T(8,128)S(1)} %bitcast.24, f32[16,128]{1,0:T(8,128)S(1)} %bitcast.21, f32[424,128]{1,0:T(8,128)S(1)} %collective-permute-done.10.pack_lo, f32[424,128]{1,0:T(8,128)S(1)} %shard_map.111.pack_hi, ...), custom_call_target="tpu_custom_call" | custom-call | tf_op jit(solution)/shard_map/pallas_call | solution.py:60
  6.5 3.4 %collective-permute-done.9.halo_ref = f32[8,128]{1,0:T(8,128)S(1)} collective-permute-done((f32[8,128]{1,0:T(8,128)S(1)}, f32[8,128]{1,0:T(8,128)S(1)}, u32[]{:S(2)}, u32[]{:S(2)}) %collective-permute-start.9) | collective-permute-done | bytes 4128 | tf_op jit(solution)/shard_map/ppermute | solution.py:504
  9.9 0.5 %shard_map.113 = (f32[32,128]{1,0:T(8,128)S(1)}, f32[32,128]{1,0:T(8,128)S(1)}, f32[32,128]{1,0:T(8,128)S(1)}, f32[32,128]{1,0:T(8,128)S(1)}) custom-call(f32[8,128]{1,0:T(8,128)S(1)} %collective-permute-done.9.halo_ref, f32[16,128]{1,0:T(8,128)S(1)} %bitcast.25, f32[16,128]{1,0:T(8,128)S(1)} %bitcast.22, f32[424,128]{1,0:T(8,128)S(1)} %collective-permute-done.10.pack_lo, ...), custom_call_target="tpu_custom_call" | custom-call | tf_op jit(solution)/shard_map/pallas_call | solution.py:60
  10.4 0.0 collective-permute-done.12
  10.4 0.2 conditional.1
  10.6 34.2 %collective-permute-start.13 = (f32[32,128]{1,0:T(8,128)S(1)}, f32[32,128]{1,0:T(8,128)S(1)}, u32[]{:S(2)}, u32[]{:S(2)}) collective-permute-start(f32[32,128]{1,0:T(8,128)S(1)} %get-tuple-element.122.both_ref), channel_id=1, source_target_pairs={{0,1},{1,0},{2,3},{3,2},{4,5},{5,4},{6,7},{7,6},{8,9},{9,8},{10,11... | collective-permute-start | bytes 49160 | tf_op jit(solution)/shard_map/ppermute | solution.py:415
  44.7 0.8 %collective-permute-done.13.got_ref = f32[32,128]{1,0:T(8,128)S(1)} collective-permute-done((f32[32,128]{1,0:T(8,128)S(1)}, f32[32,128]{1,0:T(8,128)S(1)}, u32[]{:S(2)}, u32[]{:S(2)}) %collective-permute-start.13) | collective-permute-done | bytes 16416 | tf_op jit(solution)/shard_map/ppermute | solution.py:415
  45.6 0.6 %shard_map.114 = f32[16,128]{1,0:T(8,128)} custom-call(f32[32,128]{1,0:T(8,128)S(1)} %get-tuple-element.122.both_ref, f32[32,128]{1,0:T(8,128)S(1)} %collective-permute-done.13.got_ref), custom_call_target="tpu_custom_call" | custom-call | tf_op jit(solution)/shard_map/pallas_call | solution.py:60
  (6 shorter events, 0.0 us)
Async XLA Ops:
  0.0 1.6 %copy-start.8 = (f32[16,1,1,128,128]{4,3,2,1,0:T(8,128)S(1)}, f32[16,1,1,128,128]{4,3,2,1,0:T(8,128)}, u32[]{:S(2)}) copy-start(f32[16,1,1,128,128]{4,3,2,1,0:T(8,128)} %param.21) | copy-start | bytes 3145732
  0.0 2.1 %copy-start.1 = (f32[1,128,128]{2,1,0:T(8,128)S(1)}, f32[1,128,128]{2,1,0:T(8,128)}, u32[]{:S(2)}) copy-start(f32[1,128,128]{2,1,0:T(8,128)} %param.16) | copy-start | bytes 196612
  0.0 2.1 %copy-start.2 = (f32[1,128,128]{2,1,0:T(8,128)S(1)}, f32[1,128,128]{2,1,0:T(8,128)}, u32[]{:S(2)}) copy-start(f32[1,128,128]{2,1,0:T(8,128)} %param.19) | copy-start | bytes 196612
  0.0 2.1 %copy-start.3 = (f32[1,128,128]{2,1,0:T(8,128)S(1)}, f32[1,128,128]{2,1,0:T(8,128)}, u32[]{:S(2)}) copy-start(f32[1,128,128]{2,1,0:T(8,128)} %param.22) | copy-start | bytes 196612
  0.0 2.1 %copy-start.4 = (f32[16,1,128]{2,1,0:T(1,128)S(1)}, f32[16,1,128]{2,1,0:T(1,128)}, u32[]{:S(2)}) copy-start(f32[16,1,128]{2,1,0:T(1,128)} %param.14) | copy-start | bytes 24580
  0.0 2.1 %copy-start.5 = (f32[1,128]{1,0:T(1,128)S(1)}, f32[1,128]{1,0:T(1,128)}, u32[]{:S(2)}) copy-start(f32[1,128]{1,0:T(1,128)} %cap_ref.1) | copy-start | bytes 1540
  0.0 2.1 %copy-start.6 = (f32[1,128]{1,0:T(1,128)S(1)}, f32[1,128]{1,0:T(1,128)}, u32[]{:S(2)}) copy-start(f32[1,128]{1,0:T(1,128)} %gain_ref.1) | copy-start | bytes 1540
  0.0 2.1 %copy-start.7 = (s32[1,128]{1,0:T(1,128)S(1)}, s32[1,128]{1,0:T(1,128)}, u32[]{:S(2)}) copy-start(s32[1,128]{1,0:T(1,128)} %bnd_ref.1) | copy-start | bytes 1540
  0.0 2.6 %copy-start = (f32[16,1,128]{2,1,0:T(1,128)S(1)}, f32[16,1,128]{2,1,0:T(1,128)}, u32[]{:S(2)}) copy-start(f32[16,1,128]{2,1,0:T(1,128)} %param.13) | copy-start | bytes 24580
  0.1 1.6 %collective-permute-start.8 = (f32[16,1,128]{2,0,1:T(8,128)}, f32[16,1,128]{2,0,1:T(8,128)S(1)}, u32[]{:S(2)}, u32[]{:S(2)}) collective-permute-start(f32[16,1,128]{2,0,1:T(8,128)} %bitcast.19), channel_id=1, source_target_pairs={{0,1},{1,0},{2,3},{3,2},{4,5},{5,4},{6,7},{7,6},{8,9},{9,8},{10,11... | collective-permute-start | bytes 24584 | tf_op jit(solution)/shard_map/ppermute | solution.py:415
  1.6 3.7 %collective-permute-start.11 = (f32[16,1,1,128,128]{4,3,0,2,1:T(8,128)S(1)}, f32[16,1,1,128,128]{4,3,0,2,1:T(8,128)S(1)}, u32[]{:S(2)}, u32[]{:S(2)}) collective-permute-start(f32[16,1,1,128,128]{4,3,0,2,1:T(8,128)S(1)} %bitcast.30), channel_id=1, source_target_pairs={{0,1},{1,0},{2,3},{3,2},{4,5},{5,4},{6,7},{7,6},{8,9},{9,8},{10,11... | collective-permute-start | bytes 3145736 | tf_op jit(solution)/shard_map/ppermute | solution.py:415
  2.0 8.4 %collective-permute-start.12 = (f32[16,1,1,128,128]{4,3,0,2,1:T(8,128)}, f32[16,1,1,128,128]{4,3,0,2,1:T(8,128)}, u32[]{:S(2)}, u32[]{:S(2)}) collective-permute-start(f32[16,1,1,128,128]{4,3,0,2,1:T(8,128)} %bitcast.15), channel_id=1, source_target_pairs={{0,1},{1,0},{2,3},{3,2},{4,5},{5,4},{6,7},{7,6},{8,9},{9,8},{10,11... | collective-permute-start | bytes 3145736 | tf_op jit(solution)/shard_map/ppermute | solution.py:415
  2.2 3.1 %collective-permute-start.10 = (f32[424,128]{1,0:T(8,128)S(1)}, f32[424,128]{1,0:T(8,128)S(1)}, u32[]{:S(2)}, u32[]{:S(2)}) collective-permute-start(f32[424,128]{1,0:T(8,128)S(1)} %shard_map.111.pack_hi), channel_id=1, source_target_pairs={{0,1},{1,0},{2,3},{3,2},{4,5},{5,4},{6,7},{7,6},{8,9},{9,8},{10,11... | collective-permute-start | bytes 651272 | tf_op jit(solution)/shard_map/ppermute | solution.py:415
  2.6 7.3 %collective-permute-start.9 = (f32[8,128]{1,0:T(8,128)S(1)}, f32[8,128]{1,0:T(8,128)S(1)}, u32[]{:S(2)}, u32[]{:S(2)}) collective-permute-start(f32[8,128]{1,0:T(8,128)S(1)} %shard_map.110), channel_id=1, source_target_pairs={{0,4},{4,8},{8,12},{12,16},{16,20},{20,24},{24,28},{28,0},{1,5},{5... | collective-permute-start | bytes 12296 | tf_op jit(solution)/shard_map/ppermute | solution.py:504
  10.6 35.0 %collective-permute-start.13 = (f32[32,128]{1,0:T(8,128)S(1)}, f32[32,128]{1,0:T(8,128)S(1)}, u32[]{:S(2)}, u32[]{:S(2)}) collective-permute-start(f32[32,128]{1,0:T(8,128)S(1)} %get-tuple-element.122.both_ref), channel_id=1, source_target_pairs={{0,1},{1,0},{2,3},{3,2},{4,5},{5,4},{6,7},{7,6},{8,9},{9,8},{10,11... | collective-permute-start | bytes 49160 | tf_op jit(solution)/shard_map/ppermute | solution.py:415
where the time goes:
time: 46.8 us; the launch traced here: 46.2 us
  starting transfers between devices  38.3 us (82%)
  waiting for transfers between devices  4.66 us (10%)
  Pallas kernels  2.28 us (5%)
  between operations  0.74 us (2%)
    ppermute x5, starting transfers between devices, swapped(): lax.ppermute(value, 'dom', [(i, i ^ distance) for i in range(lax.axis_siz...  35.6 us
    ppermute x1, waiting for transfers between devices, per_device(): lax.ppermute(rows, 'tm', [(i, (i + 1) % segments) for i in range(segments)])  3.43 us
    ppermute x1, starting transfers between devices, per_device(): lax.ppermute(rows, 'tm', [(i, (i + 1) % segments) for i in range(segments)])  2.68 us
    pallas_call x6, Pallas kernels, call(): pl.pallas_call(kernel, out_shape=[jax.ShapeDtypeStruct(s, d) for s, d in...  2.28 us
    ppermute x5, waiting for transfers between devices, swapped(): lax.ppermute(value, 'dom', [(i, i ^ distance) for i in range(lax.axis_siz...  1.23 us
  transfers between devices with their start and end apart: 6, of which 3 were waited for; matrix products, arithmetic and copies ran while one was open for 0% of the time, Pallas kernels for 4%

commit v1 on v0

--- a/solution.py
+++ b/solution.py
@@ -55,13 +55,14 @@
     return jnp.concatenate(rows, axis=0)
 
 
-def call(kernel, outs, *args, cost=None):
+def call(kernel, outs, *args, cost=None, source=pltpu.VMEM, scratch=()):
     vmem = pl.BlockSpec(memory_space=pltpu.VMEM)
     return pl.pallas_call(
         kernel,
         out_shape=[jax.ShapeDtypeStruct(s, d) for s, d in outs],
-        in_specs=[vmem] * len(args),
+        in_specs=[pl.BlockSpec(memory_space=source)] * len(args),
         out_specs=[vmem] * len(outs),
+        scratch_shapes=list(scratch),
         cost_estimate=cost,
         compiler_params=pltpu.CompilerParams(vmem_limit_bytes=24 * 2**20),
     )(*args)
@@ -97,18 +98,35 @@
         at += 8
 
 
-def unpacked(pack_ref, points):
-    width = pack_ref.shape[1]
-    at = 3 * width
-    inj = pack_ref[at : at + points]
+def vectors(small_ref, g, points):
+    at = g * (points + 24)
+    inj = small_ref[at : at + points]
     at += points
-    cap, gain, bnd = (pack_ref[at + 8 * i : at + 8 * i + 1] for i in range(3))
+    cap, gain, bnd = (small_ref[at + 8 * i : at + 8 * i + 1] for i in range(3))
     return inj, cap, gain, bnd.astype(jnp.int32)
 
 
-def suffix_kernel(lo_ref, hi_ref, s_ref, w_ref):
+def whole_kernel(lo_ref, hi_ref, w_ref, r_lo, r_hi, sems):
     points, width = lo_ref.shape[0], lo_ref.shape[1]
-    for g, r_ref in enumerate((lo_ref, hi_ref)):
+    moves = [
+        pltpu.make_async_copy(source, target, sems.at[g])
+        for g, (source, target) in enumerate(((lo_ref, r_lo), (hi_ref, r_hi)))
+    ]
+    for move in moves:
+        move.start()
+    u = []
+    for g, r_ref in enumerate((r_lo, r_hi)):
+        moves[g].wait()
+        u += [times(r_ref[i + 1], r_ref[i]) for i in range(0, points, 2)]
+    while len(u) > PAIR:
+        u = [times(u[i + 1], u[i]) for i in range(0, len(u), 2)]
+    for g in range(PAIR):
+        w_ref[g * width : (g + 1) * width] = u[g]
+
+
+def suffix_kernel(r_lo, r_hi, _, s_ref):
+    points, width = r_lo.shape[0], r_lo.shape[1]
+    for g, r_ref in enumerate((r_lo, r_hi)):
         u = [r_ref[i] for i in range(points)]
         span = 1
         while span < points:
@@ -117,36 +135,33 @@
                 for i in range(span):
                     u[base + i] = prod[:, i * width : (i + 1) * width]
             span *= 2
-        w_ref[g * width : (g + 1) * width] = u[0]
         for i in range(points - 1):
             s_ref[g * points + i] = u[i + 1]
         s_ref[(g + 1) * points - 1] = identity(width)
 
 
-def prefix_kernel(lo_ref, hi_ref, p_ref, l_ref):
-    points, width = lo_ref.shape[0], lo_ref.shape[1]
-    slot = 0
-    for g, r_ref in enumerate((lo_ref, hi_ref)):
-        q = [r_ref[i] for i in range(points)]
-        span = 1
-        while span < points:
-            for base in range(0, points, 2 * span):
-                upper = q[base + span : base + 2 * span]
-                for matrix in upper:
-                    l_ref[slot] = matrix
-                    slot += 1
-                prod = times(jnp.concatenate(upper, axis=0), q[base + span - 1])
-                for i in range(span):
-                    q[base + span + i] = prod[i * width : (i + 1) * width]
-            span *= 2
-        for i in range(points):
-            p_ref[g * points + i] = q[i]
-
-
-def scanned(c, l_ref, slot):
+def prefix_kernel(r_ref, p_ref, l_ref):
+    points, width = r_ref.shape[0], r_ref.shape[1]
+    q = [r_ref[i] for i in range(points)]
+    span, slot = 1, 0
+    while span < points:
+        for base in range(0, points, 2 * span):
+            upper = q[base + span : base + 2 * span]
+            for matrix in upper:
+                l_ref[slot] = matrix
+                slot += 1
+            prod = times(jnp.concatenate(upper, axis=0), q[base + span - 1])
+            for i in range(span):
+                q[base + span + i] = prod[i * width : (i + 1) * width]
+        span *= 2
+    for i in range(points):
+        p_ref[i] = q[i]
+
+
+def scanned(c, l_ref):
     points = c.shape[0]
     x = [c[i : i + 1, :] for i in range(points)]
-    span = 1
+    span, slot = 1, 0
     while span < points:
         for base in range(0, points, 2 * span):
             head = x[base + span - 1]
@@ -175,11 +190,12 @@
 
 
 def correct_both(
-    s_lo, s_hi, halo_lo, halo_hi, pack_lo, pack_hi, lo_maps, hi_maps, d_lo, d_hi, nr_ref, c_ref, msg_ref
-):
+    s_lo, s_hi, halo_lo, halo_hi, small_ref, maps_ref, d_lo, d_hi, nr_ref, c_ref, msg_ref
+):
+    lo_maps, hi_maps = [maps_ref[i] for i in range(3)], [maps_ref[i] for i in range(3, 6)]
     points = s_lo.shape[0]
-    inj_lo, cap_lo, gain_lo, bnd_lo = unpacked(pack_lo, points)
-    inj_hi, cap_hi, gain_hi, bnd_hi = unpacked(pack_hi, points)
+    inj_lo, cap_lo, gain_lo, bnd_lo = vectors(small_ref, 0, points)
+    inj_hi, cap_hi, gain_hi, bnd_hi = vectors(small_ref, 1, points)
     nr_lo = negative_residual(s_lo, halo_lo, inj_lo, cap_lo, gain_lo, lo_maps[0])
     nr_hi = negative_residual(s_hi, halo_hi, inj_hi, cap_hi, gain_hi, hi_maps[0])
     c_lo = mapped_each(d_lo, nr_lo)
@@ -190,27 +206,29 @@
     msg_ref[points:] = taken(s_hi, bnd_hi)
 
 
-def early_kernel(s_lo, s_hi, pack_lo, pack_hi, d_lo, d_hi, maps_ref, nr_ref, c_ref, msg_ref):
+def early_kernel(
+    s_lo, s_hi, pack_lo, pack_hi, d_lo, d_hi, maps_ref, small_ref, nr_ref, c_ref, msg_ref
+):
     points, width = s_lo.shape
     for i in range(3):
         rows = slice(i * width, (i + 1) * width)
         maps_ref[i] = split_cols(pack_lo[rows])
         maps_ref[3 + i] = split_cols(pack_hi[rows])
+    small_ref[: points + 24] = pack_lo[3 * width :]
+    small_ref[points + 24 :] = pack_hi[3 * width :]
     none = jnp.zeros((1, width), F32)
     correct_both(
-        s_lo[...], s_hi[...], none, none, pack_lo, pack_hi,
-        [maps_ref[i] for i in range(3)], [maps_ref[i] for i in range(3, 6)],
-        d_lo, d_hi, nr_ref, c_ref, msg_ref,
+        s_lo[...], s_hi[...], none, none, small_ref, maps_ref, d_lo, d_hi, nr_ref, c_ref, msg_ref
     )
 
 
 def first_kernel(
-    halo_ref, s_lo, s_hi, pack_lo, pack_hi, maps_ref, d_lo, d_hi, old_nr, old_c, old_msg,
+    halo_ref, s_lo, s_hi, small_ref, maps_ref, d_lo, d_hi, old_nr, old_c, old_msg,
     s_ref, nr_ref, c_ref, msg_ref,
 ):
     points = s_lo.shape[0]
-    _, cap_lo, _, bnd_lo = unpacked(pack_lo, points)
-    _, cap_hi, _, bnd_hi = unpacked(pack_hi, points)
+    _, cap_lo, _, bnd_lo = vectors(small_ref, 0, points)
+    _, cap_hi, _, bnd_hi = vectors(small_ref, 1, points)
     s_ref[:points], s_ref[points:] = s_lo[...], s_hi[...]
     nr_ref[...], c_ref[...], msg_ref[...] = old_nr[...], old_c[...], old_msg[...]
     nr_lo = old_nr[:1] + cap_lo * halo_ref[:1]
@@ -225,14 +243,14 @@
 
 
 def second_kernel(
-    got_ref, s_ref, nr_ref, c_ref, pack_lo, maps_ref, d_lo, d_hi, ss_ref, new_c_ref, tail_ref, f_ref
+    got_ref, s_ref, nr_ref, c_ref, small_ref, maps_ref, d_lo, d_hi, ss_ref, new_c_ref, tail_ref, f_ref
 ):
     points, width = got_ref.shape[0] // 2, got_ref.shape[1]
     second_pair = lax.axis_index("dom") >= PAIR
 
     @pl.when(second_pair)
     def _():
-        bnd_lo = unpacked(pack_lo, points)[3]
+        bnd_lo = vectors(small_ref, 0, points)[3]
         c_lo = corrected(
             nr_ref[:points], got_ref[:points], got_ref[points:], d_lo, maps_ref[2], maps_ref[1]
         )
@@ -273,53 +291,37 @@
     ]
 
 
-def first_level_kernel(
-    distance, mw_ref, mf_ref, got_ref, tw_ref, tf_ref, a_ref, bw_ref, bf_ref, aw_ref, af_ref
-):
+def first_maps_kernel(distance, mw_ref, gw_ref, _, tw_ref, a_ref, bw_ref, aw_ref):
     width = mw_ref.shape[1]
     later = is_later(distance)
     eye = identity(width)
-    for wide, short in sections(width):
-        mw, mf, gw = mw_ref[wide], mf_ref[short], got_ref[wide]
-        gf = got_ref[PAIR * width + short.start : PAIR * width + short.stop]
+    for wide, _ in sections(width):
+        mw, gw = mw_ref[wide], gw_ref[wide]
         a = jnp.where(later, mw, gw)
         tw_ref[wide] = times(a, jnp.where(later, gw, mw))
-        a_split = split_cols(a)
-        a_ref[wide] = a_split
-        tf_ref[short] = mapped(a_split, jnp.where(later, gf, mf)) + jnp.where(later, mf, gf)
+        a_ref[wide] = split_cols(a)
         bw_ref[wide] = jnp.where(later, gw, eye)
-        bf_ref[short] = jnp.where(later, gf, 0.0)
         aw_ref[wide] = jnp.where(later, eye, gw)
-        af_ref[short] = jnp.where(later, 0.0, gf)
-
-
-def next_level_kernel(
-    distance, mw_ref, mf_ref, got_ref, bw_ref, bf_ref, aw_ref, af_ref,
-    tw_ref, tf_ref, a_ref, x_ref, nbw_ref, nbf_ref, naw_ref, naf_ref,
+
+
+def next_maps_kernel(
+    distance, mw_ref, gw_ref, bw_ref, aw_ref, _, tw_ref, a_ref, x_ref, nbw_ref, naw_ref
 ):
     width = mw_ref.shape[1]
     later = is_later(distance)
-    for wide, short in sections(width):
-        mw, mf, gw = mw_ref[wide], mf_ref[short], got_ref[wide]
-        gf = got_ref[PAIR * width + short.start : PAIR * width + short.stop]
-        bw, bf, aw, af = bw_ref[wide], bf_ref[short], aw_ref[wide], af_ref[short]
+    for wide, _ in sections(width):
+        mw, gw, bw, aw = mw_ref[wide], gw_ref[wide], bw_ref[wide], aw_ref[wide]
         a = jnp.where(later, mw, gw)
         tw_ref[wide] = times(a, jnp.where(later, gw, mw))
-        a_split = split_cols(a)
-        a_ref[wide] = a_split
-        tf_ref[short] = mapped(a_split, jnp.where(later, gf, mf)) + jnp.where(later, mf, gf)
+        a_ref[wide] = split_cols(a)
         x = jnp.where(later, bw, gw)
         joined = times(x, jnp.where(later, gw, aw))
-        x_split = split_cols(x)
-        x_ref[wide] = x_split
-        sums = mapped(x_split, jnp.where(later, gf, af)) + jnp.where(later, bf, gf)
+        x_ref[wide] = split_cols(x)
         nbw_ref[wide] = jnp.where(later, joined, bw)
-        nbf_ref[short] = jnp.where(later, sums, bf)
         naw_ref[wide] = jnp.where(later, aw, joined)
-        naf_ref[short] = jnp.where(later, af, sums)
-
-
-def again_first_kernel(distance, mf_ref, gf_ref, a_ref, tf_ref, bf_ref, af_ref):
+
+
+def first_sums_kernel(distance, mf_ref, gf_ref, a_ref, _, tf_ref, bf_ref, af_ref):
     later = is_later(distance)
     for wide, short in sections(a_ref.shape[0] // PAIR):
         mf, gf = mf_ref[short], gf_ref[short]
@@ -328,8 +330,8 @@
         af_ref[short] = jnp.where(later, 0.0, gf)
 
 
-def again_next_kernel(
-    distance, mf_ref, gf_ref, bf_ref, af_ref, a_ref, x_ref, tf_ref, nbf_ref, naf_ref
+def next_sums_kernel(
+    distance, mf_ref, gf_ref, bf_ref, af_ref, a_ref, x_ref, _, tf_ref, nbf_ref, naf_ref
 ):
     later = is_later(distance)
     for wide, short in sections(a_ref.shape[0] // PAIR):
@@ -340,41 +342,38 @@
         naf_ref[short] = jnp.where(later, af, sums)
 
 
-def local_kernel(c_ref, ls_ref, tail_ref, aw_ref, af_ref, s_ref, base_ref, v_ref):
+def local_kernel(c_ref, l_lo, l_hi, tail_ref, aw_ref, af_ref, s_ref, base_ref, v_ref):
     points, width = s_ref.shape[0] // PAIR, s_ref.shape[1]
     for g, (wide, short) in enumerate(sections(width)):
         rows = slice(g * points, (g + 1) * points)
         long = slice(g * (points + 8), (g + 1) * (points + 8))
-        slot = g * (ls_ref.shape[0] // PAIR)
-        base_ref[rows] = s_ref[rows] + scanned(c_ref[rows], ls_ref, slot)
+        base_ref[rows] = s_ref[rows] + scanned(c_ref[rows], (l_lo, l_hi)[g])
         v_ref[long] = mapped(split_cols(aw_ref[wide]), tail_ref[long]) + af_ref[short][:1]
 
 
 def turn_kernel(
-    v_ref, got_ref, bw_ref, bf_ref, ps_ref, base_ref, halo_ref, pack_lo, pack_hi, maps_ref,
+    v_ref, gw_ref, gf_ref, bw_ref, bf_ref, p_lo, p_hi, base_ref, halo_ref, small_ref, maps_ref,
     d_lo, d_hi, s_ref, nr_ref, c_ref, msg_ref,
 ):
     points, width = s_ref.shape[0] // PAIR, s_ref.shape[1]
     came = []
     for g, (wide, short) in enumerate(sections(width)):
         long = slice(g * (points + 8), (g + 1) * (points + 8))
-        gf = got_ref[PAIR * width + 8 * g : PAIR * width + 8 * g + 1]
-        v = mapped(split_cols(got_ref[wide]), v_ref[long]) + gf
+        v = mapped(split_cols(gw_ref[wide]), v_ref[long]) + gf_ref[short][:1]
         came.append(mapped(split_cols(bw_ref[wide]), v) + bf_ref[short][:1])
-    moved = mapped_each(ps_ref, jnp.concatenate([v[:points] for v in came], axis=0))
-    s = base_ref[...] + moved
+    moved = [mapped_each(p, v[:points]) for p, v in zip((p_lo, p_hi), came)]
+    s = base_ref[...] + jnp.concatenate(moved, axis=0)
     s_ref[...] = s
     correct_both(
         s[:points], s[points:],
         halo_ref[:1] + came[0][points : points + 1],
         halo_ref[4:5] + came[1][points : points + 1],
-        pack_lo, pack_hi, [maps_ref[i] for i in range(3)], [maps_ref[i] for i in range(3, 6)],
-        d_lo, d_hi, nr_ref, c_ref, msg_ref,
+        small_ref, maps_ref, d_lo, d_hi, nr_ref, c_ref, msg_ref,
     )
 
 
 def last_local_kernel(
-    c_ref, ls_ref, tail_ref, aw_ref, af_ref, gw_ref, bw_ref, bf_ref, ps_ref, s_ref, base_ref
+    c_ref, l_lo, l_hi, tail_ref, aw_ref, af_ref, gw_ref, bw_ref, bf_ref, p_lo, p_hi, s_ref, base_ref
 ):
     points, width = s_ref.shape[0] // PAIR, s_ref.shape[1]
     came = []
@@ -383,20 +382,19 @@
         v = mapped(split_cols(aw_ref[wide]), tail_ref[at : at + points]) + af_ref[short][:1]
         v = mapped(split_cols(gw_ref[wide]), v)
         came.append(mapped(split_cols(bw_ref[wide]), v) + bf_ref[short][:1])
-    moved = mapped_each(ps_ref, jnp.concatenate(came, axis=0))
     for g in range(PAIR):
         rows = slice(g * points, (g + 1) * points)
-        slot = g * (ls_ref.shape[0] // PAIR)
-        base_ref[rows] = s_ref[rows] + moved[rows] + scanned(c_ref[rows], ls_ref, slot)
-
-
-def end_kernel(gf_ref, bw_ref, ps_ref, base_ref, s_ref):
+        moved = mapped_each((p_lo, p_hi)[g], came[g])
+        base_ref[rows] = s_ref[rows] + moved + scanned(c_ref[rows], (l_lo, l_hi)[g])
+
+
+def end_kernel(gf_ref, bw_ref, p_lo, p_hi, base_ref, s_ref):
     points, width = s_ref.shape[0] // PAIR, s_ref.shape[1]
-    came = []
-    for wide, short in sections(width):
+    for g, (wide, short) in enumerate(sections(width)):
+        rows = slice(g * points, (g + 1) * points)
         v = mapped(split_cols(bw_ref[wide]), gf_ref[short])[:1]
-        came.append(jnp.broadcast_to(v, (points, width)))
-    s_ref[...] = base_ref[...] + mapped_each(ps_ref, jnp.concatenate(came, axis=0))
+        moved = mapped_each((p_lo, p_hi)[g], jnp.broadcast_to(v, (points, width)))
+        s_ref[rows] = base_ref[rows] + moved
 
 
 def choose_kernel(both_ref, got_ref, s_ref):
@@ -415,7 +413,9 @@
     return lax.ppermute(value, "dom", [(i, i ^ distance) for i in range(lax.axis_size("dom"))])
 
 
-def both_partitions(s, nr, c, msg, halo, maps, pack_lo, pack_hi, d_lo, d_hi, r_lo, r_hi):
+def both_partitions(
+    s, nr, c, msg, halo, small, maps, d_lo, d_hi, r_lo, r_hi
+):
     points, width = s.shape[0] // PAIR, s.shape[1]
     vec, square = ((PAIR * points, width), F32), ((PAIR * width, width), F32)
     square_split = ((PAIR * width, 2 * width), BF16)
@@ -425,52 +425,67 @@
     steps = (points.bit_length() - 1) * points // 2
     distances = [2**k for k in range(lax.axis_size("tm").bit_length() - 1)]
 
+    def sums_level(level, f, bf, af, beside):
+        got = exchanged(f, distances[level])
+        if level == 0:
+            return call(
+                functools.partial(first_sums_kernel, distances[0]), [eight] * 3,
+                f, got, *kept[0], beside,
+            )
+        return call(
+            functools.partial(next_sums_kernel, distances[level]), [eight] * 3,
+            f, got, bf, af, *kept[level], beside,
+            cost=pl.CostEstimate(flops=2**33, bytes_accessed=2**25, transcendentals=0),
+        )
+
     got = swapped(msg, 2)
-    ss, w = call(suffix_kernel, [many, square], r_lo, r_hi)
-    ps, ls = call(prefix_kernel, [many, ((PAIR * steps, width, width), F32)], r_lo, r_hi)
+    w, r_lo, r_hi = call(
+        whole_kernel, [square] + [((points, width, width), F32)] * 2, r_lo, r_hi,
+        source=pltpu.HBM, scratch=[pltpu.SemaphoreType.DMA((2,))],
+    )
+    got_w = exchanged(w, distances[0])
+    (ss,) = call(
+        suffix_kernel, [many], r_lo, r_hi, got,
+        cost=pl.CostEstimate(flops=2**33, bytes_accessed=2**25, transcendentals=0),
+    )
+    p_shapes = [((points, width, width), F32), ((steps, width, width), F32)]
+    p_lo, l_lo = call(prefix_kernel, p_shapes, r_lo)
+    p_hi, l_hi = call(prefix_kernel, p_shapes, r_hi)
+    beside = [p_lo] + [ss] * (len(distances) - 2)
     c, tail, f = call(
-        second_kernel, [vec, longer, eight], got, s, nr, c, pack_lo, maps, d_lo, d_hi, ss
-    )
-    kept = []
+        second_kernel, [vec, longer, eight], got, s, nr, c, small, maps, d_lo, d_hi, ss
+    )
+    kept, bf, af = [], None, None
     for level, distance in enumerate(distances[:-1]):
-        got = exchanged(jnp.concatenate([w, f], axis=0), distance)
         if level == 0:
-            w, f, a, bw, bf, aw, af = call(
-                functools.partial(first_level_kernel, distance),
-                [square, eight, square_split, square, eight, square, eight], w, f, got,
+            w, a, bw, aw = call(
+                functools.partial(first_maps_kernel, distance),
+                [square, square_split, square, square], w, got_w, f,
             )
             kept.append((a,))
         else:
-            w, f, a, x, bw, bf, aw, af = call(
-                functools.partial(next_level_kernel, distance),
-                [square, eight, square_split, square_split, square, eight, square, eight],
-                w, f, got, bw, bf, aw, af,
+            w, a, x, bw, aw = call(
+                functools.partial(next_maps_kernel, distance),
+                [square, square_split, square_split, square, square], w, got_w, bw, aw, f,
             )
             kept.append((a, x))
-    last = exchanged(jnp.concatenate([w, f], axis=0), distances[-1])
-    base, v = call(local_kernel, [vec, longer], c, ls, tail, aw, af, s)
+        got_w = exchanged(w, distances[level + 1])
+        f, bf, af = sums_level(level, f, bf, af, beside[level])
+    got, last = exchanged(f, distances[-1]), got_w
+    base, v = call(local_kernel, [vec, longer], c, l_lo, l_hi, tail, aw, af, s)
     s, nr, c, msg = call(
         turn_kernel, [vec] * 4,
-        v, last, bw, bf, ps, base, halo, pack_lo, pack_hi, maps, d_lo, d_hi,
+        v, last, got, bw, bf, p_lo, p_hi, base, halo, small, maps, d_lo, d_hi,
     )
     got = swapped(msg, 2)
     c, tail, f = call(
-        second_kernel, [vec, longer, eight], got, s, nr, c, pack_lo, maps, d_lo, d_hi, ss
-    )
-    for level, distance in enumerate(distances[:-1]):
-        got = exchanged(f, distance)
-        if level == 0:
-            f, bf, af = call(
-                functools.partial(again_first_kernel, distance), [eight] * 3, f, got, *kept[0]
-            )
-        else:
-            f, bf, af = call(
-                functools.partial(again_next_kernel, distance), [eight] * 3,
-                f, got, bf, af, *kept[level],
-            )
+        second_kernel, [vec, longer, eight], got, s, nr, c, small, maps, d_lo, d_hi, ss
+    )
+    for level in range(len(distances) - 1):
+        f, bf, af = sums_level(level, f, bf, af, beside[level])
     got = exchanged(f, distances[-1])
-    (base,) = call(last_local_kernel, [vec], c, ls, tail, aw, af, last, bw, bf, ps, s)
-    return call(end_kernel, [vec], got, bw, ps, base)[0]
+    (base,) = call(last_local_kernel, [vec], c, l_lo, l_hi, tail, aw, af, last, bw, bf, p_lo, p_hi, s)
+    return call(end_kernel, [vec], got, bw, p_lo, p_hi, base)[0]
 
 
 def per_device(
@@ -509,20 +524,21 @@
     )
     near_pack = swapped(pack, 1)
     vec = ((PAIR * points, width), F32)
-    maps, nr, c, msg = call(
-        early_kernel, [((6, width, 2 * width), BF16), vec, vec, vec],
+    maps, small, nr, c, msg = call(
+        early_kernel,
+        [((6, width, 2 * width), BF16), ((PAIR * (points + 24), width), F32), vec, vec, vec],
         near_s, s, near_pack, pack, near_d, d,
     )
     s, nr, c, msg = call(
         first_kernel, [vec] * 4,
-        halo, near_s, s, near_pack, pack, maps, near_d, d, nr, c, msg,
+        halo, near_s, s, small, maps, near_d, d, nr, c, msg,
     )
     odd = lax.axis_index("dom") % 2 == 1
     both = lax.cond(
         odd,
         both_partitions,
         lambda s, *rest: s,
-        s, nr, c, msg, halo, maps, near_pack, pack, near_d, d, near_r, r,
+        s, nr, c, msg, halo, small, maps, near_d, d, near_r, r,
     )
     (s,) = call(choose_kernel, [((points, width), F32)], both, swapped(both, 1))
     return s[:, None]

time: 46.8 us -> 45 us (0.962)
  starting transfers between devices: 38.3 us -> 36.9 us
    ppermute x5, starting transfers between devices: 35.6 us -> 34.2 us  [swapped(): lax.ppermute(value, 'dom', [(i, i ^ distance) for i in range(lax.axis_siz...]
where the time goes in v1:
time: 45 us; the launch traced here: 44.8 us
  starting transfers between devices  36.9 us (82%)
  waiting for transfers between devices  4.66 us (10%)
  Pallas kernels  2.28 us (5%)
  between operations  0.74 us (2%)
    ppermute x5, starting transfers between devices, swapped(): lax.ppermute(value, 'dom', [(i, i ^ distance) for i in range(lax.axis_siz...  34.2 us
    ppermute x1, waiting for transfers between devices, per_device(): lax.ppermute(rows, 'tm', [(i, (i + 1) % segments) for i in range(segments)])  3.43 us
    ppermute x1, starting transfers between devices, per_device(): lax.ppermute(rows, 'tm', [(i, (i + 1) % segments) for i in range(segments)])  2.68 us
    pallas_call x6, Pallas kernels, call(): pl.pallas_call(kernel, out_shape=[jax.ShapeDtypeStruct(s, d) for s, d in...  2.28 us
    ppermute x5, waiting for transfers between devices, swapped(): lax.ppermute(value, 'dom', [(i, i ^ distance) for i in range(lax.axis_siz...  1.23 us
  transfers between devices with their start and end apart: 6, of which 3 were waited for; matrix products, arithmetic and copies ran while one was open for 0% of the time, Pallas kernels for 4%

profile of v1, /device:TPU:0, one launch (start us, length us, event | category | flops | bytes accessed | tf_op | source)
XLA Modules:
  0.0 44.8 jit_solution(15841768870265217106)
XLA Ops:
  0.0 0.0 copy-start.8
  0.0 0.0 copy-start.1
  0.0 0.0 copy-start.2
  0.0 0.0 copy-start.5
  0.0 0.0 copy-start.6
  0.0 0.0 copy-start.7
  0.0 0.0 copy-start
  0.1 0.5 %collective-permute-start.11 = (f32[16,1,128]{2,0,1:T(8,128)}, f32[16,1,128]{2,0,1:T(8,128)S(1)}, u32[]{:S(2)}, u32[]{:S(2)}) collective-permute-start(f32[16,1,128]{2,0,1:T(8,128)} %bitcast.19), channel_id=1, source_target_pairs={{0,1},{1,0},{2,3},{3,2},{4,5},{5,4},{6,7},{7,6},{8,9},{9,8},{10,11... | collective-permute-start | bytes 24584 | tf_op jit(solution)/shard_map/ppermute | solution.py:413
  1.2 0.4 collective-permute-done.11
  1.6 0.0 copy-done.8
  1.6 0.3 collective-permute-start.14
  2.0 0.2 collective-permute-start.15
  2.1 0.0 copy-done.1
  2.1 0.0 copy-done.2
  2.1 0.0 copy-done.3
  2.2 0.0 copy-done.4
  2.2 0.0 copy-done.5
  2.2 0.0 copy-done.6
  2.2 0.0 copy-done.7
  2.2 0.4 collective-permute-start.13
  2.6 0.0 copy-done
  2.6 2.7 %collective-permute-start.12 = (f32[8,128]{1,0:T(8,128)S(1)}, f32[8,128]{1,0:T(8,128)S(1)}, u32[]{:S(2)}, u32[]{:S(2)}) collective-permute-start(f32[8,128]{1,0:T(8,128)S(1)} %shard_map.110), channel_id=1, source_target_pairs={{0,4},{4,8},{8,12},{12,16},{16,20},{20,24},{24,28},{28,0},{1,5},{5... | collective-permute-start | bytes 12296 | tf_op jit(solution)/shard_map/ppermute | solution.py:519
  5.3 0.0 collective-permute-done.13.pack_lo
  5.3 0.0 collective-permute-done.14
  5.3 1.2 %shard_map.112 = (bf16[6,128,256]{2,1,0:T(8,128)(2,1)S(1)}, f32[80,128]{1,0:T(8,128)S(1)}, f32[32,128]{1,0:T(8,128)S(1)}, f32[32,128]{1,0:T(8,128)S(1)}, f32[32,128]{1,0:T(8,128)S(1)}) custom-call(f32[16,128]{1,0:T(8,128)S(1)} %bitcast.24, f32[16,128]{1,0:T(8,128)S(1)} %bitcast.21, f32[424,128]{1,0:T(8,128)S(1)} %collective-permute-done.13.pack_lo, ...), custom_call_target="tpu_custom_call" | custom-call | tf_op jit(solution)/shard_map/pallas_call | solution.py:60
  6.5 3.4 %collective-permute-done.12.halo_ref = f32[8,128]{1,0:T(8,128)S(1)} collective-permute-done((f32[8,128]{1,0:T(8,128)S(1)}, f32[8,128]{1,0:T(8,128)S(1)}, u32[]{:S(2)}, u32[]{:S(2)}) %collective-permute-start.12) | collective-permute-done | bytes 4128 | tf_op jit(solution)/shard_map/ppermute | solution.py:519
  9.9 0.5 %shard_map.113 = (f32[32,128]{1,0:T(8,128)S(1)}, f32[32,128]{1,0:T(8,128)S(1)}, f32[32,128]{1,0:T(8,128)S(1)}, f32[32,128]{1,0:T(8,128)S(1)}) custom-call(f32[8,128]{1,0:T(8,128)S(1)} %collective-permute-done.12.halo_ref, f32[16,128]{1,0:T(8,128)S(1)} %bitcast.25, f32[16,128]{1,0:T(8,128)S(1)} %bitcast.22, f32[80,128]{1,0:T(8,128)S(1)} %get-tuple-element.102.small_ref, ...), custom_call_target="tpu_custom_call" | custom-call | tf_op jit(solution)/shard_map/pallas_call | solution.py:60
  10.4 0.0 collective-permute-done.15
  10.4 0.2 conditional.1
  10.6 32.8 %collective-permute-start.16 = (f32[32,128]{1,0:T(8,128)S(1)}, f32[32,128]{1,0:T(8,128)S(1)}, u32[]{:S(2)}, u32[]{:S(2)}) collective-permute-start(f32[32,128]{1,0:T(8,128)S(1)} %get-tuple-element.123.both_ref), channel_id=1, source_target_pairs={{0,1},{1,0},{2,3},{3,2},{4,5},{5,4},{6,7},{7,6},{8,9},{9,8},{10,11... | collective-permute-start | bytes 49160 | tf_op jit(solution)/shard_map/ppermute | solution.py:413
  43.4 0.8 %collective-permute-done.16.got_ref = f32[32,128]{1,0:T(8,128)S(1)} collective-permute-done((f32[32,128]{1,0:T(8,128)S(1)}, f32[32,128]{1,0:T(8,128)S(1)}, u32[]{:S(2)}, u32[]{:S(2)}) %collective-permute-start.16) | collective-permute-done | bytes 16416 | tf_op jit(solution)/shard_map/ppermute | solution.py:413
  44.2 0.6 %shard_map.114 = f32[16,128]{1,0:T(8,128)} custom-call(f32[32,128]{1,0:T(8,128)S(1)} %get-tuple-element.123.both_ref, f32[32,128]{1,0:T(8,128)S(1)} %collective-permute-done.16.got_ref), custom_call_target="tpu_custom_call" | custom-call | tf_op jit(solution)/shard_map/pallas_call | solution.py:60
  (6 shorter events, 0.0 us)
Async XLA Ops:
  0.0 1.6 %copy-start.8 = (f32[16,1,1,128,128]{4,3,2,1,0:T(8,128)S(1)}, f32[16,1,1,128,128]{4,3,2,1,0:T(8,128)}, u32[]{:S(2)}) copy-start(f32[16,1,1,128,128]{4,3,2,1,0:T(8,128)} %param.21) | copy-start | bytes 3145732
  0.0 2.1 %copy-start.1 = (f32[1,128,128]{2,1,0:T(8,128)S(1)}, f32[1,128,128]{2,1,0:T(8,128)}, u32[]{:S(2)}) copy-start(f32[1,128,128]{2,1,0:T(8,128)} %param.16) | copy-start | bytes 196612
  0.0 2.1 %copy-start.2 = (f32[1,128,128]{2,1,0:T(8,128)S(1)}, f32[1,128,128]{2,1,0:T(8,128)}, u32[]{:S(2)}) copy-start(f32[1,128,128]{2,1,0:T(8,128)} %param.19) | copy-start | bytes 196612
  0.0 2.1 %copy-start.3 = (f32[1,128,128]{2,1,0:T(8,128)S(1)}, f32[1,128,128]{2,1,0:T(8,128)}, u32[]{:S(2)}) copy-start(f32[1,128,128]{2,1,0:T(8,128)} %param.22) | copy-start | bytes 196612
  0.0 2.1 %copy-start.4 = (f32[16,1,128]{2,1,0:T(1,128)S(1)}, f32[16,1,128]{2,1,0:T(1,128)}, u32[]{:S(2)}) copy-start(f32[16,1,128]{2,1,0:T(1,128)} %param.14) | copy-start | bytes 24580
  0.0 2.1 %copy-start.5 = (f32[1,128]{1,0:T(1,128)S(1)}, f32[1,128]{1,0:T(1,128)}, u32[]{:S(2)}) copy-start(f32[1,128]{1,0:T(1,128)} %cap_ref.1) | copy-start | bytes 1540
  0.0 2.1 %copy-start.6 = (f32[1,128]{1,0:T(1,128)S(1)}, f32[1,128]{1,0:T(1,128)}, u32[]{:S(2)}) copy-start(f32[1,128]{1,0:T(1,128)} %gain_ref.1) | copy-start | bytes 1540
  0.0 2.1 %copy-start.7 = (s32[1,128]{1,0:T(1,128)S(1)}, s32[1,128]{1,0:T(1,128)}, u32[]{:S(2)}) copy-start(s32[1,128]{1,0:T(1,128)} %bnd_ref.1) | copy-start | bytes 1540
  0.0 2.6 %copy-start = (f32[16,1,128]{2,1,0:T(1,128)S(1)}, f32[16,1,128]{2,1,0:T(1,128)}, u32[]{:S(2)}) copy-start(f32[16,1,128]{2,1,0:T(1,128)} %param.13) | copy-start | bytes 24580
  0.1 1.6 %collective-permute-start.11 = (f32[16,1,128]{2,0,1:T(8,128)}, f32[16,1,128]{2,0,1:T(8,128)S(1)}, u32[]{:S(2)}, u32[]{:S(2)}) collective-permute-start(f32[16,1,128]{2,0,1:T(8,128)} %bitcast.19), channel_id=1, source_target_pairs={{0,1},{1,0},{2,3},{3,2},{4,5},{5,4},{6,7},{7,6},{8,9},{9,8},{10,11... | collective-permute-start | bytes 24584 | tf_op jit(solution)/shard_map/ppermute | solution.py:413
  1.6 3.7 %collective-permute-start.14 = (f32[16,1,1,128,128]{4,3,0,2,1:T(8,128)S(1)}, f32[16,1,1,128,128]{4,3,0,2,1:T(8,128)S(1)}, u32[]{:S(2)}, u32[]{:S(2)}) collective-permute-start(f32[16,1,1,128,128]{4,3,0,2,1:T(8,128)S(1)} %bitcast.30), channel_id=1, source_target_pairs={{0,1},{1,0},{2,3},{3,2},{4,5},{5,4},{6,7},{7,6},{8,9},{9,8},{10,11... | collective-permute-start | bytes 3145736 | tf_op jit(solution)/shard_map/ppermute | solution.py:413
  2.0 8.4 %collective-permute-start.15 = (f32[16,1,1,128,128]{4,3,0,2,1:T(8,128)}, f32[16,1,1,128,128]{4,3,0,2,1:T(8,128)}, u32[]{:S(2)}, u32[]{:S(2)}) collective-permute-start(f32[16,1,1,128,128]{4,3,0,2,1:T(8,128)} %bitcast.15), channel_id=1, source_target_pairs={{0,1},{1,0},{2,3},{3,2},{4,5},{5,4},{6,7},{7,6},{8,9},{9,8},{10,11... | collective-permute-start | bytes 3145736 | tf_op jit(solution)/shard_map/ppermute | solution.py:413
  2.2 3.1 %collective-permute-start.13 = (f32[424,128]{1,0:T(8,128)S(1)}, f32[424,128]{1,0:T(8,128)S(1)}, u32[]{:S(2)}, u32[]{:S(2)}) collective-permute-start(f32[424,128]{1,0:T(8,128)S(1)} %shard_map.111.pack_hi), channel_id=1, source_target_pairs={{0,1},{1,0},{2,3},{3,2},{4,5},{5,4},{6,7},{7,6},{8,9},{9,8},{10,11... | collective-permute-start | bytes 651272 | tf_op jit(solution)/shard_map/ppermute | solution.py:413
  2.6 7.3 %collective-permute-start.12 = (f32[8,128]{1,0:T(8,128)S(1)}, f32[8,128]{1,0:T(8,128)S(1)}, u32[]{:S(2)}, u32[]{:S(2)}) collective-permute-start(f32[8,128]{1,0:T(8,128)S(1)} %shard_map.110), channel_id=1, source_target_pairs={{0,4},{4,8},{8,12},{12,16},{16,20},{20,24},{24,28},{28,0},{1,5},{5... | collective-permute-start | bytes 12296 | tf_op jit(solution)/shard_map/ppermute | solution.py:519
  10.6 33.6 %collective-permute-start.16 = (f32[32,128]{1,0:T(8,128)S(1)}, f32[32,128]{1,0:T(8,128)S(1)}, u32[]{:S(2)}, u32[]{:S(2)}) collective-permute-start(f32[32,128]{1,0:T(8,128)S(1)} %get-tuple-element.123.both_ref), channel_id=1, source_target_pairs={{0,1},{1,0},{2,3},{3,2},{4,5},{5,4},{6,7},{7,6},{8,9},{9,8},{10,11... | collective-permute-start | bytes 49160 | tf_op jit(solution)/shard_map/ppermute | solution.py:413

commit v2 on v1

--- a/solution.py
+++ b/solution.py
@@ -55,12 +55,31 @@
     return jnp.concatenate(rows, axis=0)
 
 
-def call(kernel, outs, *args, cost=None, source=pltpu.VMEM, scratch=()):
+def mapped_each_split(matrices_split, vectors):
+    count, width = vectors.shape
+    both = dot_nt(split_rows(vectors), matrices_split)
+    row = lax.broadcasted_iota(jnp.int32, (2 * count, width), 0) % count
+    picked = [
+        jnp.where(row == r, both[:, r * width : (r + 1) * width], 0.0) for r in range(count)
+    ]
+    while len(picked) > 1:
+        picked = [a + b for a, b in zip(picked[::2], picked[1::2])]
+    return picked[0][:count] + picked[0][count:]
+
+
+def mapped_sum(matrices, vectors):
+    products = matrices[0] * vectors[:1, :]
+    for r in range(1, vectors.shape[0]):
+        products = products + matrices[r] * vectors[r : r + 1, :]
+    return jnp.sum(products.T, axis=0, keepdims=True)
+
+
+def call(kernel, outs, *args, cost=None, in_hbm=0, scratch=()):
     vmem = pl.BlockSpec(memory_space=pltpu.VMEM)
     return pl.pallas_call(
         kernel,
         out_shape=[jax.ShapeDtypeStruct(s, d) for s, d in outs],
-        in_specs=[pl.BlockSpec(memory_space=source)] * len(args),
+        in_specs=[vmem] * (len(args) - in_hbm) + [pl.BlockSpec(memory_space=pltpu.HBM)] * in_hbm,
         out_specs=[vmem] * len(outs),
         scratch_shapes=list(scratch),
         cost_estimate=cost,
@@ -106,17 +125,22 @@
     return inj, cap, gain, bnd.astype(jnp.int32)
 
 
-def whole_kernel(lo_ref, hi_ref, w_ref, r_lo, r_hi, sems):
-    points, width = lo_ref.shape[0], lo_ref.shape[1]
+def fetched(sources, targets, sems):
     moves = [
-        pltpu.make_async_copy(source, target, sems.at[g])
-        for g, (source, target) in enumerate(((lo_ref, r_lo), (hi_ref, r_hi)))
+        pltpu.make_async_copy(source, target, sems.at[i])
+        for i, (source, target) in enumerate(zip(sources, targets))
     ]
     for move in moves:
         move.start()
+    return moves
+
+
+def whole_kernel(lo_ref, hi_ref, w_ref, r_lo, r_hi, sems):
+    points, width = lo_ref.shape[0], lo_ref.shape[1]
+    moves = fetched((lo_ref, hi_ref), (r_lo, r_hi), sems)
     u = []
-    for g, r_ref in enumerate((r_lo, r_hi)):
-        moves[g].wait()
+    for move, r_ref in zip(moves, (r_lo, r_hi)):
+        move.wait()
         u += [times(r_ref[i + 1], r_ref[i]) for i in range(0, points, 2)]
     while len(u) > PAIR:
         u = [times(u[i + 1], u[i]) for i in range(0, len(u), 2)]
@@ -124,9 +148,11 @@
         w_ref[g * width : (g + 1) * width] = u[g]
 
 
-def suffix_kernel(r_lo, r_hi, _, s_ref):
-    points, width = r_lo.shape[0], r_lo.shape[1]
+def suffix_kernel(lo_ref, hi_ref, s_ref, r_lo, r_hi, sems):
+    points, width = lo_ref.shape[0], lo_ref.shape[1]
+    moves = fetched((lo_ref, hi_ref), (r_lo, r_hi), sems)
     for g, r_ref in enumerate((r_lo, r_hi)):
+        moves[g].wait()
         u = [r_ref[i] for i in range(points)]
         span = 1
         while span < points:
@@ -140,7 +166,7 @@
         s_ref[(g + 1) * points - 1] = identity(width)
 
 
-def prefix_kernel(r_ref, p_ref, l_ref):
+def prefix_kernel(split, r_ref, p_ref, l_ref):
     points, width = r_ref.shape[0], r_ref.shape[1]
     q = [r_ref[i] for i in range(points)]
     span, slot = 1, 0
@@ -155,7 +181,10 @@
                 q[base + span + i] = prod[i * width : (i + 1) * width]
         span *= 2
     for i in range(points):
-        p_ref[i] = q[i]
+        if split:
+            p_ref[i * width : (i + 1) * width] = split_cols(q[i])
+        else:
+            p_ref[i] = q[i]
 
 
 def scanned(c, l_ref):
@@ -207,7 +236,7 @@
 
 
 def early_kernel(
-    s_lo, s_hi, pack_lo, pack_hi, d_lo, d_hi, maps_ref, small_ref, nr_ref, c_ref, msg_ref
+    s_lo, s_hi, pack_lo, pack_hi, d_lo, d_hi, _, maps_ref, small_ref, nr_ref, c_ref, msg_ref
 ):
     points, width = s_lo.shape
     for i in range(3):
@@ -243,7 +272,7 @@
 
 
 def second_kernel(
-    got_ref, s_ref, nr_ref, c_ref, small_ref, maps_ref, d_lo, d_hi, ss_ref, new_c_ref, tail_ref, f_ref
+    got_ref, s_ref, nr_ref, c_ref, small_ref, maps_ref, d_lo, d_hi, ss_ref, new_c_ref, f_ref
 ):
     points, width = got_ref.shape[0] // 2, got_ref.shape[1]
     second_pair = lax.axis_index("dom") >= PAIR
@@ -255,15 +284,26 @@
             nr_ref[:points], got_ref[:points], got_ref[points:], d_lo, maps_ref[2], maps_ref[1]
         )
         new_c_ref[:points] = c_lo
-        new_c_ref[points:] = pair_corrected(
+        c_hi = pair_corrected(
             nr_ref[points:], s_ref[:points], c_lo, bnd_lo, d_hi, maps_ref[5], maps_ref[4]
         )
+        new_c_ref[points:] = c_hi
+        for g, c in enumerate((c_lo, c_hi)):
+            whole = mapped_sum(ss_ref[g * points : (g + 1) * points], c)
+            f_ref[8 * g : 8 * g + 8] = jnp.broadcast_to(whole, (8, width))
 
     @pl.when(jnp.logical_not(second_pair))
     def _():
         new_c_ref[...] = c_ref[...]
-
-    each = mapped_each(ss_ref, new_c_ref[...])
+        for g in range(PAIR):
+            rows = slice(g * points, (g + 1) * points)
+            whole = mapped_sum(ss_ref[rows], c_ref[rows])
+            f_ref[8 * g : 8 * g + 8] = jnp.broadcast_to(whole, (8, width))
+
+
+def tail_kernel(c_ref, ss_ref, tail_ref):
+    points, width = c_ref.shape[0] // PAIR, c_ref.shape[1]
+    each = mapped_each(ss_ref, c_ref[...])
     for g in range(PAIR):
         total = each[g * points : (g + 1) * points]
         shift = 1
@@ -276,9 +316,7 @@
         tail_ref[at : at + points] = jnp.concatenate(
             [total[1:], jnp.zeros((1, width), F32)], axis=0
         )
-        whole = jnp.broadcast_to(total[:1], (8, width))
-        tail_ref[at + points : at + points + 8] = whole
-        f_ref[8 * g : 8 * g + 8] = whole
+        tail_ref[at + points : at + points + 8] = jnp.broadcast_to(total[:1], (8, width))
 
 
 def is_later(distance):
@@ -321,7 +359,7 @@
         naw_ref[wide] = jnp.where(later, aw, joined)
 
 
-def first_sums_kernel(distance, mf_ref, gf_ref, a_ref, _, tf_ref, bf_ref, af_ref):
+def first_sums_kernel(distance, mf_ref, gf_ref, a_ref, _, __, tf_ref, bf_ref, af_ref):
     later = is_later(distance)
     for wide, short in sections(a_ref.shape[0] // PAIR):
         mf, gf = mf_ref[short], gf_ref[short]
@@ -331,7 +369,7 @@
 
 
 def next_sums_kernel(
-    distance, mf_ref, gf_ref, bf_ref, af_ref, a_ref, x_ref, _, tf_ref, nbf_ref, naf_ref
+    distance, mf_ref, gf_ref, bf_ref, af_ref, a_ref, x_ref, tf_ref, nbf_ref, naf_ref
 ):
     later = is_later(distance)
     for wide, short in sections(a_ref.shape[0] // PAIR):
@@ -361,7 +399,10 @@
         long = slice(g * (points + 8), (g + 1) * (points + 8))
         v = mapped(split_cols(gw_ref[wide]), v_ref[long]) + gf_ref[short][:1]
         came.append(mapped(split_cols(bw_ref[wide]), v) + bf_ref[short][:1])
-    moved = [mapped_each(p, v[:points]) for p, v in zip((p_lo, p_hi), came)]
+    moved = [
+        mapped_each(p_lo, came[0][:points]),
+        mapped_each_split(p_hi[...], came[1][:points]),
+    ]
     s = base_ref[...] + jnp.concatenate(moved, axis=0)
     s_ref[...] = s
     correct_both(
@@ -384,7 +425,7 @@
         came.append(mapped(split_cols(bw_ref[wide]), v) + bf_ref[short][:1])
     for g in range(PAIR):
         rows = slice(g * points, (g + 1) * points)
-        moved = mapped_each((p_lo, p_hi)[g], came[g])
+        moved = mapped_each_split(p_hi[...], came[g]) if g else mapped_each(p_lo, came[g])
         base_ref[rows] = s_ref[rows] + moved + scanned(c_ref[rows], (l_lo, l_hi)[g])
 
 
@@ -392,8 +433,14 @@
     points, width = s_ref.shape[0] // PAIR, s_ref.shape[1]
     for g, (wide, short) in enumerate(sections(width)):
         rows = slice(g * points, (g + 1) * points)
-        v = mapped(split_cols(bw_ref[wide]), gf_ref[short])[:1]
-        moved = mapped_each((p_lo, p_hi)[g], jnp.broadcast_to(v, (points, width)))
+        v = mapped(split_cols(bw_ref[wide]), gf_ref[short])
+        if g:
+            both = dot_nt(split_rows(v), p_hi[...])
+            both = both[:1] + both[8:9]
+            moved = [both[:, i * width : (i + 1) * width] for i in range(points)]
+            moved = jnp.concatenate(moved, axis=0)
+        else:
+            moved = mapped_each(p_lo, jnp.broadcast_to(v[:1], (points, width)))
         s_ref[rows] = base_ref[rows] + moved
 
 
@@ -414,7 +461,7 @@
 
 
 def both_partitions(
-    s, nr, c, msg, halo, small, maps, d_lo, d_hi, r_lo, r_hi
+    s, nr, c, msg, halo, small, maps, d_lo, d_hi, r_lo, r_hi, w
 ):
     points, width = s.shape[0] // PAIR, s.shape[1]
     vec, square = ((PAIR * points, width), F32), ((PAIR * width, width), F32)
@@ -430,31 +477,31 @@
         if level == 0:
             return call(
                 functools.partial(first_sums_kernel, distances[0]), [eight] * 3,
-                f, got, *kept[0], beside,
+                f, got, *kept[0], *beside,
             )
         return call(
             functools.partial(next_sums_kernel, distances[level]), [eight] * 3,
-            f, got, bf, af, *kept[level], beside,
+            f, got, bf, af, *kept[level],
             cost=pl.CostEstimate(flops=2**33, bytes_accessed=2**25, transcendentals=0),
         )
 
     got = swapped(msg, 2)
-    w, r_lo, r_hi = call(
-        whole_kernel, [square] + [((points, width, width), F32)] * 2, r_lo, r_hi,
-        source=pltpu.HBM, scratch=[pltpu.SemaphoreType.DMA((2,))],
-    )
     got_w = exchanged(w, distances[0])
-    (ss,) = call(
-        suffix_kernel, [many], r_lo, r_hi, got,
-        cost=pl.CostEstimate(flops=2**33, bytes_accessed=2**25, transcendentals=0),
-    )
-    p_shapes = [((points, width, width), F32), ((steps, width, width), F32)]
-    p_lo, l_lo = call(prefix_kernel, p_shapes, r_lo)
-    p_hi, l_hi = call(prefix_kernel, p_shapes, r_hi)
-    beside = [p_lo] + [ss] * (len(distances) - 2)
-    c, tail, f = call(
-        second_kernel, [vec, longer, eight], got, s, nr, c, small, maps, d_lo, d_hi, ss
-    )
+    ss, r_lo, r_hi = call(
+        suffix_kernel, [many] + [((points, width, width), F32)] * 2, r_lo, r_hi,
+        in_hbm=2, scratch=[pltpu.SemaphoreType.DMA((2,))],
+    )
+    l_shape = ((steps, width, width), F32)
+    p_lo, l_lo = call(
+        functools.partial(prefix_kernel, False), [((points, width, width), F32), l_shape], r_lo
+    )
+    p_hi, l_hi = call(
+        functools.partial(prefix_kernel, True), [((points * width, 2 * width), BF16), l_shape], r_hi
+    )
+    c, f = call(
+        second_kernel, [vec, eight], got, s, nr, c, small, maps, d_lo, d_hi, ss
+    )
+    (tail,) = call(tail_kernel, [longer], c, ss)
     kept, bf, af = [], None, None
     for level, distance in enumerate(distances[:-1]):
         if level == 0:
@@ -470,7 +517,7 @@
             )
             kept.append((a, x))
         got_w = exchanged(w, distances[level + 1])
-        f, bf, af = sums_level(level, f, bf, af, beside[level])
+        f, bf, af = sums_level(level, f, bf, af, (p_lo, p_hi))
     got, last = exchanged(f, distances[-1]), got_w
     base, v = call(local_kernel, [vec, longer], c, l_lo, l_hi, tail, aw, af, s)
     s, nr, c, msg = call(
@@ -478,11 +525,12 @@
         v, last, got, bw, bf, p_lo, p_hi, base, halo, small, maps, d_lo, d_hi,
     )
     got = swapped(msg, 2)
-    c, tail, f = call(
-        second_kernel, [vec, longer, eight], got, s, nr, c, small, maps, d_lo, d_hi, ss
-    )
+    c, f = call(
+        second_kernel, [vec, eight], got, s, nr, c, small, maps, d_lo, d_hi, ss
+    )
+    (tail,) = call(tail_kernel, [longer], c, ss)
     for level in range(len(distances) - 1):
-        f, bf, af = sums_level(level, f, bf, af, beside[level])
+        f, bf, af = sums_level(level, f, bf, af, (tail, tail))
     got = exchanged(f, distances[-1])
     (base,) = call(last_local_kernel, [vec], c, l_lo, l_hi, tail, aw, af, last, bw, bf, p_lo, p_hi, s)
     return call(end_kernel, [vec], got, bw, p_lo, p_hi, base)[0]
@@ -524,10 +572,14 @@
     )
     near_pack = swapped(pack, 1)
     vec = ((PAIR * points, width), F32)
+    (w,) = call(
+        whole_kernel, [((PAIR * width, width), F32)], near_r, r, in_hbm=2,
+        scratch=[pltpu.VMEM((points, width, width), F32)] * 2 + [pltpu.SemaphoreType.DMA((2,))],
+    )
     maps, small, nr, c, msg = call(
         early_kernel,
         [((6, width, 2 * width), BF16), ((PAIR * (points + 24), width), F32), vec, vec, vec],
-        near_s, s, near_pack, pack, near_d, d,
+        near_s, s, near_pack, pack, near_d, d, w,
     )
     s, nr, c, msg = call(
         first_kernel, [vec] * 4,
@@ -538,7 +590,7 @@
         odd,
         both_partitions,
         lambda s, *rest: s,
-        s, nr, c, msg, halo, small, maps, near_d, d, near_r, r,
+        s, nr, c, msg, halo, small, maps, near_d, d, near_r, r, w,
     )
     (s,) = call(choose_kernel, [((points, width), F32)], both, swapped(both, 1))
     return s[:, None]

time: 45 us -> 44.1 us (0.980)
  waiting for transfers between devices: 4.66 us -> 2.17 us
  Pallas kernels: 2.28 us -> 4.75 us
  starting transfers between devices: 36.9 us -> 35.8 us
    ppermute x1, waiting for transfers between devices: 3.43 us -> 0.94 us  [per_device(): lax.ppermute(rows, 'tm', [(i, (i + 1) % segments) for i in range(segments)])]
    pallas_call x6 -> x7, Pallas kernels: 2.28 us -> 4.75 us  [call(): pl.pallas_call(kernel, out_shape=[jax.ShapeDtypeStruct(s, d) for s, d in...]
    ppermute x5, starting transfers between devices: 34.2 us -> 33.1 us  [swapped(): lax.ppermute(value, 'dom', [(i, i ^ distance) for i in range(lax.axis_siz...]
  transfers between devices with their start and end apart: 6 -> 6, of which waited for: 3 -> 3; matrix products, arithmetic and copies ran while one was open for 0% -> 0% of each run, Pallas kernels for 4% -> 8%
where the time goes in v2:
time: 44.1 us; the launch traced here: 43.7 us
  starting transfers between devices  35.8 us (81%)
  Pallas kernels  4.75 us (11%)
  waiting for transfers between devices  2.17 us (5%)
  between operations  0.77 us (2%)
    ppermute x5, starting transfers between devices, swapped(): lax.ppermute(value, 'dom', [(i, i ^ distance) for i in range(lax.axis_siz...  33.1 us
    pallas_call x7, Pallas kernels, call(): pl.pallas_call(kernel, out_shape=[jax.ShapeDtypeStruct(s, d) for s, d in...  4.75 us
    ppermute x1, starting transfers between devices, per_device(): lax.ppermute(rows, 'tm', [(i, (i + 1) % segments) for i in range(segments)])  2.68 us
    ppermute x5, waiting for transfers between devices, swapped(): lax.ppermute(value, 'dom', [(i, i ^ distance) for i in range(lax.axis_siz...  1.23 us
    ppermute x1, waiting for transfers between devices, per_device(): lax.ppermute(rows, 'tm', [(i, (i + 1) % segments) for i in range(segments)])  0.94 us
  transfers between devices with their start and end apart: 6, of which 3 were waited for; matrix products, arithmetic and copies ran while one was open for 0% of the time, Pallas kernels for 8%

profile of v2, /device:TPU:0, one launch (start us, length us, event | category | flops | bytes accessed | tf_op | source)
XLA Modules:
  0.0 43.7 jit_solution(2575594794945310690)
XLA Ops:
  0.0 0.0 copy-start.8
  0.0 0.0 copy-start.1
  0.0 0.0 copy-start.5
  0.0 0.0 copy-start.6
  0.0 0.0 copy-start.7
  0.0 0.0 copy-start
  0.1 0.5 %collective-permute-start.11 = (f32[16,1,128]{2,0,1:T(8,128)}, f32[16,1,128]{2,0,1:T(8,128)S(1)}, u32[]{:S(2)}, u32[]{:S(2)}) collective-permute-start(f32[16,1,128]{2,0,1:T(8,128)} %bitcast.17), channel_id=1, source_target_pairs={{0,1},{1,0},{2,3},{3,2},{4,5},{5,4},{6,7},{7,6},{8,9},{9,8},{10,11... | collective-permute-start | bytes 24584 | tf_op jit(solution)/shard_map/ppermute | solution.py:460
  1.2 0.4 collective-permute-done.11
  1.6 0.3 collective-permute-start.15
  2.0 0.0 copy-done.8
  2.0 0.2 collective-permute-start.14
  2.1 0.0 copy-done.1
  2.1 0.0 copy-done.2
  2.1 0.0 copy-done.3
  2.2 0.0 copy-done.4
  2.2 0.0 copy-done.5
  2.2 0.0 copy-done.6
  2.2 0.0 copy-done.7
  2.2 0.4 collective-permute-start.13
  2.6 0.0 copy-done
  2.6 2.7 %collective-permute-start.12 = (f32[8,128]{1,0:T(8,128)S(1)}, f32[8,128]{1,0:T(8,128)S(1)}, u32[]{:S(2)}, u32[]{:S(2)}) collective-permute-start(f32[8,128]{1,0:T(8,128)S(1)} %shard_map.110), channel_id=1, source_target_pairs={{0,4},{4,8},{8,12},{12,16},{16,20},{20,24},{24,28},{28,0},{1,5},{5... | collective-permute-start | bytes 12296 | tf_op jit(solution)/shard_map/ppermute | solution.py:567
  5.3 0.0 collective-permute-done.15
  5.3 2.5 %shard_map.112._ = f32[256,128]{1,0:T(8,128)S(1)} custom-call(f32[16,128,128]{2,1,0:T(8,128)} %bitcast.12.lo_ref, f32[16,128,128]{2,1,0:T(8,128)} %bitcast.13.hi_ref), custom_call_target="tpu_custom_call" | custom-call | tf_op jit(solution)/shard_map/pallas_call | solution.py:79
  7.8 0.0 collective-permute-done.13.pack_lo
  7.8 0.0 collective-permute-done.14
  7.8 1.2 %shard_map.113 = (bf16[6,128,256]{2,1,0:T(8,128)(2,1)S(1)}, f32[80,128]{1,0:T(8,128)S(1)}, f32[32,128]{1,0:T(8,128)S(1)}, f32[32,128]{1,0:T(8,128)S(1)}, f32[32,128]{1,0:T(8,128)S(1)}) custom-call(f32[16,128]{1,0:T(8,128)S(1)} %bitcast.22, f32[16,128]{1,0:T(8,128)S(1)} %bitcast.19, f32[424,128]{1,0:T(8,128)S(1)} %collective-permute-done.13.pack_lo, ...), custom_call_target="tpu_custom_call" | custom-call | tf_op jit(solution)/shard_map/pallas_call | solution.py:79
  9.0 0.9 %collective-permute-done.12.halo_ref = f32[8,128]{1,0:T(8,128)S(1)} collective-permute-done((f32[8,128]{1,0:T(8,128)S(1)}, f32[8,128]{1,0:T(8,128)S(1)}, u32[]{:S(2)}, u32[]{:S(2)}) %collective-permute-start.12) | collective-permute-done | bytes 4128 | tf_op jit(solution)/shard_map/ppermute | solution.py:567
  9.9 0.5 %shard_map.114 = (f32[32,128]{1,0:T(8,128)S(1)}, f32[32,128]{1,0:T(8,128)S(1)}, f32[32,128]{1,0:T(8,128)S(1)}, f32[32,128]{1,0:T(8,128)S(1)}) custom-call(f32[8,128]{1,0:T(8,128)S(1)} %collective-permute-done.12.halo_ref, f32[16,128]{1,0:T(8,128)S(1)} %bitcast.23, f32[16,128]{1,0:T(8,128)S(1)} %bitcast.20, f32[80,128]{1,0:T(8,128)S(1)} %get-tuple-element.102.small_ref, ...), custom_call_target="tpu_custom_call" | custom-call | tf_op jit(solution)/shard_map/pallas_call | solution.py:79
  10.4 0.2 conditional.1
  10.6 31.7 %collective-permute-start.16 = (f32[32,128]{1,0:T(8,128)S(1)}, f32[32,128]{1,0:T(8,128)S(1)}, u32[]{:S(2)}, u32[]{:S(2)}) collective-permute-start(f32[32,128]{1,0:T(8,128)S(1)} %get-tuple-element.111.both_ref), channel_id=1, source_target_pairs={{0,1},{1,0},{2,3},{3,2},{4,5},{5,4},{6,7},{7,6},{8,9},{9,8},{10,11... | collective-permute-start | bytes 49160 | tf_op jit(solution)/shard_map/ppermute | solution.py:460
  42.2 0.8 %collective-permute-done.16.got_ref = f32[32,128]{1,0:T(8,128)S(1)} collective-permute-done((f32[32,128]{1,0:T(8,128)S(1)}, f32[32,128]{1,0:T(8,128)S(1)}, u32[]{:S(2)}, u32[]{:S(2)}) %collective-permute-start.16) | collective-permute-done | bytes 16416 | tf_op jit(solution)/shard_map/ppermute | solution.py:460
  43.1 0.6 %shard_map.115 = f32[16,128]{1,0:T(8,128)} custom-call(f32[32,128]{1,0:T(8,128)S(1)} %get-tuple-element.111.both_ref, f32[32,128]{1,0:T(8,128)S(1)} %collective-permute-done.16.got_ref), custom_call_target="tpu_custom_call" | custom-call | tf_op jit(solution)/shard_map/pallas_call | solution.py:79
  (7 shorter events, 0.0 us)
Async XLA Ops:
  0.0 2.0 %copy-start.8 = (f32[16,1,1,128,128]{4,3,2,1,0:T(8,128)S(1)}, f32[16,1,1,128,128]{4,3,2,1,0:T(8,128)}, u32[]{:S(2)}) copy-start(f32[16,1,1,128,128]{4,3,2,1,0:T(8,128)} %param.21) | copy-start | bytes 3145732
  0.0 2.1 %copy-start.1 = (f32[1,128,128]{2,1,0:T(8,128)S(1)}, f32[1,128,128]{2,1,0:T(8,128)}, u32[]{:S(2)}) copy-start(f32[1,128,128]{2,1,0:T(8,128)} %param.16) | copy-start | bytes 196612
  0.0 2.1 %copy-start.2 = (f32[1,128,128]{2,1,0:T(8,128)S(1)}, f32[1,128,128]{2,1,0:T(8,128)}, u32[]{:S(2)}) copy-start(f32[1,128,128]{2,1,0:T(8,128)} %param.19) | copy-start | bytes 196612
  0.0 2.1 %copy-start.3 = (f32[1,128,128]{2,1,0:T(8,128)S(1)}, f32[1,128,128]{2,1,0:T(8,128)}, u32[]{:S(2)}) copy-start(f32[1,128,128]{2,1,0:T(8,128)} %param.22) | copy-start | bytes 196612
  0.0 2.1 %copy-start.4 = (f32[16,1,128]{2,1,0:T(1,128)S(1)}, f32[16,1,128]{2,1,0:T(1,128)}, u32[]{:S(2)}) copy-start(f32[16,1,128]{2,1,0:T(1,128)} %param.14) | copy-start | bytes 24580
  0.0 2.1 %copy-start.5 = (f32[1,128]{1,0:T(1,128)S(1)}, f32[1,128]{1,0:T(1,128)}, u32[]{:S(2)}) copy-start(f32[1,128]{1,0:T(1,128)} %cap_ref.1) | copy-start | bytes 1540
  0.0 2.1 %copy-start.6 = (f32[1,128]{1,0:T(1,128)S(1)}, f32[1,128]{1,0:T(1,128)}, u32[]{:S(2)}) copy-start(f32[1,128]{1,0:T(1,128)} %gain_ref.1) | copy-start | bytes 1540
  0.0 2.1 %copy-start.7 = (s32[1,128]{1,0:T(1,128)S(1)}, s32[1,128]{1,0:T(1,128)}, u32[]{:S(2)}) copy-start(s32[1,128]{1,0:T(1,128)} %bnd_ref.1) | copy-start | bytes 1540
  0.0 2.6 %copy-start = (f32[16,1,128]{2,1,0:T(1,128)S(1)}, f32[16,1,128]{2,1,0:T(1,128)}, u32[]{:S(2)}) copy-start(f32[16,1,128]{2,1,0:T(1,128)} %param.13) | copy-start | bytes 24580
  0.1 1.6 %collective-permute-start.11 = (f32[16,1,128]{2,0,1:T(8,128)}, f32[16,1,128]{2,0,1:T(8,128)S(1)}, u32[]{:S(2)}, u32[]{:S(2)}) collective-permute-start(f32[16,1,128]{2,0,1:T(8,128)} %bitcast.17), channel_id=1, source_target_pairs={{0,1},{1,0},{2,3},{3,2},{4,5},{5,4},{6,7},{7,6},{8,9},{9,8},{10,11... | collective-permute-start | bytes 24584 | tf_op jit(solution)/shard_map/ppermute | solution.py:460
  1.6 3.7 %collective-permute-start.15 = (f32[16,1,1,128,128]{4,3,0,2,1:T(8,128)}, f32[16,1,1,128,128]{4,3,0,2,1:T(8,128)}, u32[]{:S(2)}, u32[]{:S(2)}) collective-permute-start(f32[16,1,1,128,128]{4,3,0,2,1:T(8,128)} %bitcast.11), channel_id=1, source_target_pairs={{0,1},{1,0},{2,3},{3,2},{4,5},{5,4},{6,7},{7,6},{8,9},{9,8},{10,11... | collective-permute-start | bytes 3145736 | tf_op jit(solution)/shard_map/ppermute | solution.py:460
  2.0 5.8 %collective-permute-start.14 = (f32[16,1,1,128,128]{4,3,0,2,1:T(8,128)S(1)}, f32[16,1,1,128,128]{4,3,0,2,1:T(8,128)S(1)}, u32[]{:S(2)}, u32[]{:S(2)}) collective-permute-start(f32[16,1,1,128,128]{4,3,0,2,1:T(8,128)S(1)} %bitcast.28), channel_id=1, source_target_pairs={{0,1},{1,0},{2,3},{3,2},{4,5},{5,4},{6,7},{7,6},{8,9},{9,8},{10,11... | collective-permute-start | bytes 3145736 | tf_op jit(solution)/shard_map/ppermute | solution.py:460
  2.2 5.6 %collective-permute-start.13 = (f32[424,128]{1,0:T(8,128)S(1)}, f32[424,128]{1,0:T(8,128)S(1)}, u32[]{:S(2)}, u32[]{:S(2)}) collective-permute-start(f32[424,128]{1,0:T(8,128)S(1)} %shard_map.111.pack_hi), channel_id=1, source_target_pairs={{0,1},{1,0},{2,3},{3,2},{4,5},{5,4},{6,7},{7,6},{8,9},{9,8},{10,11... | collective-permute-start | bytes 651272 | tf_op jit(solution)/shard_map/ppermute | solution.py:460
  2.6 7.3 %collective-permute-start.12 = (f32[8,128]{1,0:T(8,128)S(1)}, f32[8,128]{1,0:T(8,128)S(1)}, u32[]{:S(2)}, u32[]{:S(2)}) collective-permute-start(f32[8,128]{1,0:T(8,128)S(1)} %shard_map.110), channel_id=1, source_target_pairs={{0,4},{4,8},{8,12},{12,16},{16,20},{20,24},{24,28},{28,0},{1,5},{5... | collective-permute-start | bytes 12296 | tf_op jit(solution)/shard_map/ppermute | solution.py:567
  10.6 32.5 %collective-permute-start.16 = (f32[32,128]{1,0:T(8,128)S(1)}, f32[32,128]{1,0:T(8,128)S(1)}, u32[]{:S(2)}, u32[]{:S(2)}) collective-permute-start(f32[32,128]{1,0:T(8,128)S(1)} %get-tuple-element.111.both_ref), channel_id=1, source_target_pairs={{0,1},{1,0},{2,3},{3,2},{4,5},{5,4},{6,7},{7,6},{8,9},{9,8},{10,11... | collective-permute-start | bytes 49160 | tf_op jit(solution)/shard_map/ppermute | solution.py:460

commit v3 on v2

--- a/solution.py
+++ b/solution.py
@@ -148,11 +148,10 @@
         w_ref[g * width : (g + 1) * width] = u[g]
 
 
-def suffix_kernel(lo_ref, hi_ref, s_ref, r_lo, r_hi, sems):
-    points, width = lo_ref.shape[0], lo_ref.shape[1]
-    moves = fetched((lo_ref, hi_ref), (r_lo, r_hi), sems)
+def suffix_kernel(r_lo, r_hi, lo_ref, hi_ref, s_ref, d_lo, d_hi, sems):
+    points, width = r_lo.shape[0], r_lo.shape[1]
+    moves = fetched((lo_ref, hi_ref), (d_lo, d_hi), sems)
     for g, r_ref in enumerate((r_lo, r_hi)):
-        moves[g].wait()
         u = [r_ref[i] for i in range(points)]
         span = 1
         while span < points:
@@ -164,6 +163,8 @@
         for i in range(points - 1):
             s_ref[g * points + i] = u[i + 1]
         s_ref[(g + 1) * points - 1] = identity(width)
+    for move in moves:
+        move.wait()
 
 
 def prefix_kernel(split, r_ref, p_ref, l_ref):
@@ -227,48 +228,74 @@
     inj_hi, cap_hi, gain_hi, bnd_hi = vectors(small_ref, 1, points)
     nr_lo = negative_residual(s_lo, halo_lo, inj_lo, cap_lo, gain_lo, lo_maps[0])
     nr_hi = negative_residual(s_hi, halo_hi, inj_hi, cap_hi, gain_hi, hi_maps[0])
-    c_lo = mapped_each(d_lo, nr_lo)
-    c_hi = pair_corrected(nr_hi, s_lo, c_lo, bnd_lo, d_hi, hi_maps[2], hi_maps[1])
     nr_ref[:points], nr_ref[points:] = nr_lo, nr_hi
-    c_ref[:points], c_ref[points:] = c_lo, c_hi
-    msg_ref[:points] = taken(c_hi, bnd_hi)
     msg_ref[points:] = taken(s_hi, bnd_hi)
 
-
-def early_kernel(
-    s_lo, s_hi, pack_lo, pack_hi, d_lo, d_hi, _, maps_ref, small_ref, nr_ref, c_ref, msg_ref
-):
+    @pl.when(in_first_pair())
+    def _():
+        c_lo = mapped_each(d_lo, nr_lo)
+        c_hi = pair_corrected(nr_hi, s_lo, c_lo, bnd_lo, d_hi, hi_maps[2], hi_maps[1])
+        c_ref[:points], c_ref[points:] = c_lo, c_hi
+        msg_ref[:points] = taken(c_hi, bnd_hi)
+
+    @pl.when(jnp.logical_not(in_first_pair()))
+    def _():
+        c_ref[...] = jnp.zeros(c_ref.shape, F32)
+        msg_ref[:points] = jnp.zeros((points, c_ref.shape[1]), F32)
+
+
+def early_kernel(s_lo, s_hi, pack_lo, pack_hi, _, maps_ref, small_ref, nr_ref):
     points, width = s_lo.shape
     for i in range(3):
         rows = slice(i * width, (i + 1) * width)
         maps_ref[i] = split_cols(pack_lo[rows])
         maps_ref[3 + i] = split_cols(pack_hi[rows])
-    small_ref[: points + 24] = pack_lo[3 * width :]
-    small_ref[points + 24 :] = pack_hi[3 * width :]
     none = jnp.zeros((1, width), F32)
-    correct_both(
-        s_lo[...], s_hi[...], none, none, small_ref, maps_ref, d_lo, d_hi, nr_ref, c_ref, msg_ref
-    )
+    for g, (s_ref, pack) in enumerate(((s_lo, pack_lo), (s_hi, pack_hi))):
+        at = g * (points + 24)
+        small_ref[at : at + points + 24] = pack[3 * width :]
+        inj, cap, gain, _ = vectors(small_ref, g, points)
+        nr_ref[g * points : (g + 1) * points] = negative_residual(
+            s_ref[...], none, inj, cap, gain, maps_ref[3 * g]
+        )
+
+
+def diagonal_kernel(lo_ref, hi_ref, d_lo, d_hi, sems):
+    for move in fetched((lo_ref, hi_ref), (d_lo, d_hi), sems):
+        move.wait()
+
+
+def in_first_pair():
+    return lax.axis_index("dom") < PAIR
 
 
 def first_kernel(
-    halo_ref, s_lo, s_hi, small_ref, maps_ref, d_lo, d_hi, old_nr, old_c, old_msg,
-    s_ref, nr_ref, c_ref, msg_ref,
+    halo_ref, s_lo, s_hi, small_ref, maps_ref, d_lo, d_hi, old_nr, s_ref, nr_ref, c_ref, msg_ref
 ):
     points = s_lo.shape[0]
-    _, cap_lo, _, bnd_lo = vectors(small_ref, 0, points)
-    _, cap_hi, _, bnd_hi = vectors(small_ref, 1, points)
+    bnd_lo, bnd_hi = (vectors(small_ref, g, points)[3] for g in range(PAIR))
     s_ref[:points], s_ref[points:] = s_lo[...], s_hi[...]
-    nr_ref[...], c_ref[...], msg_ref[...] = old_nr[...], old_c[...], old_msg[...]
-    nr_lo = old_nr[:1] + cap_lo * halo_ref[:1]
-    nr_hi = old_nr[points : points + 1] + cap_hi * halo_ref[4:5]
-    c_lo = mapped_each(d_lo, nr_lo)
-    came = mapped(maps_ref[5], taken(jnp.broadcast_to(c_lo, (8, c_lo.shape[1])), bnd_lo))
-    came = came + mapped(maps_ref[4], taken(s_lo[:8], bnd_lo))
-    c_hi = mapped_each(d_hi, nr_hi + came[:1])
-    nr_ref[:1], nr_ref[points : points + 1] = nr_lo, nr_hi
-    c_ref[:1], c_ref[points : points + 1] = c_lo, c_hi
-    msg_ref[:1] = taken(jnp.broadcast_to(c_hi, (8, c_hi.shape[1])), bnd_hi)[:1]
+    msg_ref[points:] = taken(s_hi[...], bnd_hi)
+    nr_ref[...] = old_nr[...]
+    for g in range(PAIR):
+        at = g * points
+        cap = vectors(small_ref, g, points)[1]
+        nr_ref[at : at + 1] = old_nr[at : at + 1] + cap * halo_ref[4 * g : 4 * g + 1]
+
+    @pl.when(in_first_pair())
+    def _():
+        c_lo = mapped_each(d_lo, nr_ref[:points])
+        linked = mapped(maps_ref[4], taken(s_lo[...], bnd_lo))
+        c_hi = mapped_each(
+            d_hi, nr_ref[points:] + linked + mapped(maps_ref[5], taken(c_lo, bnd_lo))
+        )
+        c_ref[:points], c_ref[points:] = c_lo, c_hi
+        msg_ref[:points] = taken(c_hi, bnd_hi)
+
+    @pl.when(jnp.logical_not(in_first_pair()))
+    def _():
+        c_ref[...] = jnp.zeros(c_ref.shape, F32)
+        msg_ref[:points] = jnp.zeros((points, c_ref.shape[1]), F32)
 
 
 def second_kernel(
@@ -369,7 +396,7 @@
 
 
 def next_sums_kernel(
-    distance, mf_ref, gf_ref, bf_ref, af_ref, a_ref, x_ref, tf_ref, nbf_ref, naf_ref
+    distance, mf_ref, gf_ref, bf_ref, af_ref, a_ref, x_ref, _, tf_ref, nbf_ref, naf_ref
 ):
     later = is_later(distance)
     for wide, short in sections(a_ref.shape[0] // PAIR):
@@ -413,10 +440,17 @@
     )
 
 
+def scan_kernel(c_ref, l_lo, l_hi, s_ref, base_ref):
+    points = s_ref.shape[0] // PAIR
+    for g, l_ref in enumerate((l_lo, l_hi)):
+        rows = slice(g * points, (g + 1) * points)
+        base_ref[rows] = s_ref[rows] + scanned(c_ref[rows], l_ref)
+
+
 def last_local_kernel(
-    c_ref, l_lo, l_hi, tail_ref, aw_ref, af_ref, gw_ref, bw_ref, bf_ref, p_lo, p_hi, s_ref, base_ref
-):
-    points, width = s_ref.shape[0] // PAIR, s_ref.shape[1]
+    tail_ref, aw_ref, af_ref, gw_ref, bw_ref, bf_ref, p_lo, p_hi, old_ref, base_ref
+):
+    points, width = old_ref.shape[0] // PAIR, old_ref.shape[1]
     came = []
     for g, (wide, short) in enumerate(sections(width)):
         at = g * (points + 8)
@@ -426,7 +460,7 @@
     for g in range(PAIR):
         rows = slice(g * points, (g + 1) * points)
         moved = mapped_each_split(p_hi[...], came[g]) if g else mapped_each(p_lo, came[g])
-        base_ref[rows] = s_ref[rows] + moved + scanned(c_ref[rows], (l_lo, l_hi)[g])
+        base_ref[rows] = old_ref[rows] + moved
 
 
 def end_kernel(gf_ref, bw_ref, p_lo, p_hi, base_ref, s_ref):
@@ -481,14 +515,14 @@
             )
         return call(
             functools.partial(next_sums_kernel, distances[level]), [eight] * 3,
-            f, got, bf, af, *kept[level],
+            f, got, bf, af, *kept[level], beside[1],
             cost=pl.CostEstimate(flops=2**33, bytes_accessed=2**25, transcendentals=0),
         )
 
     got = swapped(msg, 2)
     got_w = exchanged(w, distances[0])
-    ss, r_lo, r_hi = call(
-        suffix_kernel, [many] + [((points, width, width), F32)] * 2, r_lo, r_hi,
+    ss, d_lo, d_hi = call(
+        suffix_kernel, [many] + [((points, width, width), F32)] * 2, r_lo, r_hi, d_lo, d_hi,
         in_hbm=2, scratch=[pltpu.SemaphoreType.DMA((2,))],
     )
     l_shape = ((steps, width, width), F32)
@@ -529,10 +563,11 @@
         second_kernel, [vec, eight], got, s, nr, c, small, maps, d_lo, d_hi, ss
     )
     (tail,) = call(tail_kernel, [longer], c, ss)
+    (base,) = call(scan_kernel, [vec], c, l_lo, l_hi, s)
     for level in range(len(distances) - 1):
-        f, bf, af = sums_level(level, f, bf, af, (tail, tail))
+        f, bf, af = sums_level(level, f, bf, af, (tail, base))
     got = exchanged(f, distances[-1])
-    (base,) = call(last_local_kernel, [vec], c, l_lo, l_hi, tail, aw, af, last, bw, bf, p_lo, p_hi, s)
+    (base,) = call(last_local_kernel, [vec], tail, aw, af, last, bw, bf, p_lo, p_hi, base)
     return call(end_kernel, [vec], got, bw, p_lo, p_hi, base)[0]
 
 
@@ -576,14 +611,17 @@
         whole_kernel, [((PAIR * width, width), F32)], near_r, r, in_hbm=2,
         scratch=[pltpu.VMEM((points, width, width), F32)] * 2 + [pltpu.SemaphoreType.DMA((2,))],
     )
-    maps, small, nr, c, msg = call(
+    maps, small, nr = call(
         early_kernel,
-        [((6, width, 2 * width), BF16), ((PAIR * (points + 24), width), F32), vec, vec, vec],
-        near_s, s, near_pack, pack, near_d, d, w,
+        [((6, width, 2 * width), BF16), ((PAIR * (points + 24), width), F32), vec],
+        near_s, s, near_pack, pack, w,
+    )
+    d_lo, d_hi = call(
+        diagonal_kernel, [((points, width, width), F32)] * 2, near_d, d,
+        in_hbm=2, scratch=[pltpu.SemaphoreType.DMA((2,))],
     )
     s, nr, c, msg = call(
-        first_kernel, [vec] * 4,
-        halo, near_s, s, small, maps, near_d, d, nr, c, msg,
+        first_kernel, [vec] * 4, halo, near_s, s, small, maps, d_lo, d_hi, nr
     )
     odd = lax.axis_index("dom") % 2 == 1
     both = lax.cond(

time: 44.1 us -> 42.9 us (0.973)
  starting transfers between devices: 35.8 us -> 34.3 us
  waiting for transfers between devices: 2.17 us -> 2.69 us
    ppermute x5, starting transfers between devices: 33.1 us -> 31.7 us  [swapped(): lax.ppermute(value, 'dom', [(i, i ^ distance) for i in range(lax.axis_siz...]
    ppermute x1, waiting for transfers between devices: 0.94 us -> 1.46 us  [per_device(): lax.ppermute(rows, 'tm', [(i, (i + 1) % segments) for i in range(segments)])]
    pallas_call x7 -> x8, Pallas kernels: 4.75 us -> 4.75 us  [call(): pl.pallas_call(kernel, out_shape=[jax.ShapeDtypeStruct(s, d) for s, d in...]
  transfers between devices with their start and end apart: 6 -> 6, of which waited for: 3 -> 3; matrix products, arithmetic and copies ran while one was open for 0% -> 0% of each run, Pallas kernels for 8% -> 7%
where the time goes in v3:
time: 42.9 us; the launch traced here: 42.8 us
  starting transfers between devices  34.3 us (80%)
  Pallas kernels  4.75 us (11%)
  waiting for transfers between devices  2.69 us (6%)
  between operations  0.77 us (2%)
    ppermute x5, starting transfers between devices, swapped(): lax.ppermute(value, 'dom', [(i, i ^ distance) for i in range(lax.axis_siz...  31.7 us
    pallas_call x8, Pallas kernels, call(): pl.pallas_call(kernel, out_shape=[jax.ShapeDtypeStruct(s, d) for s, d in...  4.75 us
    ppermute x1, starting transfers between devices, per_device(): lax.ppermute(rows, 'tm', [(i, (i + 1) % segments) for i in range(segments)])  2.68 us
    ppermute x1, waiting for transfers between devices, per_device(): lax.ppermute(rows, 'tm', [(i, (i + 1) % segments) for i in range(segments)])  1.46 us
    ppermute x5, waiting for transfers between devices, swapped(): lax.ppermute(value, 'dom', [(i, i ^ distance) for i in range(lax.axis_siz...  1.23 us
  transfers between devices with their start and end apart: 6, of which 3 were waited for; matrix products, arithmetic and copies ran while one was open for 0% of the time, Pallas kernels for 7%

profile of v3, /device:TPU:0, one launch (start us, length us, event | category | flops | bytes accessed | tf_op | source)
XLA Modules:
  0.0 42.8 jit_solution(13374905754223543966)
XLA Ops:
  0.0 0.0 copy-start.1
  0.0 0.0 copy-start.5
  0.0 0.0 copy-start.6
  0.0 0.0 copy-start.7
  0.0 0.0 copy-start
  0.1 0.5 %collective-permute-start.11 = (f32[16,1,128]{2,0,1:T(8,128)}, f32[16,1,128]{2,0,1:T(8,128)S(1)}, u32[]{:S(2)}, u32[]{:S(2)}) collective-permute-start(f32[16,1,128]{2,0,1:T(8,128)} %bitcast.17), channel_id=1, source_target_pairs={{0,1},{1,0},{2,3},{3,2},{4,5},{5,4},{6,7},{7,6},{8,9},{9,8},{10,11... | collective-permute-start | bytes 24584 | tf_op jit(solution)/shard_map/ppermute | solution.py:494
  1.2 0.4 collective-permute-done.11
  1.6 0.0 copy-done.8
  1.6 0.3 collective-permute-start.14
  2.0 0.2 collective-permute-start.15
  2.1 0.0 copy-done.1
  2.1 0.0 copy-done.2
  2.1 0.0 copy-done.3
  2.2 0.0 copy-done.4
  2.2 0.0 copy-done.5
  2.2 0.0 copy-done.6
  2.2 0.0 copy-done.7
  2.2 0.4 collective-permute-start.13
  2.6 0.0 copy-done
  2.6 2.7 %collective-permute-start.12 = (f32[8,128]{1,0:T(8,128)S(1)}, f32[8,128]{1,0:T(8,128)S(1)}, u32[]{:S(2)}, u32[]{:S(2)}) collective-permute-start(f32[8,128]{1,0:T(8,128)S(1)} %shard_map.110), channel_id=1, source_target_pairs={{0,4},{4,8},{8,12},{12,16},{16,20},{20,24},{24,28},{28,0},{1,5},{5... | collective-permute-start | bytes 12296 | tf_op jit(solution)/shard_map/ppermute | solution.py:602
  5.3 0.0 collective-permute-done.14
  5.3 1.4 %shard_map.112._ = f32[256,128]{1,0:T(8,128)S(1)} custom-call(f32[16,128,128]{2,1,0:T(8,128)S(1)} %bitcast.31, f32[16,128,128]{2,1,0:T(8,128)S(1)} %bitcast.29), custom_call_target="tpu_custom_call" | custom-call | tf_op jit(solution)/shard_map/pallas_call | solution.py:79
  6.7 0.0 collective-permute-done.15
  6.7 1.6 %shard_map.114 = (f32[16,128,128]{2,1,0:T(8,128)S(1)}, f32[16,128,128]{2,1,0:T(8,128)S(1)}) custom-call(f32[16,128,128]{2,1,0:T(8,128)} %bitcast.12.lo_ref, f32[16,128,128]{2,1,0:T(8,128)} %bitcast.13.hi_ref), custom_call_target="tpu_custom_call" | custom-call | tf_op jit(solution)/shard_map/pallas_call | solution.py:79
  8.3 0.0 collective-permute-done.13.pack_lo
  8.3 0.2 shard_map.113
  8.5 1.5 %collective-permute-done.12.halo_ref = f32[8,128]{1,0:T(8,128)S(1)} collective-permute-done((f32[8,128]{1,0:T(8,128)S(1)}, f32[8,128]{1,0:T(8,128)S(1)}, u32[]{:S(2)}, u32[]{:S(2)}) %collective-permute-start.12) | collective-permute-done | bytes 4128 | tf_op jit(solution)/shard_map/ppermute | solution.py:602
  9.9 1.0 %shard_map.115 = (f32[32,128]{1,0:T(8,128)S(1)}, f32[32,128]{1,0:T(8,128)S(1)}, f32[32,128]{1,0:T(8,128)S(1)}, f32[32,128]{1,0:T(8,128)S(1)}) custom-call(f32[8,128]{1,0:T(8,128)S(1)} %collective-permute-done.12.halo_ref, f32[16,128]{1,0:T(8,128)S(1)} %bitcast.23, f32[16,128]{1,0:T(8,128)S(1)} %bitcast.20, f32[80,128]{1,0:T(8,128)S(1)} %get-tuple-element.101.small_ref, ...), custom_call_target="tpu_custom_call" | custom-call | tf_op jit(solution)/shard_map/pallas_call | solution.py:79
  10.9 0.2 conditional.1
  11.1 30.2 %collective-permute-start.16 = (f32[32,128]{1,0:T(8,128)S(1)}, f32[32,128]{1,0:T(8,128)S(1)}, u32[]{:S(2)}, u32[]{:S(2)}) collective-permute-start(f32[32,128]{1,0:T(8,128)S(1)} %get-tuple-element.111.both_ref), channel_id=1, source_target_pairs={{0,1},{1,0},{2,3},{3,2},{4,5},{5,4},{6,7},{7,6},{8,9},{9,8},{10,11... | collective-permute-start | bytes 49160 | tf_op jit(solution)/shard_map/ppermute | solution.py:494
  41.3 0.8 %collective-permute-done.16.got_ref = f32[32,128]{1,0:T(8,128)S(1)} collective-permute-done((f32[32,128]{1,0:T(8,128)S(1)}, f32[32,128]{1,0:T(8,128)S(1)}, u32[]{:S(2)}, u32[]{:S(2)}) %collective-permute-start.16) | collective-permute-done | bytes 16416 | tf_op jit(solution)/shard_map/ppermute | solution.py:494
  42.2 0.6 %shard_map.116 = f32[16,128]{1,0:T(8,128)} custom-call(f32[32,128]{1,0:T(8,128)S(1)} %get-tuple-element.111.both_ref, f32[32,128]{1,0:T(8,128)S(1)} %collective-permute-done.16.got_ref), custom_call_target="tpu_custom_call" | custom-call | tf_op jit(solution)/shard_map/pallas_call | solution.py:79
  (8 shorter events, 0.0 us)
Async XLA Ops:
  0.0 1.6 %copy-start.8 = (f32[16,1,1,128,128]{4,3,2,1,0:T(8,128)S(1)}, f32[16,1,1,128,128]{4,3,2,1,0:T(8,128)}, u32[]{:S(2)}) copy-start(f32[16,1,1,128,128]{4,3,2,1,0:T(8,128)} %param.23) | copy-start | bytes 3145732
  0.0 2.1 %copy-start.1 = (f32[1,128,128]{2,1,0:T(8,128)S(1)}, f32[1,128,128]{2,1,0:T(8,128)}, u32[]{:S(2)}) copy-start(f32[1,128,128]{2,1,0:T(8,128)} %param.16) | copy-start | bytes 196612
  0.0 2.1 %copy-start.2 = (f32[1,128,128]{2,1,0:T(8,128)S(1)}, f32[1,128,128]{2,1,0:T(8,128)}, u32[]{:S(2)}) copy-start(f32[1,128,128]{2,1,0:T(8,128)} %param.19) | copy-start | bytes 196612
  0.0 2.1 %copy-start.3 = (f32[1,128,128]{2,1,0:T(8,128)S(1)}, f32[1,128,128]{2,1,0:T(8,128)}, u32[]{:S(2)}) copy-start(f32[1,128,128]{2,1,0:T(8,128)} %param.22) | copy-start | bytes 196612
  0.0 2.1 %copy-start.4 = (f32[16,1,128]{2,1,0:T(1,128)S(1)}, f32[16,1,128]{2,1,0:T(1,128)}, u32[]{:S(2)}) copy-start(f32[16,1,128]{2,1,0:T(1,128)} %param.14) | copy-start | bytes 24580
  0.0 2.1 %copy-start.5 = (f32[1,128]{1,0:T(1,128)S(1)}, f32[1,128]{1,0:T(1,128)}, u32[]{:S(2)}) copy-start(f32[1,128]{1,0:T(1,128)} %cap_ref.1) | copy-start | bytes 1540
  0.0 2.1 %copy-start.6 = (f32[1,128]{1,0:T(1,128)S(1)}, f32[1,128]{1,0:T(1,128)}, u32[]{:S(2)}) copy-start(f32[1,128]{1,0:T(1,128)} %gain_ref.1) | copy-start | bytes 1540
  0.0 2.1 %copy-start.7 = (s32[1,128]{1,0:T(1,128)S(1)}, s32[1,128]{1,0:T(1,128)}, u32[]{:S(2)}) copy-start(s32[1,128]{1,0:T(1,128)} %bnd_ref.1) | copy-start | bytes 1540
  0.0 2.6 %copy-start = (f32[16,1,128]{2,1,0:T(1,128)S(1)}, f32[16,1,128]{2,1,0:T(1,128)}, u32[]{:S(2)}) copy-start(f32[16,1,128]{2,1,0:T(1,128)} %param.13) | copy-start | bytes 24580
  0.1 1.6 %collective-permute-start.11 = (f32[16,1,128]{2,0,1:T(8,128)}, f32[16,1,128]{2,0,1:T(8,128)S(1)}, u32[]{:S(2)}, u32[]{:S(2)}) collective-permute-start(f32[16,1,128]{2,0,1:T(8,128)} %bitcast.17), channel_id=1, source_target_pairs={{0,1},{1,0},{2,3},{3,2},{4,5},{5,4},{6,7},{7,6},{8,9},{9,8},{10,11... | collective-permute-start | bytes 24584 | tf_op jit(solution)/shard_map/ppermute | solution.py:494
  1.6 3.7 %collective-permute-start.14 = (f32[16,1,1,128,128]{4,3,0,2,1:T(8,128)S(1)}, f32[16,1,1,128,128]{4,3,0,2,1:T(8,128)S(1)}, u32[]{:S(2)}, u32[]{:S(2)}) collective-permute-start(f32[16,1,1,128,128]{4,3,0,2,1:T(8,128)S(1)} %bitcast.28), channel_id=1, source_target_pairs={{0,1},{1,0},{2,3},{3,2},{4,5},{5,4},{6,7},{7,6},{8,9},{9,8},{10,11... | collective-permute-start | bytes 3145736 | tf_op jit(solution)/shard_map/ppermute | solution.py:494
  2.0 4.7 %collective-permute-start.15 = (f32[16,1,1,128,128]{4,3,0,2,1:T(8,128)}, f32[16,1,1,128,128]{4,3,0,2,1:T(8,128)}, u32[]{:S(2)}, u32[]{:S(2)}) collective-permute-start(f32[16,1,1,128,128]{4,3,0,2,1:T(8,128)} %bitcast.11), channel_id=1, source_target_pairs={{0,1},{1,0},{2,3},{3,2},{4,5},{5,4},{6,7},{7,6},{8,9},{9,8},{10,11... | collective-permute-start | bytes 3145736 | tf_op jit(solution)/shard_map/ppermute | solution.py:494
  2.2 6.1 %collective-permute-start.13 = (f32[424,128]{1,0:T(8,128)S(1)}, f32[424,128]{1,0:T(8,128)S(1)}, u32[]{:S(2)}, u32[]{:S(2)}) collective-permute-start(f32[424,128]{1,0:T(8,128)S(1)} %shard_map.111.pack_hi), channel_id=1, source_target_pairs={{0,1},{1,0},{2,3},{3,2},{4,5},{5,4},{6,7},{7,6},{8,9},{9,8},{10,11... | collective-permute-start | bytes 651272 | tf_op jit(solution)/shard_map/ppermute | solution.py:494
  2.6 7.3 %collective-permute-start.12 = (f32[8,128]{1,0:T(8,128)S(1)}, f32[8,128]{1,0:T(8,128)S(1)}, u32[]{:S(2)}, u32[]{:S(2)}) collective-permute-start(f32[8,128]{1,0:T(8,128)S(1)} %shard_map.110), channel_id=1, source_target_pairs={{0,4},{4,8},{8,12},{12,16},{16,20},{20,24},{24,28},{28,0},{1,5},{5... | collective-permute-start | bytes 12296 | tf_op jit(solution)/shard_map/ppermute | solution.py:602
  11.1 31.0 %collective-permute-start.16 = (f32[32,128]{1,0:T(8,128)S(1)}, f32[32,128]{1,0:T(8,128)S(1)}, u32[]{:S(2)}, u32[]{:S(2)}) collective-permute-start(f32[32,128]{1,0:T(8,128)S(1)} %get-tuple-element.111.both_ref), channel_id=1, source_target_pairs={{0,1},{1,0},{2,3},{3,2},{4,5},{5,4},{6,7},{7,6},{8,9},{9,8},{10,11... | collective-permute-start | bytes 49160 | tf_op jit(solution)/shard_map/ppermute | solution.py:494

commit v4 on v3

--- a/solution.py
+++ b/solution.py
@@ -151,15 +151,20 @@
 def suffix_kernel(r_lo, r_hi, lo_ref, hi_ref, s_ref, d_lo, d_hi, sems):
     points, width = r_lo.shape[0], r_lo.shape[1]
     moves = fetched((lo_ref, hi_ref), (d_lo, d_hi), sems)
-    for g, r_ref in enumerate((r_lo, r_hi)):
-        u = [r_ref[i] for i in range(points)]
-        span = 1
-        while span < points:
-            for base in range(0, points, 2 * span):
-                prod = times(u[base + span], jnp.concatenate(u[base : base + span], axis=1))
-                for i in range(span):
-                    u[base + i] = prod[:, i * width : (i + 1) * width]
-            span *= 2
+    both = [[r_ref[i] for i in range(points)] for r_ref in (r_lo, r_hi)]
+    span = 1
+    while span < points:
+        for base in range(0, points, 2 * span):
+            first = max(base, 1)
+            if first == base + span:
+                continue
+            for u in both:
+                prod = times(u[base + span], jnp.concatenate(u[first : base + span], axis=1))
+                for i in range(first, base + span):
+                    at = (i - first) * width
+                    u[i] = prod[:, at : at + width]
+        span *= 2
+    for g, u in enumerate(both):
         for i in range(points - 1):
             s_ref[g * points + i] = u[i + 1]
         s_ref[(g + 1) * points - 1] = identity(width)
@@ -167,25 +172,28 @@
         move.wait()
 
 
-def prefix_kernel(split, r_ref, p_ref, l_ref):
-    points, width = r_ref.shape[0], r_ref.shape[1]
-    q = [r_ref[i] for i in range(points)]
+def prefix_kernel(r_lo, r_hi, p_lo, l_lo, p_hi, l_hi):
+    points, width = r_lo.shape[0], r_lo.shape[1]
+    both = [[r_ref[i] for i in range(points)] for r_ref in (r_lo, r_hi)]
     span, slot = 1, 0
     while span < points:
         for base in range(0, points, 2 * span):
-            upper = q[base + span : base + 2 * span]
-            for matrix in upper:
-                l_ref[slot] = matrix
-                slot += 1
-            prod = times(jnp.concatenate(upper, axis=0), q[base + span - 1])
-            for i in range(span):
-                q[base + span + i] = prod[i * width : (i + 1) * width]
+            for q, l_ref in zip(both, (l_lo, l_hi)):
+                upper = q[base + span : base + 2 * span]
+                for i, matrix in enumerate(upper):
+                    if l_ref is l_hi:
+                        at = (slot + i) * width
+                        l_ref[at : at + width] = split_cols(matrix)
+                    else:
+                        l_ref[slot + i] = matrix
+                prod = times(jnp.concatenate(upper, axis=0), q[base + span - 1])
+                for i in range(span):
+                    q[base + span + i] = prod[i * width : (i + 1) * width]
+            slot += span
         span *= 2
     for i in range(points):
-        if split:
-            p_ref[i * width : (i + 1) * width] = split_cols(q[i])
-        else:
-            p_ref[i] = q[i]
+        p_lo[i] = both[0][i]
+        p_hi[i * width : (i + 1) * width] = split_cols(both[1][i])
 
 
 def scanned(c, l_ref):
@@ -199,6 +207,23 @@
                 x[i] = x[i] + mapped_each(l_ref[slot : slot + 1], head)
                 slot += 1
         span *= 2
+    return jnp.concatenate(x, axis=0)
+
+
+def scanned_split(c, l_ref):
+    points, width = c.shape
+    half = points // 2
+    x = [c[i : i + 1, :] for i in range(points)]
+    span, level = 1, 0
+    while span < points:
+        later = [i for i in range(points) if i & span]
+        heads = jnp.concatenate([x[(i & ~(2 * span - 1)) + span - 1] for i in later], axis=0)
+        rows = slice(level * half * width, (level + 1) * half * width)
+        moved = mapped_each_split(l_ref[rows], heads)
+        for slot, i in enumerate(later):
+            x[i] = x[i] + moved[slot : slot + 1]
+        span *= 2
+        level += 1
     return jnp.concatenate(x, axis=0)
 
 
@@ -260,7 +285,7 @@
         )
 
 
-def diagonal_kernel(lo_ref, hi_ref, d_lo, d_hi, sems):
+def diagonal_kernel(_, lo_ref, hi_ref, d_lo, d_hi, sems):
     for move in fetched((lo_ref, hi_ref), (d_lo, d_hi), sems):
         move.wait()
 
@@ -412,7 +437,8 @@
     for g, (wide, short) in enumerate(sections(width)):
         rows = slice(g * points, (g + 1) * points)
         long = slice(g * (points + 8), (g + 1) * (points + 8))
-        base_ref[rows] = s_ref[rows] + scanned(c_ref[rows], (l_lo, l_hi)[g])
+        scan = scanned_split if g else scanned
+        base_ref[rows] = s_ref[rows] + scan(c_ref[rows], (l_lo, l_hi)[g])
         v_ref[long] = mapped(split_cols(aw_ref[wide]), tail_ref[long]) + af_ref[short][:1]
 
 
@@ -442,9 +468,9 @@
 
 def scan_kernel(c_ref, l_lo, l_hi, s_ref, base_ref):
     points = s_ref.shape[0] // PAIR
-    for g, l_ref in enumerate((l_lo, l_hi)):
+    for g, (scan, l_ref) in enumerate(((scanned, l_lo), (scanned_split, l_hi))):
         rows = slice(g * points, (g + 1) * points)
-        base_ref[rows] = s_ref[rows] + scanned(c_ref[rows], l_ref)
+        base_ref[rows] = s_ref[rows] + scan(c_ref[rows], l_ref)
 
 
 def last_local_kernel(
@@ -525,12 +551,11 @@
         suffix_kernel, [many] + [((points, width, width), F32)] * 2, r_lo, r_hi, d_lo, d_hi,
         in_hbm=2, scratch=[pltpu.SemaphoreType.DMA((2,))],
     )
-    l_shape = ((steps, width, width), F32)
-    p_lo, l_lo = call(
-        functools.partial(prefix_kernel, False), [((points, width, width), F32), l_shape], r_lo
-    )
-    p_hi, l_hi = call(
-        functools.partial(prefix_kernel, True), [((points * width, 2 * width), BF16), l_shape], r_hi
+    p_lo, l_lo, p_hi, l_hi = call(
+        prefix_kernel,
+        [((points, width, width), F32), ((steps, width, width), F32)]
+        + [((points * width, 2 * width), BF16), ((steps * width, 2 * width), BF16)],
+        r_lo, r_hi,
     )
     c, f = call(
         second_kernel, [vec, eight], got, s, nr, c, small, maps, d_lo, d_hi, ss
@@ -617,7 +642,7 @@
         near_s, s, near_pack, pack, w,
     )
     d_lo, d_hi = call(
-        diagonal_kernel, [((points, width, width), F32)] * 2, near_d, d,
+        diagonal_kernel, [((points, width, width), F32)] * 2, nr, near_d, d,
         in_hbm=2, scratch=[pltpu.SemaphoreType.DMA((2,))],
     )
     s, nr, c, msg = call(

time: 42.9 us -> 41.7 us (0.972)
  starting transfers between devices: 34.3 us -> 33.3 us
    ppermute x5, starting transfers between devices: 31.7 us -> 30.6 us  [swapped(): lax.ppermute(value, 'dom', [(i, i ^ distance) for i in range(lax.axis_siz...]
  transfers between devices with their start and end apart: 6 -> 6, of which waited for: 3 -> 3; matrix products, arithmetic and copies ran while one was open for 0% -> 0% of each run, Pallas kernels for 7% -> 8%
where the time goes in v4:
time: 41.7 us; the launch traced here: 41.5 us
  starting transfers between devices  33.3 us (80%)
  Pallas kernels  4.75 us (11%)
  waiting for transfers between devices  2.69 us (6%)
  between operations  0.76 us (2%)
    ppermute x5, starting transfers between devices, swapped(): lax.ppermute(value, 'dom', [(i, i ^ distance) for i in range(lax.axis_siz...  30.6 us
    pallas_call x8, Pallas kernels, call(): pl.pallas_call(kernel, out_shape=[jax.ShapeDtypeStruct(s, d) for s, d in...  4.75 us
    ppermute x1, starting transfers between devices, per_device(): lax.ppermute(rows, 'tm', [(i, (i + 1) % segments) for i in range(segments)])  2.68 us
    ppermute x1, waiting for transfers between devices, per_device(): lax.ppermute(rows, 'tm', [(i, (i + 1) % segments) for i in range(segments)])  1.46 us
    ppermute x5, waiting for transfers between devices, swapped(): lax.ppermute(value, 'dom', [(i, i ^ distance) for i in range(lax.axis_siz...  1.23 us
  transfers between devices with their start and end apart: 6, of which 3 were waited for; matrix products, arithmetic and copies ran while one was open for 0% of the time, Pallas kernels for 8%

profile of v4, /device:TPU:0, one launch (start us, length us, event | category | flops | bytes accessed | tf_op | source)
XLA Modules:
  0.0 41.5 jit_solution(6545457154956596381)
XLA Ops:
  0.0 0.0 copy-start.8
  0.0 0.0 copy-start.1
  0.0 0.0 copy-start.5
  0.0 0.0 copy-start.6
  0.0 0.0 copy-start.7
  0.0 0.0 copy-start
  0.1 0.5 %collective-permute-start.11 = (f32[16,1,128]{2,0,1:T(8,128)}, f32[16,1,128]{2,0,1:T(8,128)S(1)}, u32[]{:S(2)}, u32[]{:S(2)}) collective-permute-start(f32[16,1,128]{2,0,1:T(8,128)} %bitcast.17), channel_id=1, source_target_pairs={{0,1},{1,0},{2,3},{3,2},{4,5},{5,4},{6,7},{7,6},{8,9},{9,8},{10,11... | collective-permute-start | bytes 24584 | tf_op jit(solution)/shard_map/ppermute | solution.py:520
  1.2 0.4 collective-permute-done.11
  1.6 0.0 copy-done.8
  1.6 0.3 collective-permute-start.14
  2.0 0.2 collective-permute-start.15
  2.1 0.0 copy-done.1
  2.1 0.0 copy-done.2
  2.1 0.0 copy-done.3
  2.2 0.0 copy-done.4
  2.2 0.0 copy-done.5
  2.2 0.0 copy-done.6
  2.2 0.0 copy-done.7
  2.2 0.4 collective-permute-start.13
  2.6 0.0 copy-done
  2.6 2.7 %collective-permute-start.12 = (f32[8,128]{1,0:T(8,128)S(1)}, f32[8,128]{1,0:T(8,128)S(1)}, u32[]{:S(2)}, u32[]{:S(2)}) collective-permute-start(f32[8,128]{1,0:T(8,128)S(1)} %shard_map.110), channel_id=1, source_target_pairs={{0,4},{4,8},{8,12},{12,16},{16,20},{20,24},{24,28},{28,0},{1,5},{5... | collective-permute-start | bytes 12296 | tf_op jit(solution)/shard_map/ppermute | solution.py:627
  5.3 0.0 collective-permute-done.14
  5.3 1.4 %shard_map.112._ = f32[256,128]{1,0:T(8,128)S(1)} custom-call(f32[16,128,128]{2,1,0:T(8,128)S(1)} %bitcast.31, f32[16,128,128]{2,1,0:T(8,128)S(1)} %bitcast.29), custom_call_target="tpu_custom_call" | custom-call | tf_op jit(solution)/shard_map/pallas_call | solution.py:79
  6.7 0.0 collective-permute-done.13.pack_lo
  6.7 0.2 shard_map.113
  6.9 0.0 collective-permute-done.15
  6.9 1.6 %shard_map.114 = (f32[16,128,128]{2,1,0:T(8,128)S(1)}, f32[16,128,128]{2,1,0:T(8,128)S(1)}) custom-call(f32[32,128]{1,0:T(8,128)S(1)} %get-tuple-element.103._.old_nr, f32[16,128,128]{2,1,0:T(8,128)} %bitcast.12.lo_ref, f32[16,128,128]{2,1,0:T(8,128)} %bitcast.13.hi_ref), custom_call_target="tpu_custom_call" | custom-call | tf_op jit(solution)/shard_map/pallas_call | solution.py:79
  8.5 1.5 %collective-permute-done.12.halo_ref = f32[8,128]{1,0:T(8,128)S(1)} collective-permute-done((f32[8,128]{1,0:T(8,128)S(1)}, f32[8,128]{1,0:T(8,128)S(1)}, u32[]{:S(2)}, u32[]{:S(2)}) %collective-permute-start.12) | collective-permute-done | bytes 4128 | tf_op jit(solution)/shard_map/ppermute | solution.py:627
  9.9 1.0 %shard_map.115 = (f32[32,128]{1,0:T(8,128)S(1)}, f32[32,128]{1,0:T(8,128)S(1)}, f32[32,128]{1,0:T(8,128)S(1)}, f32[32,128]{1,0:T(8,128)S(1)}) custom-call(f32[8,128]{1,0:T(8,128)S(1)} %collective-permute-done.12.halo_ref, f32[16,128]{1,0:T(8,128)S(1)} %bitcast.23, f32[16,128]{1,0:T(8,128)S(1)} %bitcast.20, f32[80,128]{1,0:T(8,128)S(1)} %get-tuple-element.101.small_ref, ...), custom_call_target="tpu_custom_call" | custom-call | tf_op jit(solution)/shard_map/pallas_call | solution.py:79
  10.9 29.2 %collective-permute-start.16 = (f32[32,128]{1,0:T(8,128)S(1)}, f32[32,128]{1,0:T(8,128)S(1)}, u32[]{:S(2)}, u32[]{:S(2)}) collective-permute-start(f32[32,128]{1,0:T(8,128)S(1)} %get-tuple-element.111.both_ref), channel_id=1, source_target_pairs={{0,1},{1,0},{2,3},{3,2},{4,5},{5,4},{6,7},{7,6},{8,9},{9,8},{10,11... | collective-permute-start | bytes 49160 | tf_op jit(solution)/shard_map/ppermute | solution.py:520
  40.1 0.8 %collective-permute-done.16.got_ref = f32[32,128]{1,0:T(8,128)S(1)} collective-permute-done((f32[32,128]{1,0:T(8,128)S(1)}, f32[32,128]{1,0:T(8,128)S(1)}, u32[]{:S(2)}, u32[]{:S(2)}) %collective-permute-start.16) | collective-permute-done | bytes 16416 | tf_op jit(solution)/shard_map/ppermute | solution.py:520
  40.9 0.6 %shard_map.116 = f32[16,128]{1,0:T(8,128)} custom-call(f32[32,128]{1,0:T(8,128)S(1)} %get-tuple-element.111.both_ref, f32[32,128]{1,0:T(8,128)S(1)} %collective-permute-done.16.got_ref), custom_call_target="tpu_custom_call" | custom-call | tf_op jit(solution)/shard_map/pallas_call | solution.py:79
  (8 shorter events, 0.0 us)
Async XLA Ops:
  0.0 1.6 %copy-start.8 = (f32[16,1,1,128,128]{4,3,2,1,0:T(8,128)S(1)}, f32[16,1,1,128,128]{4,3,2,1,0:T(8,128)}, u32[]{:S(2)}) copy-start(f32[16,1,1,128,128]{4,3,2,1,0:T(8,128)} %param.23) | copy-start | bytes 3145732
  0.0 2.1 %copy-start.1 = (f32[1,128,128]{2,1,0:T(8,128)S(1)}, f32[1,128,128]{2,1,0:T(8,128)}, u32[]{:S(2)}) copy-start(f32[1,128,128]{2,1,0:T(8,128)} %param.16) | copy-start | bytes 196612
  0.0 2.1 %copy-start.2 = (f32[1,128,128]{2,1,0:T(8,128)S(1)}, f32[1,128,128]{2,1,0:T(8,128)}, u32[]{:S(2)}) copy-start(f32[1,128,128]{2,1,0:T(8,128)} %param.19) | copy-start | bytes 196612
  0.0 2.1 %copy-start.3 = (f32[1,128,128]{2,1,0:T(8,128)S(1)}, f32[1,128,128]{2,1,0:T(8,128)}, u32[]{:S(2)}) copy-start(f32[1,128,128]{2,1,0:T(8,128)} %param.22) | copy-start | bytes 196612
  0.0 2.1 %copy-start.4 = (f32[16,1,128]{2,1,0:T(1,128)S(1)}, f32[16,1,128]{2,1,0:T(1,128)}, u32[]{:S(2)}) copy-start(f32[16,1,128]{2,1,0:T(1,128)} %param.14) | copy-start | bytes 24580
  0.0 2.1 %copy-start.5 = (f32[1,128]{1,0:T(1,128)S(1)}, f32[1,128]{1,0:T(1,128)}, u32[]{:S(2)}) copy-start(f32[1,128]{1,0:T(1,128)} %cap_ref.1) | copy-start | bytes 1540
  0.0 2.1 %copy-start.6 = (f32[1,128]{1,0:T(1,128)S(1)}, f32[1,128]{1,0:T(1,128)}, u32[]{:S(2)}) copy-start(f32[1,128]{1,0:T(1,128)} %gain_ref.1) | copy-start | bytes 1540
  0.0 2.1 %copy-start.7 = (s32[1,128]{1,0:T(1,128)S(1)}, s32[1,128]{1,0:T(1,128)}, u32[]{:S(2)}) copy-start(s32[1,128]{1,0:T(1,128)} %bnd_ref.1) | copy-start | bytes 1540
  0.0 2.6 %copy-start = (f32[16,1,128]{2,1,0:T(1,128)S(1)}, f32[16,1,128]{2,1,0:T(1,128)}, u32[]{:S(2)}) copy-start(f32[16,1,128]{2,1,0:T(1,128)} %param.13) | copy-start | bytes 24580
  0.1 1.6 %collective-permute-start.11 = (f32[16,1,128]{2,0,1:T(8,128)}, f32[16,1,128]{2,0,1:T(8,128)S(1)}, u32[]{:S(2)}, u32[]{:S(2)}) collective-permute-start(f32[16,1,128]{2,0,1:T(8,128)} %bitcast.17), channel_id=1, source_target_pairs={{0,1},{1,0},{2,3},{3,2},{4,5},{5,4},{6,7},{7,6},{8,9},{9,8},{10,11... | collective-permute-start | bytes 24584 | tf_op jit(solution)/shard_map/ppermute | solution.py:520
  1.6 3.7 %collective-permute-start.14 = (f32[16,1,1,128,128]{4,3,0,2,1:T(8,128)S(1)}, f32[16,1,1,128,128]{4,3,0,2,1:T(8,128)S(1)}, u32[]{:S(2)}, u32[]{:S(2)}) collective-permute-start(f32[16,1,1,128,128]{4,3,0,2,1:T(8,128)S(1)} %bitcast.28), channel_id=1, source_target_pairs={{0,1},{1,0},{2,3},{3,2},{4,5},{5,4},{6,7},{7,6},{8,9},{9,8},{10,11... | collective-permute-start | bytes 3145736 | tf_op jit(solution)/shard_map/ppermute | solution.py:520
  2.0 4.9 %collective-permute-start.15 = (f32[16,1,1,128,128]{4,3,0,2,1:T(8,128)}, f32[16,1,1,128,128]{4,3,0,2,1:T(8,128)}, u32[]{:S(2)}, u32[]{:S(2)}) collective-permute-start(f32[16,1,1,128,128]{4,3,0,2,1:T(8,128)} %bitcast.11), channel_id=1, source_target_pairs={{0,1},{1,0},{2,3},{3,2},{4,5},{5,4},{6,7},{7,6},{8,9},{9,8},{10,11... | collective-permute-start | bytes 3145736 | tf_op jit(solution)/shard_map/ppermute | solution.py:520
  2.2 4.5 %collective-permute-start.13 = (f32[424,128]{1,0:T(8,128)S(1)}, f32[424,128]{1,0:T(8,128)S(1)}, u32[]{:S(2)}, u32[]{:S(2)}) collective-permute-start(f32[424,128]{1,0:T(8,128)S(1)} %shard_map.111.pack_hi), channel_id=1, source_target_pairs={{0,1},{1,0},{2,3},{3,2},{4,5},{5,4},{6,7},{7,6},{8,9},{9,8},{10,11... | collective-permute-start | bytes 651272 | tf_op jit(solution)/shard_map/ppermute | solution.py:520
  2.6 7.3 %collective-permute-start.12 = (f32[8,128]{1,0:T(8,128)S(1)}, f32[8,128]{1,0:T(8,128)S(1)}, u32[]{:S(2)}, u32[]{:S(2)}) collective-permute-start(f32[8,128]{1,0:T(8,128)S(1)} %shard_map.110), channel_id=1, source_target_pairs={{0,4},{4,8},{8,12},{12,16},{16,20},{20,24},{24,28},{28,0},{1,5},{5... | collective-permute-start | bytes 12296 | tf_op jit(solution)/shard_map/ppermute | solution.py:627
  10.9 30.0 %collective-permute-start.16 = (f32[32,128]{1,0:T(8,128)S(1)}, f32[32,128]{1,0:T(8,128)S(1)}, u32[]{:S(2)}, u32[]{:S(2)}) collective-permute-start(f32[32,128]{1,0:T(8,128)S(1)} %get-tuple-element.111.both_ref), channel_id=1, source_target_pairs={{0,1},{1,0},{2,3},{3,2},{4,5},{5,4},{6,7},{7,6},{8,9},{9,8},{10,11... | collective-permute-start | bytes 49160 | tf_op jit(solution)/shard_map/ppermute | solution.py:520

commit v5 on v4

--- a/solution.py
+++ b/solution.py
@@ -135,9 +135,9 @@
     return moves
 
 
-def whole_kernel(lo_ref, hi_ref, w_ref, r_lo, r_hi, sems):
+def whole_kernel(lo_ref, hi_ref, diag_ref, w_ref, d_hi, r_lo, r_hi, sems):
     points, width = lo_ref.shape[0], lo_ref.shape[1]
-    moves = fetched((lo_ref, hi_ref), (r_lo, r_hi), sems)
+    moves = fetched((lo_ref, hi_ref, diag_ref), (r_lo, r_hi, d_hi), sems)
     u = []
     for move, r_ref in zip(moves, (r_lo, r_hi)):
         move.wait()
@@ -146,6 +146,7 @@
         u = [times(u[i + 1], u[i]) for i in range(0, len(u), 2)]
     for g in range(PAIR):
         w_ref[g * width : (g + 1) * width] = u[g]
+    moves[-1].wait()
 
 
 def suffix_kernel(r_lo, r_hi, lo_ref, hi_ref, s_ref, d_lo, d_hi, sems):
@@ -285,8 +286,8 @@
         )
 
 
-def diagonal_kernel(_, lo_ref, hi_ref, d_lo, d_hi, sems):
-    for move in fetched((lo_ref, hi_ref), (d_lo, d_hi), sems):
+def diagonal_kernel(_, lo_ref, d_lo, sems):
+    for move in fetched((lo_ref,), (d_lo,), sems):
         move.wait()
 
 
@@ -632,18 +633,19 @@
     )
     near_pack = swapped(pack, 1)
     vec = ((PAIR * points, width), F32)
-    (w,) = call(
-        whole_kernel, [((PAIR * width, width), F32)], near_r, r, in_hbm=2,
-        scratch=[pltpu.VMEM((points, width, width), F32)] * 2 + [pltpu.SemaphoreType.DMA((2,))],
+    w, d_hi = call(
+        whole_kernel, [((PAIR * width, width), F32), ((points, width, width), F32)],
+        near_r, r, d, in_hbm=3,
+        scratch=[pltpu.VMEM((points, width, width), F32)] * 2 + [pltpu.SemaphoreType.DMA((3,))],
     )
     maps, small, nr = call(
         early_kernel,
         [((6, width, 2 * width), BF16), ((PAIR * (points + 24), width), F32), vec],
         near_s, s, near_pack, pack, w,
     )
-    d_lo, d_hi = call(
-        diagonal_kernel, [((points, width, width), F32)] * 2, nr, near_d, d,
-        in_hbm=2, scratch=[pltpu.SemaphoreType.DMA((2,))],
+    (d_lo,) = call(
+        diagonal_kernel, [((points, width, width), F32)], nr, near_d,
+        in_hbm=1, scratch=[pltpu.SemaphoreType.DMA((1,))],
     )
     s, nr, c, msg = call(
         first_kernel, [vec] * 4, halo, near_s, s, small, maps, d_lo, d_hi, nr

time: 41.7 us -> 41.4 us (level)
  transfers between devices with their start and end apart: 6 -> 6, of which waited for: 3 -> 3; matrix products, arithmetic and copies ran while one was open for 0% -> 0% of each run, Pallas kernels for 8% -> 7%
where the time goes in v5:
time: 41.4 us; the launch traced here: 41.2 us
  starting transfers between devices  33 us (80%)
  Pallas kernels  4.45 us (11%)
  waiting for transfers between devices  3 us (7%)
  between operations  0.76 us (2%)
    ppermute x5, starting transfers between devices, swapped(): lax.ppermute(value, 'dom', [(i, i ^ distance) for i in range(lax.axis_siz...  30.3 us
    pallas_call x8, Pallas kernels, call(): pl.pallas_call(kernel, out_shape=[jax.ShapeDtypeStruct(s, d) for s, d in...  4.45 us
    ppermute x1, starting transfers between devices, per_device(): lax.ppermute(rows, 'tm', [(i, (i + 1) % segments) for i in range(segments)])  2.68 us
    ppermute x1, waiting for transfers between devices, per_device(): lax.ppermute(rows, 'tm', [(i, (i + 1) % segments) for i in range(segments)])  1.77 us
    ppermute x5, waiting for transfers between devices, swapped(): lax.ppermute(value, 'dom', [(i, i ^ distance) for i in range(lax.axis_siz...  1.23 us
  transfers between devices with their start and end apart: 6, of which 3 were waited for; matrix products, arithmetic and copies ran while one was open for 0% of the time, Pallas kernels for 7%

profile of v5, /device:TPU:0, one launch (start us, length us, event | category | flops | bytes accessed | tf_op | source)
XLA Modules:
  0.0 41.2 jit_solution(14064649337439510626)
XLA Ops:
  0.0 0.0 copy-start.8
  0.0 0.0 copy-start.1
  0.0 0.0 copy-start.5
  0.0 0.0 copy-start.6
  0.0 0.0 copy-start.7
  0.0 0.0 copy-start
  0.1 0.5 %collective-permute-start.11 = (f32[16,1,128]{2,0,1:T(8,128)}, f32[16,1,128]{2,0,1:T(8,128)S(1)}, u32[]{:S(2)}, u32[]{:S(2)}) collective-permute-start(f32[16,1,128]{2,0,1:T(8,128)} %bitcast.17), channel_id=1, source_target_pairs={{0,1},{1,0},{2,3},{3,2},{4,5},{5,4},{6,7},{7,6},{8,9},{9,8},{10,11... | collective-permute-start | bytes 24584 | tf_op jit(solution)/shard_map/ppermute | solution.py:521
  1.2 0.4 collective-permute-done.11
  1.6 0.0 copy-done.8
  1.6 0.3 collective-permute-start.14
  2.0 0.2 collective-permute-start.15
  2.1 0.0 copy-done.1
  2.1 0.0 copy-done.2
  2.1 0.0 copy-done.3
  2.2 0.0 copy-done.4
  2.2 0.0 copy-done.5
  2.2 0.0 copy-done.6
  2.2 0.0 copy-done.7
  2.2 0.4 collective-permute-start.13
  2.6 0.0 copy-done
  2.6 2.7 %collective-permute-start.12 = (f32[8,128]{1,0:T(8,128)S(1)}, f32[8,128]{1,0:T(8,128)S(1)}, u32[]{:S(2)}, u32[]{:S(2)}) collective-permute-start(f32[8,128]{1,0:T(8,128)S(1)} %shard_map.110), channel_id=1, source_target_pairs={{0,4},{4,8},{8,12},{12,16},{16,20},{20,24},{24,28},{28,0},{1,5},{5... | collective-permute-start | bytes 12296 | tf_op jit(solution)/shard_map/ppermute | solution.py:628
  5.3 0.0 collective-permute-done.14
  5.3 1.4 %shard_map.112 = (f32[256,128]{1,0:T(8,128)S(1)}, f32[16,128,128]{2,1,0:T(8,128)S(1)}) custom-call(f32[16,128,128]{2,1,0:T(8,128)S(1)} %bitcast.31, f32[16,128,128]{2,1,0:T(8,128)S(1)} %bitcast.29, f32[16,128,128]{2,1,0:T(8,128)} %bitcast.11.diag_ref), custom_call_target="tpu_custom_call" | custom-call | tf_op jit(solution)/shard_map/pallas_call | solution.py:79
  6.7 0.0 collective-permute-done.13.pack_lo
  6.7 0.2 shard_map.113
  6.9 0.0 collective-permute-done.15
  6.9 1.2 %shard_map.114.d_lo = f32[16,128,128]{2,1,0:T(8,128)S(1)} custom-call(f32[32,128]{1,0:T(8,128)S(1)} %get-tuple-element.105._.old_nr, f32[16,128,128]{2,1,0:T(8,128)} %bitcast.13.lo_ref), custom_call_target="tpu_custom_call" | custom-call | tf_op jit(solution)/shard_map/pallas_call | solution.py:79
  8.2 1.8 %collective-permute-done.12.halo_ref = f32[8,128]{1,0:T(8,128)S(1)} collective-permute-done((f32[8,128]{1,0:T(8,128)S(1)}, f32[8,128]{1,0:T(8,128)S(1)}, u32[]{:S(2)}, u32[]{:S(2)}) %collective-permute-start.12) | collective-permute-done | bytes 4128 | tf_op jit(solution)/shard_map/ppermute | solution.py:628
  9.9 1.0 %shard_map.115 = (f32[32,128]{1,0:T(8,128)S(1)}, f32[32,128]{1,0:T(8,128)S(1)}, f32[32,128]{1,0:T(8,128)S(1)}, f32[32,128]{1,0:T(8,128)S(1)}) custom-call(f32[8,128]{1,0:T(8,128)S(1)} %collective-permute-done.12.halo_ref, f32[16,128]{1,0:T(8,128)S(1)} %bitcast.23, f32[16,128]{1,0:T(8,128)S(1)} %bitcast.20, f32[80,128]{1,0:T(8,128)S(1)} %get-tuple-element.103.small_ref, ...), custom_call_target="tpu_custom_call" | custom-call | tf_op jit(solution)/shard_map/pallas_call | solution.py:79
  10.9 28.8 %collective-permute-start.16 = (f32[32,128]{1,0:T(8,128)S(1)}, f32[32,128]{1,0:T(8,128)S(1)}, u32[]{:S(2)}, u32[]{:S(2)}) collective-permute-start(f32[32,128]{1,0:T(8,128)S(1)} %get-tuple-element.111.both_ref), channel_id=1, source_target_pairs={{0,1},{1,0},{2,3},{3,2},{4,5},{5,4},{6,7},{7,6},{8,9},{9,8},{10,11... | collective-permute-start | bytes 49160 | tf_op jit(solution)/shard_map/ppermute | solution.py:521
  39.8 0.8 %collective-permute-done.16.got_ref = f32[32,128]{1,0:T(8,128)S(1)} collective-permute-done((f32[32,128]{1,0:T(8,128)S(1)}, f32[32,128]{1,0:T(8,128)S(1)}, u32[]{:S(2)}, u32[]{:S(2)}) %collective-permute-start.16) | collective-permute-done | bytes 16416 | tf_op jit(solution)/shard_map/ppermute | solution.py:521
  40.6 0.6 %shard_map.116 = f32[16,128]{1,0:T(8,128)} custom-call(f32[32,128]{1,0:T(8,128)S(1)} %get-tuple-element.111.both_ref, f32[32,128]{1,0:T(8,128)S(1)} %collective-permute-done.16.got_ref), custom_call_target="tpu_custom_call" | custom-call | tf_op jit(solution)/shard_map/pallas_call | solution.py:79
  (8 shorter events, 0.0 us)
Async XLA Ops:
  0.0 1.6 %copy-start.8 = (f32[16,1,1,128,128]{4,3,2,1,0:T(8,128)S(1)}, f32[16,1,1,128,128]{4,3,2,1,0:T(8,128)}, u32[]{:S(2)}) copy-start(f32[16,1,1,128,128]{4,3,2,1,0:T(8,128)} %param.23) | copy-start | bytes 3145732
  0.0 2.1 %copy-start.1 = (f32[1,128,128]{2,1,0:T(8,128)S(1)}, f32[1,128,128]{2,1,0:T(8,128)}, u32[]{:S(2)}) copy-start(f32[1,128,128]{2,1,0:T(8,128)} %param.16) | copy-start | bytes 196612
  0.0 2.1 %copy-start.2 = (f32[1,128,128]{2,1,0:T(8,128)S(1)}, f32[1,128,128]{2,1,0:T(8,128)}, u32[]{:S(2)}) copy-start(f32[1,128,128]{2,1,0:T(8,128)} %param.19) | copy-start | bytes 196612
  0.0 2.1 %copy-start.3 = (f32[1,128,128]{2,1,0:T(8,128)S(1)}, f32[1,128,128]{2,1,0:T(8,128)}, u32[]{:S(2)}) copy-start(f32[1,128,128]{2,1,0:T(8,128)} %param.22) | copy-start | bytes 196612
  0.0 2.1 %copy-start.4 = (f32[16,1,128]{2,1,0:T(1,128)S(1)}, f32[16,1,128]{2,1,0:T(1,128)}, u32[]{:S(2)}) copy-start(f32[16,1,128]{2,1,0:T(1,128)} %param.14) | copy-start | bytes 24580
  0.0 2.1 %copy-start.5 = (f32[1,128]{1,0:T(1,128)S(1)}, f32[1,128]{1,0:T(1,128)}, u32[]{:S(2)}) copy-start(f32[1,128]{1,0:T(1,128)} %cap_ref.1) | copy-start | bytes 1540
  0.0 2.1 %copy-start.6 = (f32[1,128]{1,0:T(1,128)S(1)}, f32[1,128]{1,0:T(1,128)}, u32[]{:S(2)}) copy-start(f32[1,128]{1,0:T(1,128)} %gain_ref.1) | copy-start | bytes 1540
  0.0 2.1 %copy-start.7 = (s32[1,128]{1,0:T(1,128)S(1)}, s32[1,128]{1,0:T(1,128)}, u32[]{:S(2)}) copy-start(s32[1,128]{1,0:T(1,128)} %bnd_ref.1) | copy-start | bytes 1540
  0.0 2.6 %copy-start = (f32[16,1,128]{2,1,0:T(1,128)S(1)}, f32[16,1,128]{2,1,0:T(1,128)}, u32[]{:S(2)}) copy-start(f32[16,1,128]{2,1,0:T(1,128)} %param.13) | copy-start | bytes 24580
  0.1 1.6 %collective-permute-start.11 = (f32[16,1,128]{2,0,1:T(8,128)}, f32[16,1,128]{2,0,1:T(8,128)S(1)}, u32[]{:S(2)}, u32[]{:S(2)}) collective-permute-start(f32[16,1,128]{2,0,1:T(8,128)} %bitcast.17), channel_id=1, source_target_pairs={{0,1},{1,0},{2,3},{3,2},{4,5},{5,4},{6,7},{7,6},{8,9},{9,8},{10,11... | collective-permute-start | bytes 24584 | tf_op jit(solution)/shard_map/ppermute | solution.py:521
  1.6 3.7 %collective-permute-start.14 = (f32[16,1,1,128,128]{4,3,0,2,1:T(8,128)S(1)}, f32[16,1,1,128,128]{4,3,0,2,1:T(8,128)S(1)}, u32[]{:S(2)}, u32[]{:S(2)}) collective-permute-start(f32[16,1,1,128,128]{4,3,0,2,1:T(8,128)S(1)} %bitcast.28), channel_id=1, source_target_pairs={{0,1},{1,0},{2,3},{3,2},{4,5},{5,4},{6,7},{7,6},{8,9},{9,8},{10,11... | collective-permute-start | bytes 3145736 | tf_op jit(solution)/shard_map/ppermute | solution.py:521
  2.0 4.9 %collective-permute-start.15 = (f32[16,1,1,128,128]{4,3,0,2,1:T(8,128)}, f32[16,1,1,128,128]{4,3,0,2,1:T(8,128)}, u32[]{:S(2)}, u32[]{:S(2)}) collective-permute-start(f32[16,1,1,128,128]{4,3,0,2,1:T(8,128)} %bitcast.12), channel_id=1, source_target_pairs={{0,1},{1,0},{2,3},{3,2},{4,5},{5,4},{6,7},{7,6},{8,9},{9,8},{10,11... | collective-permute-start | bytes 3145736 | tf_op jit(solution)/shard_map/ppermute | solution.py:521
  2.2 4.5 %collective-permute-start.13 = (f32[424,128]{1,0:T(8,128)S(1)}, f32[424,128]{1,0:T(8,128)S(1)}, u32[]{:S(2)}, u32[]{:S(2)}) collective-permute-start(f32[424,128]{1,0:T(8,128)S(1)} %shard_map.111.pack_hi), channel_id=1, source_target_pairs={{0,1},{1,0},{2,3},{3,2},{4,5},{5,4},{6,7},{7,6},{8,9},{9,8},{10,11... | collective-permute-start | bytes 651272 | tf_op jit(solution)/shard_map/ppermute | solution.py:521
  2.6 7.3 %collective-permute-start.12 = (f32[8,128]{1,0:T(8,128)S(1)}, f32[8,128]{1,0:T(8,128)S(1)}, u32[]{:S(2)}, u32[]{:S(2)}) collective-permute-start(f32[8,128]{1,0:T(8,128)S(1)} %shard_map.110), channel_id=1, source_target_pairs={{0,4},{4,8},{8,12},{12,16},{16,20},{20,24},{24,28},{28,0},{1,5},{5... | collective-permute-start | bytes 12296 | tf_op jit(solution)/shard_map/ppermute | solution.py:628
  10.9 29.7 %collective-permute-start.16 = (f32[32,128]{1,0:T(8,128)S(1)}, f32[32,128]{1,0:T(8,128)S(1)}, u32[]{:S(2)}, u32[]{:S(2)}) collective-permute-start(f32[32,128]{1,0:T(8,128)S(1)} %get-tuple-element.111.both_ref), channel_id=1, source_target_pairs={{0,1},{1,0},{2,3},{3,2},{4,5},{5,4},{6,7},{7,6},{8,9},{9,8},{10,11... | collective-permute-start | bytes 49160 | tf_op jit(solution)/shard_map/ppermute | solution.py:521

commit v6 on v5

--- a/solution.py
+++ b/solution.py
@@ -48,6 +48,10 @@
 
 
 def mapped_each(matrices, vectors):
+    if isinstance(matrices, tuple):
+        half = vectors.shape[0] // 2
+        near = mapped_each(matrices[0], vectors[:half])
+        return jnp.concatenate([near, mapped_each_split(matrices[1], vectors[half:])], axis=0)
     rows = []
     for r in range(vectors.shape[0]):
         products = matrices[r] * vectors[r : r + 1, :]
@@ -173,7 +177,7 @@
         move.wait()
 
 
-def prefix_kernel(r_lo, r_hi, p_lo, l_lo, p_hi, l_hi):
+def prefix_kernel(r_lo, r_hi, d_lo, d_hi, p_lo, l_lo, p_hi, l_hi, ds_lo, ds_hi):
     points, width = r_lo.shape[0], r_lo.shape[1]
     both = [[r_ref[i] for i in range(points)] for r_ref in (r_lo, r_hi)]
     span, slot = 1, 0
@@ -195,6 +199,10 @@
     for i in range(points):
         p_lo[i] = both[0][i]
         p_hi[i * width : (i + 1) * width] = split_cols(both[1][i])
+    for i in range(points // 2):
+        rows = slice(i * width, (i + 1) * width)
+        ds_lo[rows] = split_cols(d_lo[points // 2 + i])
+        ds_hi[rows] = split_cols(d_hi[points // 2 + i])
 
 
 def scanned(c, l_ref):
@@ -325,8 +333,11 @@
 
 
 def second_kernel(
-    got_ref, s_ref, nr_ref, c_ref, small_ref, maps_ref, d_lo, d_hi, ss_ref, new_c_ref, f_ref
-):
+    got_ref, s_ref, nr_ref, c_ref, small_ref, maps_ref, d_lo, d_hi, ss_ref, *refs
+):
+    new_c_ref, f_ref = refs[-2:]
+    if len(refs) == 4:
+        d_lo, d_hi = (d_lo, refs[0][...]), (d_hi, refs[1][...])
     points, width = got_ref.shape[0] // 2, got_ref.shape[1]
     second_pair = lax.axis_index("dom") >= PAIR
 
@@ -445,7 +456,7 @@
 
 def turn_kernel(
     v_ref, gw_ref, gf_ref, bw_ref, bf_ref, p_lo, p_hi, base_ref, halo_ref, small_ref, maps_ref,
-    d_lo, d_hi, s_ref, nr_ref, c_ref, msg_ref,
+    d_lo, d_hi, ds_lo, ds_hi, s_ref, nr_ref, c_ref, msg_ref,
 ):
     points, width = s_ref.shape[0] // PAIR, s_ref.shape[1]
     came = []
@@ -463,7 +474,7 @@
         s[:points], s[points:],
         halo_ref[:1] + came[0][points : points + 1],
         halo_ref[4:5] + came[1][points : points + 1],
-        small_ref, maps_ref, d_lo, d_hi, nr_ref, c_ref, msg_ref,
+        small_ref, maps_ref, (d_lo, ds_lo[...]), (d_hi, ds_hi[...]), nr_ref, c_ref, msg_ref,
     )
 
 
@@ -552,11 +563,12 @@
         suffix_kernel, [many] + [((points, width, width), F32)] * 2, r_lo, r_hi, d_lo, d_hi,
         in_hbm=2, scratch=[pltpu.SemaphoreType.DMA((2,))],
     )
-    p_lo, l_lo, p_hi, l_hi = call(
+    p_lo, l_lo, p_hi, l_hi, ds_lo, ds_hi = call(
         prefix_kernel,
         [((points, width, width), F32), ((steps, width, width), F32)]
-        + [((points * width, 2 * width), BF16), ((steps * width, 2 * width), BF16)],
-        r_lo, r_hi,
+        + [((points * width, 2 * width), BF16), ((steps * width, 2 * width), BF16)]
+        + [((points // 2 * width, 2 * width), BF16)] * 2,
+        r_lo, r_hi, d_lo, d_hi,
     )
     c, f = call(
         second_kernel, [vec, eight], got, s, nr, c, small, maps, d_lo, d_hi, ss
@@ -582,11 +594,11 @@
     base, v = call(local_kernel, [vec, longer], c, l_lo, l_hi, tail, aw, af, s)
     s, nr, c, msg = call(
         turn_kernel, [vec] * 4,
-        v, last, got, bw, bf, p_lo, p_hi, base, halo, small, maps, d_lo, d_hi,
+        v, last, got, bw, bf, p_lo, p_hi, base, halo, small, maps, d_lo, d_hi, ds_lo, ds_hi,
     )
     got = swapped(msg, 2)
     c, f = call(
-        second_kernel, [vec, eight], got, s, nr, c, small, maps, d_lo, d_hi, ss
+        second_kernel, [vec, eight], got, s, nr, c, small, maps, d_lo, d_hi, ss, ds_lo, ds_hi
     )
     (tail,) = call(tail_kernel, [longer], c, ss)
     (base,) = call(scan_kernel, [vec], c, l_lo, l_hi, s)

time: 41.4 us -> 41.3 us (level)
  no operation moved by 1% of the time
where the time goes in v6:
time: 41.3 us; the launch traced here: 41.1 us
  starting transfers between devices  32.8 us (79%)
  Pallas kernels  4.45 us (11%)
  waiting for transfers between devices  3 us (7%)
  between operations  0.76 us (2%)
    ppermute x5, starting transfers between devices, swapped(): lax.ppermute(value, 'dom', [(i, i ^ distance) for i in range(lax.axis_siz...  30.1 us
    pallas_call x8, Pallas kernels, call(): pl.pallas_call(kernel, out_shape=[jax.ShapeDtypeStruct(s, d) for s, d in...  4.45 us
    ppermute x1, starting transfers between devices, per_device(): lax.ppermute(rows, 'tm', [(i, (i + 1) % segments) for i in range(segments)])  2.68 us
    ppermute x1, waiting for transfers between devices, per_device(): lax.ppermute(rows, 'tm', [(i, (i + 1) % segments) for i in range(segments)])  1.77 us
    ppermute x5, waiting for transfers between devices, swapped(): lax.ppermute(value, 'dom', [(i, i ^ distance) for i in range(lax.axis_siz...  1.23 us
  transfers between devices with their start and end apart: 6, of which 3 were waited for; matrix products, arithmetic and copies ran while one was open for 0% of the time, Pallas kernels for 7%

profile of v6, /device:TPU:0, one launch (start us, length us, event | category | flops | bytes accessed | tf_op | source)
XLA Modules:
  0.0 41.1 jit_solution(3910929580850862446)
XLA Ops:
  0.0 0.0 copy-start.8
  0.0 0.0 copy-start.1
  0.0 0.0 copy-start.5
  0.0 0.0 copy-start.6
  0.0 0.0 copy-start.7
  0.0 0.0 copy-start
  0.1 0.5 %collective-permute-start.11 = (f32[16,1,128]{2,0,1:T(8,128)}, f32[16,1,128]{2,0,1:T(8,128)S(1)}, u32[]{:S(2)}, u32[]{:S(2)}) collective-permute-start(f32[16,1,128]{2,0,1:T(8,128)} %bitcast.17), channel_id=1, source_target_pairs={{0,1},{1,0},{2,3},{3,2},{4,5},{5,4},{6,7},{7,6},{8,9},{9,8},{10,11... | collective-permute-start | bytes 24584 | tf_op jit(solution)/shard_map/ppermute | solution.py:532
  1.2 0.4 collective-permute-done.11
  1.6 0.0 copy-done.8
  1.6 0.3 collective-permute-start.14
  2.0 0.2 collective-permute-start.15
  2.1 0.0 copy-done.1
  2.1 0.0 copy-done.2
  2.1 0.0 copy-done.3
  2.2 0.0 copy-done.4
  2.2 0.0 copy-done.5
  2.2 0.0 copy-done.6
  2.2 0.0 copy-done.7
  2.2 0.4 collective-permute-start.13
  2.6 0.0 copy-done
  2.6 2.7 %collective-permute-start.12 = (f32[8,128]{1,0:T(8,128)S(1)}, f32[8,128]{1,0:T(8,128)S(1)}, u32[]{:S(2)}, u32[]{:S(2)}) collective-permute-start(f32[8,128]{1,0:T(8,128)S(1)} %shard_map.110), channel_id=1, source_target_pairs={{0,4},{4,8},{8,12},{12,16},{16,20},{20,24},{24,28},{28,0},{1,5},{5... | collective-permute-start | bytes 12296 | tf_op jit(solution)/shard_map/ppermute | solution.py:640
  5.3 0.0 collective-permute-done.14
  5.3 1.4 %shard_map.112 = (f32[256,128]{1,0:T(8,128)S(1)}, f32[16,128,128]{2,1,0:T(8,128)S(1)}) custom-call(f32[16,128,128]{2,1,0:T(8,128)S(1)} %bitcast.31, f32[16,128,128]{2,1,0:T(8,128)S(1)} %bitcast.29, f32[16,128,128]{2,1,0:T(8,128)} %bitcast.11.diag_ref), custom_call_target="tpu_custom_call" | custom-call | tf_op jit(solution)/shard_map/pallas_call | solution.py:83
  6.7 0.0 collective-permute-done.13.pack_lo
  6.7 0.2 shard_map.113
  6.9 0.0 collective-permute-done.15
  6.9 1.2 %shard_map.114.d_lo = f32[16,128,128]{2,1,0:T(8,128)S(1)} custom-call(f32[32,128]{1,0:T(8,128)S(1)} %get-tuple-element.107._.old_nr, f32[16,128,128]{2,1,0:T(8,128)} %bitcast.13.lo_ref), custom_call_target="tpu_custom_call" | custom-call | tf_op jit(solution)/shard_map/pallas_call | solution.py:83
  8.2 1.8 %collective-permute-done.12.halo_ref = f32[8,128]{1,0:T(8,128)S(1)} collective-permute-done((f32[8,128]{1,0:T(8,128)S(1)}, f32[8,128]{1,0:T(8,128)S(1)}, u32[]{:S(2)}, u32[]{:S(2)}) %collective-permute-start.12) | collective-permute-done | bytes 4128 | tf_op jit(solution)/shard_map/ppermute | solution.py:640
  9.9 1.0 %shard_map.115 = (f32[32,128]{1,0:T(8,128)S(1)}, f32[32,128]{1,0:T(8,128)S(1)}, f32[32,128]{1,0:T(8,128)S(1)}, f32[32,128]{1,0:T(8,128)S(1)}) custom-call(f32[8,128]{1,0:T(8,128)S(1)} %collective-permute-done.12.halo_ref, f32[16,128]{1,0:T(8,128)S(1)} %bitcast.23, f32[16,128]{1,0:T(8,128)S(1)} %bitcast.20, f32[80,128]{1,0:T(8,128)S(1)} %get-tuple-element.105.small_ref, ...), custom_call_target="tpu_custom_call" | custom-call | tf_op jit(solution)/shard_map/pallas_call | solution.py:83
  10.9 28.7 %collective-permute-start.16 = (f32[32,128]{1,0:T(8,128)S(1)}, f32[32,128]{1,0:T(8,128)S(1)}, u32[]{:S(2)}, u32[]{:S(2)}) collective-permute-start(f32[32,128]{1,0:T(8,128)S(1)} %get-tuple-element.113.both_ref), channel_id=1, source_target_pairs={{0,1},{1,0},{2,3},{3,2},{4,5},{5,4},{6,7},{7,6},{8,9},{9,8},{10,11... | collective-permute-start | bytes 49160 | tf_op jit(solution)/shard_map/ppermute | solution.py:532
  39.6 0.8 %collective-permute-done.16.got_ref = f32[32,128]{1,0:T(8,128)S(1)} collective-permute-done((f32[32,128]{1,0:T(8,128)S(1)}, f32[32,128]{1,0:T(8,128)S(1)}, u32[]{:S(2)}, u32[]{:S(2)}) %collective-permute-start.16) | collective-permute-done | bytes 16416 | tf_op jit(solution)/shard_map/ppermute | solution.py:532
  40.5 0.6 %shard_map.116 = f32[16,128]{1,0:T(8,128)} custom-call(f32[32,128]{1,0:T(8,128)S(1)} %get-tuple-element.113.both_ref, f32[32,128]{1,0:T(8,128)S(1)} %collective-permute-done.16.got_ref), custom_call_target="tpu_custom_call" | custom-call | tf_op jit(solution)/shard_map/pallas_call | solution.py:83
  (8 shorter events, 0.0 us)
Async XLA Ops:
  0.0 1.6 %copy-start.8 = (f32[16,1,1,128,128]{4,3,2,1,0:T(8,128)S(1)}, f32[16,1,1,128,128]{4,3,2,1,0:T(8,128)}, u32[]{:S(2)}) copy-start(f32[16,1,1,128,128]{4,3,2,1,0:T(8,128)} %param.23) | copy-start | bytes 3145732
  0.0 2.1 %copy-start.1 = (f32[1,128,128]{2,1,0:T(8,128)S(1)}, f32[1,128,128]{2,1,0:T(8,128)}, u32[]{:S(2)}) copy-start(f32[1,128,128]{2,1,0:T(8,128)} %param.16) | copy-start | bytes 196612
  0.0 2.1 %copy-start.2 = (f32[1,128,128]{2,1,0:T(8,128)S(1)}, f32[1,128,128]{2,1,0:T(8,128)}, u32[]{:S(2)}) copy-start(f32[1,128,128]{2,1,0:T(8,128)} %param.19) | copy-start | bytes 196612
  0.0 2.1 %copy-start.3 = (f32[1,128,128]{2,1,0:T(8,128)S(1)}, f32[1,128,128]{2,1,0:T(8,128)}, u32[]{:S(2)}) copy-start(f32[1,128,128]{2,1,0:T(8,128)} %param.22) | copy-start | bytes 196612
  0.0 2.1 %copy-start.4 = (f32[16,1,128]{2,1,0:T(1,128)S(1)}, f32[16,1,128]{2,1,0:T(1,128)}, u32[]{:S(2)}) copy-start(f32[16,1,128]{2,1,0:T(1,128)} %param.14) | copy-start | bytes 24580
  0.0 2.1 %copy-start.5 = (f32[1,128]{1,0:T(1,128)S(1)}, f32[1,128]{1,0:T(1,128)}, u32[]{:S(2)}) copy-start(f32[1,128]{1,0:T(1,128)} %cap_ref.1) | copy-start | bytes 1540
  0.0 2.1 %copy-start.6 = (f32[1,128]{1,0:T(1,128)S(1)}, f32[1,128]{1,0:T(1,128)}, u32[]{:S(2)}) copy-start(f32[1,128]{1,0:T(1,128)} %gain_ref.1) | copy-start | bytes 1540
  0.0 2.1 %copy-start.7 = (s32[1,128]{1,0:T(1,128)S(1)}, s32[1,128]{1,0:T(1,128)}, u32[]{:S(2)}) copy-start(s32[1,128]{1,0:T(1,128)} %bnd_ref.1) | copy-start | bytes 1540
  0.0 2.6 %copy-start = (f32[16,1,128]{2,1,0:T(1,128)S(1)}, f32[16,1,128]{2,1,0:T(1,128)}, u32[]{:S(2)}) copy-start(f32[16,1,128]{2,1,0:T(1,128)} %param.13) | copy-start | bytes 24580
  0.1 1.6 %collective-permute-start.11 = (f32[16,1,128]{2,0,1:T(8,128)}, f32[16,1,128]{2,0,1:T(8,128)S(1)}, u32[]{:S(2)}, u32[]{:S(2)}) collective-permute-start(f32[16,1,128]{2,0,1:T(8,128)} %bitcast.17), channel_id=1, source_target_pairs={{0,1},{1,0},{2,3},{3,2},{4,5},{5,4},{6,7},{7,6},{8,9},{9,8},{10,11... | collective-permute-start | bytes 24584 | tf_op jit(solution)/shard_map/ppermute | solution.py:532
  1.6 3.7 %collective-permute-start.14 = (f32[16,1,1,128,128]{4,3,0,2,1:T(8,128)S(1)}, f32[16,1,1,128,128]{4,3,0,2,1:T(8,128)S(1)}, u32[]{:S(2)}, u32[]{:S(2)}) collective-permute-start(f32[16,1,1,128,128]{4,3,0,2,1:T(8,128)S(1)} %bitcast.28), channel_id=1, source_target_pairs={{0,1},{1,0},{2,3},{3,2},{4,5},{5,4},{6,7},{7,6},{8,9},{9,8},{10,11... | collective-permute-start | bytes 3145736 | tf_op jit(solution)/shard_map/ppermute | solution.py:532
  2.0 4.9 %collective-permute-start.15 = (f32[16,1,1,128,128]{4,3,0,2,1:T(8,128)}, f32[16,1,1,128,128]{4,3,0,2,1:T(8,128)}, u32[]{:S(2)}, u32[]{:S(2)}) collective-permute-start(f32[16,1,1,128,128]{4,3,0,2,1:T(8,128)} %bitcast.12), channel_id=1, source_target_pairs={{0,1},{1,0},{2,3},{3,2},{4,5},{5,4},{6,7},{7,6},{8,9},{9,8},{10,11... | collective-permute-start | bytes 3145736 | tf_op jit(solution)/shard_map/ppermute | solution.py:532
  2.2 4.5 %collective-permute-start.13 = (f32[424,128]{1,0:T(8,128)S(1)}, f32[424,128]{1,0:T(8,128)S(1)}, u32[]{:S(2)}, u32[]{:S(2)}) collective-permute-start(f32[424,128]{1,0:T(8,128)S(1)} %shard_map.111.pack_hi), channel_id=1, source_target_pairs={{0,1},{1,0},{2,3},{3,2},{4,5},{5,4},{6,7},{7,6},{8,9},{9,8},{10,11... | collective-permute-start | bytes 651272 | tf_op jit(solution)/shard_map/ppermute | solution.py:532
  2.6 7.3 %collective-permute-start.12 = (f32[8,128]{1,0:T(8,128)S(1)}, f32[8,128]{1,0:T(8,128)S(1)}, u32[]{:S(2)}, u32[]{:S(2)}) collective-permute-start(f32[8,128]{1,0:T(8,128)S(1)} %shard_map.110), channel_id=1, source_target_pairs={{0,4},{4,8},{8,12},{12,16},{16,20},{20,24},{24,28},{28,0},{1,5},{5... | collective-permute-start | bytes 12296 | tf_op jit(solution)/shard_map/ppermute | solution.py:640
  10.9 29.5 %collective-permute-start.16 = (f32[32,128]{1,0:T(8,128)S(1)}, f32[32,128]{1,0:T(8,128)S(1)}, u32[]{:S(2)}, u32[]{:S(2)}) collective-permute-start(f32[32,128]{1,0:T(8,128)S(1)} %get-tuple-element.113.both_ref), channel_id=1, source_target_pairs={{0,1},{1,0},{2,3},{3,2},{4,5},{5,4},{6,7},{7,6},{8,9},{9,8},{10,11... | collective-permute-start | bytes 49160 | tf_op jit(solution)/shard_map/ppermute | solution.py:532

commit v7 on v6

--- a/solution.py
+++ b/solution.py
@@ -177,7 +177,7 @@
         move.wait()
 
 
-def prefix_kernel(r_lo, r_hi, d_lo, d_hi, p_lo, l_lo, p_hi, l_hi, ds_lo, ds_hi):
+def prefix_kernel(r_lo, r_hi, p_lo, l_lo, p_hi, l_hi):
     points, width = r_lo.shape[0], r_lo.shape[1]
     both = [[r_ref[i] for i in range(points)] for r_ref in (r_lo, r_hi)]
     span, slot = 1, 0
@@ -199,10 +199,6 @@
     for i in range(points):
         p_lo[i] = both[0][i]
         p_hi[i * width : (i + 1) * width] = split_cols(both[1][i])
-    for i in range(points // 2):
-        rows = slice(i * width, (i + 1) * width)
-        ds_lo[rows] = split_cols(d_lo[points // 2 + i])
-        ds_hi[rows] = split_cols(d_hi[points // 2 + i])
 
 
 def scanned(c, l_ref):
@@ -363,6 +359,15 @@
             rows = slice(g * points, (g + 1) * points)
             whole = mapped_sum(ss_ref[rows], c_ref[rows])
             f_ref[8 * g : 8 * g + 8] = jnp.broadcast_to(whole, (8, width))
+
+
+def tail_and_split_kernel(c_ref, ss_ref, d_lo, d_hi, tail_ref, ds_lo, ds_hi):
+    points, width = d_lo.shape[0], d_lo.shape[1]
+    for i in range(points // 2):
+        rows = slice(i * width, (i + 1) * width)
+        ds_lo[rows] = split_cols(d_lo[points // 2 + i])
+        ds_hi[rows] = split_cols(d_hi[points // 2 + i])
+    tail_kernel(c_ref, ss_ref, tail_ref)
 
 
 def tail_kernel(c_ref, ss_ref, tail_ref):
@@ -563,17 +568,19 @@
         suffix_kernel, [many] + [((points, width, width), F32)] * 2, r_lo, r_hi, d_lo, d_hi,
         in_hbm=2, scratch=[pltpu.SemaphoreType.DMA((2,))],
     )
-    p_lo, l_lo, p_hi, l_hi, ds_lo, ds_hi = call(
+    p_lo, l_lo, p_hi, l_hi = call(
         prefix_kernel,
         [((points, width, width), F32), ((steps, width, width), F32)]
-        + [((points * width, 2 * width), BF16), ((steps * width, 2 * width), BF16)]
-        + [((points // 2 * width, 2 * width), BF16)] * 2,
-        r_lo, r_hi, d_lo, d_hi,
+        + [((points * width, 2 * width), BF16), ((steps * width, 2 * width), BF16)],
+        r_lo, r_hi,
     )
     c, f = call(
         second_kernel, [vec, eight], got, s, nr, c, small, maps, d_lo, d_hi, ss
     )
-    (tail,) = call(tail_kernel, [longer], c, ss)
+    tail, ds_lo, ds_hi = call(
+        tail_and_split_kernel, [longer] + [((points // 2 * width, 2 * width), BF16)] * 2,
+        c, ss, d_lo, d_hi,
+    )
     kept, bf, af = [], None, None
     for level, distance in enumerate(distances[:-1]):
         if level == 0:

time: 41.3 us -> 41.2 us (level)
  no operation moved by 1% of the time
where the time goes in v7:
time: 41.2 us; the launch traced here: 41 us
  starting transfers between devices  32.7 us (79%)
  Pallas kernels  4.45 us (11%)
  waiting for transfers between devices  3 us (7%)
  between operations  0.76 us (2%)
    ppermute x5, starting transfers between devices, swapped(): lax.ppermute(value, 'dom', [(i, i ^ distance) for i in range(lax.axis_siz...  30.1 us
    pallas_call x8, Pallas kernels, call(): pl.pallas_call(kernel, out_shape=[jax.ShapeDtypeStruct(s, d) for s, d in...  4.45 us
    ppermute x1, starting transfers between devices, per_device(): lax.ppermute(rows, 'tm', [(i, (i + 1) % segments) for i in range(segments)])  2.68 us
    ppermute x1, waiting for transfers between devices, per_device(): lax.ppermute(rows, 'tm', [(i, (i + 1) % segments) for i in range(segments)])  1.77 us
    ppermute x5, waiting for transfers between devices, swapped(): lax.ppermute(value, 'dom', [(i, i ^ distance) for i in range(lax.axis_siz...  1.23 us
  transfers between devices with their start and end apart: 6, of which 3 were waited for; matrix products, arithmetic and copies ran while one was open for 0% of the time, Pallas kernels for 7%

profile of v7, /device:TPU:0, one launch (start us, length us, event | category | flops | bytes accessed | tf_op | source)
XLA Modules:
  0.0 41.0 jit_solution(1611914612050898481)
XLA Ops:
  0.0 0.0 copy-start.8
  0.0 0.0 copy-start.1
  0.0 0.0 copy-start.5
  0.0 0.0 copy-start.6
  0.0 0.0 copy-start.7
  0.0 0.0 copy-start
  0.1 0.5 %collective-permute-start.11 = (f32[16,1,128]{2,0,1:T(8,128)}, f32[16,1,128]{2,0,1:T(8,128)S(1)}, u32[]{:S(2)}, u32[]{:S(2)}) collective-permute-start(f32[16,1,128]{2,0,1:T(8,128)} %bitcast.17), channel_id=1, source_target_pairs={{0,1},{1,0},{2,3},{3,2},{4,5},{5,4},{6,7},{7,6},{8,9},{9,8},{10,11... | collective-permute-start | bytes 24584 | tf_op jit(solution)/shard_map/ppermute | solution.py:537
  1.2 0.4 collective-permute-done.11
  1.6 0.0 copy-done.8
  1.6 0.3 collective-permute-start.14
  2.0 0.2 collective-permute-start.15
  2.1 0.0 copy-done.1
  2.1 0.0 copy-done.2
  2.1 0.0 copy-done.3
  2.2 0.0 copy-done.4
  2.2 0.0 copy-done.5
  2.2 0.0 copy-done.6
  2.2 0.0 copy-done.7
  2.2 0.4 collective-permute-start.13
  2.6 0.0 copy-done
  2.6 2.7 %collective-permute-start.12 = (f32[8,128]{1,0:T(8,128)S(1)}, f32[8,128]{1,0:T(8,128)S(1)}, u32[]{:S(2)}, u32[]{:S(2)}) collective-permute-start(f32[8,128]{1,0:T(8,128)S(1)} %shard_map.110), channel_id=1, source_target_pairs={{0,4},{4,8},{8,12},{12,16},{16,20},{20,24},{24,28},{28,0},{1,5},{5... | collective-permute-start | bytes 12296 | tf_op jit(solution)/shard_map/ppermute | solution.py:647
  5.3 0.0 collective-permute-done.14
  5.3 1.4 %shard_map.112 = (f32[256,128]{1,0:T(8,128)S(1)}, f32[16,128,128]{2,1,0:T(8,128)S(1)}) custom-call(f32[16,128,128]{2,1,0:T(8,128)S(1)} %bitcast.31, f32[16,128,128]{2,1,0:T(8,128)S(1)} %bitcast.29, f32[16,128,128]{2,1,0:T(8,128)} %bitcast.11.diag_ref), custom_call_target="tpu_custom_call" | custom-call | tf_op jit(solution)/shard_map/pallas_call | solution.py:83
  6.7 0.0 collective-permute-done.13.pack_lo
  6.7 0.2 shard_map.113
  6.9 0.0 collective-permute-done.15
  6.9 1.2 %shard_map.114.d_lo = f32[16,128,128]{2,1,0:T(8,128)S(1)} custom-call(f32[32,128]{1,0:T(8,128)S(1)} %get-tuple-element.108._.old_nr, f32[16,128,128]{2,1,0:T(8,128)} %bitcast.13.lo_ref), custom_call_target="tpu_custom_call" | custom-call | tf_op jit(solution)/shard_map/pallas_call | solution.py:83
  8.2 1.8 %collective-permute-done.12.halo_ref = f32[8,128]{1,0:T(8,128)S(1)} collective-permute-done((f32[8,128]{1,0:T(8,128)S(1)}, f32[8,128]{1,0:T(8,128)S(1)}, u32[]{:S(2)}, u32[]{:S(2)}) %collective-permute-start.12) | collective-permute-done | bytes 4128 | tf_op jit(solution)/shard_map/ppermute | solution.py:647
  9.9 1.0 %shard_map.115 = (f32[32,128]{1,0:T(8,128)S(1)}, f32[32,128]{1,0:T(8,128)S(1)}, f32[32,128]{1,0:T(8,128)S(1)}, f32[32,128]{1,0:T(8,128)S(1)}) custom-call(f32[8,128]{1,0:T(8,128)S(1)} %collective-permute-done.12.halo_ref, f32[16,128]{1,0:T(8,128)S(1)} %bitcast.23, f32[16,128]{1,0:T(8,128)S(1)} %bitcast.20, f32[80,128]{1,0:T(8,128)S(1)} %get-tuple-element.106.small_ref, ...), custom_call_target="tpu_custom_call" | custom-call | tf_op jit(solution)/shard_map/pallas_call | solution.py:83
  10.9 28.6 %collective-permute-start.16 = (f32[32,128]{1,0:T(8,128)S(1)}, f32[32,128]{1,0:T(8,128)S(1)}, u32[]{:S(2)}, u32[]{:S(2)}) collective-permute-start(f32[32,128]{1,0:T(8,128)S(1)} %get-tuple-element.114.both_ref), channel_id=1, source_target_pairs={{0,1},{1,0},{2,3},{3,2},{4,5},{5,4},{6,7},{7,6},{8,9},{9,8},{10,11... | collective-permute-start | bytes 49160 | tf_op jit(solution)/shard_map/ppermute | solution.py:537
  39.5 0.8 %collective-permute-done.16.got_ref = f32[32,128]{1,0:T(8,128)S(1)} collective-permute-done((f32[32,128]{1,0:T(8,128)S(1)}, f32[32,128]{1,0:T(8,128)S(1)}, u32[]{:S(2)}, u32[]{:S(2)}) %collective-permute-start.16) | collective-permute-done | bytes 16416 | tf_op jit(solution)/shard_map/ppermute | solution.py:537
  40.4 0.6 %shard_map.116 = f32[16,128]{1,0:T(8,128)} custom-call(f32[32,128]{1,0:T(8,128)S(1)} %get-tuple-element.114.both_ref, f32[32,128]{1,0:T(8,128)S(1)} %collective-permute-done.16.got_ref), custom_call_target="tpu_custom_call" | custom-call | tf_op jit(solution)/shard_map/pallas_call | solution.py:83
  (8 shorter events, 0.0 us)
Async XLA Ops:
  0.0 1.6 %copy-start.8 = (f32[16,1,1,128,128]{4,3,2,1,0:T(8,128)S(1)}, f32[16,1,1,128,128]{4,3,2,1,0:T(8,128)}, u32[]{:S(2)}) copy-start(f32[16,1,1,128,128]{4,3,2,1,0:T(8,128)} %param.23) | copy-start | bytes 3145732
  0.0 2.1 %copy-start.1 = (f32[1,128,128]{2,1,0:T(8,128)S(1)}, f32[1,128,128]{2,1,0:T(8,128)}, u32[]{:S(2)}) copy-start(f32[1,128,128]{2,1,0:T(8,128)} %param.16) | copy-start | bytes 196612
  0.0 2.1 %copy-start.2 = (f32[1,128,128]{2,1,0:T(8,128)S(1)}, f32[1,128,128]{2,1,0:T(8,128)}, u32[]{:S(2)}) copy-start(f32[1,128,128]{2,1,0:T(8,128)} %param.19) | copy-start | bytes 196612
  0.0 2.1 %copy-start.3 = (f32[1,128,128]{2,1,0:T(8,128)S(1)}, f32[1,128,128]{2,1,0:T(8,128)}, u32[]{:S(2)}) copy-start(f32[1,128,128]{2,1,0:T(8,128)} %param.22) | copy-start | bytes 196612
  0.0 2.1 %copy-start.4 = (f32[16,1,128]{2,1,0:T(1,128)S(1)}, f32[16,1,128]{2,1,0:T(1,128)}, u32[]{:S(2)}) copy-start(f32[16,1,128]{2,1,0:T(1,128)} %param.14) | copy-start | bytes 24580
  0.0 2.1 %copy-start.5 = (f32[1,128]{1,0:T(1,128)S(1)}, f32[1,128]{1,0:T(1,128)}, u32[]{:S(2)}) copy-start(f32[1,128]{1,0:T(1,128)} %cap_ref.1) | copy-start | bytes 1540
  0.0 2.1 %copy-start.6 = (f32[1,128]{1,0:T(1,128)S(1)}, f32[1,128]{1,0:T(1,128)}, u32[]{:S(2)}) copy-start(f32[1,128]{1,0:T(1,128)} %gain_ref.1) | copy-start | bytes 1540
  0.0 2.1 %copy-start.7 = (s32[1,128]{1,0:T(1,128)S(1)}, s32[1,128]{1,0:T(1,128)}, u32[]{:S(2)}) copy-start(s32[1,128]{1,0:T(1,128)} %bnd_ref.1) | copy-start | bytes 1540
  0.0 2.6 %copy-start = (f32[16,1,128]{2,1,0:T(1,128)S(1)}, f32[16,1,128]{2,1,0:T(1,128)}, u32[]{:S(2)}) copy-start(f32[16,1,128]{2,1,0:T(1,128)} %param.13) | copy-start | bytes 24580
  0.1 1.6 %collective-permute-start.11 = (f32[16,1,128]{2,0,1:T(8,128)}, f32[16,1,128]{2,0,1:T(8,128)S(1)}, u32[]{:S(2)}, u32[]{:S(2)}) collective-permute-start(f32[16,1,128]{2,0,1:T(8,128)} %bitcast.17), channel_id=1, source_target_pairs={{0,1},{1,0},{2,3},{3,2},{4,5},{5,4},{6,7},{7,6},{8,9},{9,8},{10,11... | collective-permute-start | bytes 24584 | tf_op jit(solution)/shard_map/ppermute | solution.py:537
  1.6 3.7 %collective-permute-start.14 = (f32[16,1,1,128,128]{4,3,0,2,1:T(8,128)S(1)}, f32[16,1,1,128,128]{4,3,0,2,1:T(8,128)S(1)}, u32[]{:S(2)}, u32[]{:S(2)}) collective-permute-start(f32[16,1,1,128,128]{4,3,0,2,1:T(8,128)S(1)} %bitcast.28), channel_id=1, source_target_pairs={{0,1},{1,0},{2,3},{3,2},{4,5},{5,4},{6,7},{7,6},{8,9},{9,8},{10,11... | collective-permute-start | bytes 3145736 | tf_op jit(solution)/shard_map/ppermute | solution.py:537
  2.0 4.9 %collective-permute-start.15 = (f32[16,1,1,128,128]{4,3,0,2,1:T(8,128)}, f32[16,1,1,128,128]{4,3,0,2,1:T(8,128)}, u32[]{:S(2)}, u32[]{:S(2)}) collective-permute-start(f32[16,1,1,128,128]{4,3,0,2,1:T(8,128)} %bitcast.12), channel_id=1, source_target_pairs={{0,1},{1,0},{2,3},{3,2},{4,5},{5,4},{6,7},{7,6},{8,9},{9,8},{10,11... | collective-permute-start | bytes 3145736 | tf_op jit(solution)/shard_map/ppermute | solution.py:537
  2.2 4.5 %collective-permute-start.13 = (f32[424,128]{1,0:T(8,128)S(1)}, f32[424,128]{1,0:T(8,128)S(1)}, u32[]{:S(2)}, u32[]{:S(2)}) collective-permute-start(f32[424,128]{1,0:T(8,128)S(1)} %shard_map.111.pack_hi), channel_id=1, source_target_pairs={{0,1},{1,0},{2,3},{3,2},{4,5},{5,4},{6,7},{7,6},{8,9},{9,8},{10,11... | collective-permute-start | bytes 651272 | tf_op jit(solution)/shard_map/ppermute | solution.py:537
  2.6 7.3 %collective-permute-start.12 = (f32[8,128]{1,0:T(8,128)S(1)}, f32[8,128]{1,0:T(8,128)S(1)}, u32[]{:S(2)}, u32[]{:S(2)}) collective-permute-start(f32[8,128]{1,0:T(8,128)S(1)} %shard_map.110), channel_id=1, source_target_pairs={{0,4},{4,8},{8,12},{12,16},{16,20},{20,24},{24,28},{28,0},{1,5},{5... | collective-permute-start | bytes 12296 | tf_op jit(solution)/shard_map/ppermute | solution.py:647
  10.9 29.4 %collective-permute-start.16 = (f32[32,128]{1,0:T(8,128)S(1)}, f32[32,128]{1,0:T(8,128)S(1)}, u32[]{:S(2)}, u32[]{:S(2)}) collective-permute-start(f32[32,128]{1,0:T(8,128)S(1)} %get-tuple-element.114.both_ref), channel_id=1, source_target_pairs={{0,1},{1,0},{2,3},{3,2},{4,5},{5,4},{6,7},{7,6},{8,9},{9,8},{10,11... | collective-permute-start | bytes 49160 | tf_op jit(solution)/shard_map/ppermute | solution.py:537

commit v8 on v7

--- a/solution.py
+++ b/solution.py
@@ -291,8 +291,10 @@
 
 
 def diagonal_kernel(_, lo_ref, d_lo, sems):
-    for move in fetched((lo_ref,), (d_lo,), sems):
-        move.wait()
+    @pl.when(in_first_pair())
+    def _():
+        for move in fetched((lo_ref,), (d_lo,), sems):
+            move.wait()
 
 
 def in_first_pair():

time: 41.2 us -> 41.2 us (level)
  no operation moved by 1% of the time
where the time goes in v8:
time: 41.2 us; the launch traced here: 41 us
  starting transfers between devices  32.7 us (79%)
  Pallas kernels  4.45 us (11%)
  waiting for transfers between devices  3 us (7%)
  between operations  0.76 us (2%)
    ppermute x5, starting transfers between devices, swapped(): lax.ppermute(value, 'dom', [(i, i ^ distance) for i in range(lax.axis_siz...  30.1 us
    pallas_call x8, Pallas kernels, call(): pl.pallas_call(kernel, out_shape=[jax.ShapeDtypeStruct(s, d) for s, d in...  4.45 us
    ppermute x1, starting transfers between devices, per_device(): lax.ppermute(rows, 'tm', [(i, (i + 1) % segments) for i in range(segments)])  2.68 us
    ppermute x1, waiting for transfers between devices, per_device(): lax.ppermute(rows, 'tm', [(i, (i + 1) % segments) for i in range(segments)])  1.77 us
    ppermute x5, waiting for transfers between devices, swapped(): lax.ppermute(value, 'dom', [(i, i ^ distance) for i in range(lax.axis_siz...  1.23 us
  transfers between devices with their start and end apart: 6, of which 3 were waited for; matrix products, arithmetic and copies ran while one was open for 0% of the time, Pallas kernels for 7%

profile of v8, /device:TPU:0, one launch (start us, length us, event | category | flops | bytes accessed | tf_op | source)
XLA Modules:
  0.0 41.0 jit_solution(13780089968409781063)
XLA Ops:
  0.0 0.0 copy-start.8
  0.0 0.0 copy-start.1
  0.0 0.0 copy-start.5
  0.0 0.0 copy-start.6
  0.0 0.0 copy-start.7
  0.0 0.0 copy-start
  0.1 0.5 %collective-permute-start.11 = (f32[16,1,128]{2,0,1:T(8,128)}, f32[16,1,128]{2,0,1:T(8,128)S(1)}, u32[]{:S(2)}, u32[]{:S(2)}) collective-permute-start(f32[16,1,128]{2,0,1:T(8,128)} %bitcast.17), channel_id=1, source_target_pairs={{0,1},{1,0},{2,3},{3,2},{4,5},{5,4},{6,7},{7,6},{8,9},{9,8},{10,11... | collective-permute-start | bytes 24584 | tf_op jit(solution)/shard_map/ppermute | solution.py:539
  1.2 0.4 collective-permute-done.11
  1.6 0.0 copy-done.8
  1.6 0.3 collective-permute-start.14
  2.0 0.2 collective-permute-start.15
  2.1 0.0 copy-done.1
  2.1 0.0 copy-done.2
  2.1 0.0 copy-done.3
  2.2 0.0 copy-done.4
  2.2 0.0 copy-done.5
  2.2 0.0 copy-done.6
  2.2 0.0 copy-done.7
  2.2 0.4 collective-permute-start.13
  2.6 0.0 copy-done
  2.6 2.7 %collective-permute-start.12 = (f32[8,128]{1,0:T(8,128)S(1)}, f32[8,128]{1,0:T(8,128)S(1)}, u32[]{:S(2)}, u32[]{:S(2)}) collective-permute-start(f32[8,128]{1,0:T(8,128)S(1)} %shard_map.110), channel_id=1, source_target_pairs={{0,4},{4,8},{8,12},{12,16},{16,20},{20,24},{24,28},{28,0},{1,5},{5... | collective-permute-start | bytes 12296 | tf_op jit(solution)/shard_map/ppermute | solution.py:649
  5.3 0.0 collective-permute-done.14
  5.3 1.4 %shard_map.112 = (f32[256,128]{1,0:T(8,128)S(1)}, f32[16,128,128]{2,1,0:T(8,128)S(1)}) custom-call(f32[16,128,128]{2,1,0:T(8,128)S(1)} %bitcast.31, f32[16,128,128]{2,1,0:T(8,128)S(1)} %bitcast.29, f32[16,128,128]{2,1,0:T(8,128)} %bitcast.11.diag_ref), custom_call_target="tpu_custom_call" | custom-call | tf_op jit(solution)/shard_map/pallas_call | solution.py:83
  6.7 0.0 collective-permute-done.13.pack_lo
  6.7 0.2 shard_map.113
  6.9 0.0 collective-permute-done.15
  6.9 1.2 %shard_map.114.d_lo = f32[16,128,128]{2,1,0:T(8,128)S(1)} custom-call(f32[32,128]{1,0:T(8,128)S(1)} %get-tuple-element.108._.old_nr, f32[16,128,128]{2,1,0:T(8,128)} %bitcast.13.lo_ref), custom_call_target="tpu_custom_call" | custom-call | tf_op jit(solution)/shard_map/pallas_call | solution.py:83
  8.2 1.8 %collective-permute-done.12.halo_ref = f32[8,128]{1,0:T(8,128)S(1)} collective-permute-done((f32[8,128]{1,0:T(8,128)S(1)}, f32[8,128]{1,0:T(8,128)S(1)}, u32[]{:S(2)}, u32[]{:S(2)}) %collective-permute-start.12) | collective-permute-done | bytes 4128 | tf_op jit(solution)/shard_map/ppermute | solution.py:649
  9.9 1.0 %shard_map.115 = (f32[32,128]{1,0:T(8,128)S(1)}, f32[32,128]{1,0:T(8,128)S(1)}, f32[32,128]{1,0:T(8,128)S(1)}, f32[32,128]{1,0:T(8,128)S(1)}) custom-call(f32[8,128]{1,0:T(8,128)S(1)} %collective-permute-done.12.halo_ref, f32[16,128]{1,0:T(8,128)S(1)} %bitcast.23, f32[16,128]{1,0:T(8,128)S(1)} %bitcast.20, f32[80,128]{1,0:T(8,128)S(1)} %get-tuple-element.106.small_ref, ...), custom_call_target="tpu_custom_call" | custom-call | tf_op jit(solution)/shard_map/pallas_call | solution.py:83
  10.9 28.6 %collective-permute-start.16 = (f32[32,128]{1,0:T(8,128)S(1)}, f32[32,128]{1,0:T(8,128)S(1)}, u32[]{:S(2)}, u32[]{:S(2)}) collective-permute-start(f32[32,128]{1,0:T(8,128)S(1)} %get-tuple-element.114.both_ref), channel_id=1, source_target_pairs={{0,1},{1,0},{2,3},{3,2},{4,5},{5,4},{6,7},{7,6},{8,9},{9,8},{10,11... | collective-permute-start | bytes 49160 | tf_op jit(solution)/shard_map/ppermute | solution.py:539
  39.5 0.8 %collective-permute-done.16.got_ref = f32[32,128]{1,0:T(8,128)S(1)} collective-permute-done((f32[32,128]{1,0:T(8,128)S(1)}, f32[32,128]{1,0:T(8,128)S(1)}, u32[]{:S(2)}, u32[]{:S(2)}) %collective-permute-start.16) | collective-permute-done | bytes 16416 | tf_op jit(solution)/shard_map/ppermute | solution.py:539
  40.4 0.6 %shard_map.116 = f32[16,128]{1,0:T(8,128)} custom-call(f32[32,128]{1,0:T(8,128)S(1)} %get-tuple-element.114.both_ref, f32[32,128]{1,0:T(8,128)S(1)} %collective-permute-done.16.got_ref), custom_call_target="tpu_custom_call" | custom-call | tf_op jit(solution)/shard_map/pallas_call | solution.py:83
  (8 shorter events, 0.0 us)
Async XLA Ops:
  0.0 1.6 %copy-start.8 = (f32[16,1,1,128,128]{4,3,2,1,0:T(8,128)S(1)}, f32[16,1,1,128,128]{4,3,2,1,0:T(8,128)}, u32[]{:S(2)}) copy-start(f32[16,1,1,128,128]{4,3,2,1,0:T(8,128)} %param.23) | copy-start | bytes 3145732
  0.0 2.1 %copy-start.1 = (f32[1,128,128]{2,1,0:T(8,128)S(1)}, f32[1,128,128]{2,1,0:T(8,128)}, u32[]{:S(2)}) copy-start(f32[1,128,128]{2,1,0:T(8,128)} %param.16) | copy-start | bytes 196612
  0.0 2.1 %copy-start.2 = (f32[1,128,128]{2,1,0:T(8,128)S(1)}, f32[1,128,128]{2,1,0:T(8,128)}, u32[]{:S(2)}) copy-start(f32[1,128,128]{2,1,0:T(8,128)} %param.19) | copy-start | bytes 196612
  0.0 2.1 %copy-start.3 = (f32[1,128,128]{2,1,0:T(8,128)S(1)}, f32[1,128,128]{2,1,0:T(8,128)}, u32[]{:S(2)}) copy-start(f32[1,128,128]{2,1,0:T(8,128)} %param.22) | copy-start | bytes 196612
  0.0 2.1 %copy-start.4 = (f32[16,1,128]{2,1,0:T(1,128)S(1)}, f32[16,1,128]{2,1,0:T(1,128)}, u32[]{:S(2)}) copy-start(f32[16,1,128]{2,1,0:T(1,128)} %param.14) | copy-start | bytes 24580
  0.0 2.1 %copy-start.5 = (f32[1,128]{1,0:T(1,128)S(1)}, f32[1,128]{1,0:T(1,128)}, u32[]{:S(2)}) copy-start(f32[1,128]{1,0:T(1,128)} %cap_ref.1) | copy-start | bytes 1540
  0.0 2.1 %copy-start.6 = (f32[1,128]{1,0:T(1,128)S(1)}, f32[1,128]{1,0:T(1,128)}, u32[]{:S(2)}) copy-start(f32[1,128]{1,0:T(1,128)} %gain_ref.1) | copy-start | bytes 1540
  0.0 2.1 %copy-start.7 = (s32[1,128]{1,0:T(1,128)S(1)}, s32[1,128]{1,0:T(1,128)}, u32[]{:S(2)}) copy-start(s32[1,128]{1,0:T(1,128)} %bnd_ref.1) | copy-start | bytes 1540
  0.0 2.6 %copy-start = (f32[16,1,128]{2,1,0:T(1,128)S(1)}, f32[16,1,128]{2,1,0:T(1,128)}, u32[]{:S(2)}) copy-start(f32[16,1,128]{2,1,0:T(1,128)} %param.13) | copy-start | bytes 24580
  0.1 1.6 %collective-permute-start.11 = (f32[16,1,128]{2,0,1:T(8,128)}, f32[16,1,128]{2,0,1:T(8,128)S(1)}, u32[]{:S(2)}, u32[]{:S(2)}) collective-permute-start(f32[16,1,128]{2,0,1:T(8,128)} %bitcast.17), channel_id=1, source_target_pairs={{0,1},{1,0},{2,3},{3,2},{4,5},{5,4},{6,7},{7,6},{8,9},{9,8},{10,11... | collective-permute-start | bytes 24584 | tf_op jit(solution)/shard_map/ppermute | solution.py:539
  1.6 3.7 %collective-permute-start.14 = (f32[16,1,1,128,128]{4,3,0,2,1:T(8,128)S(1)}, f32[16,1,1,128,128]{4,3,0,2,1:T(8,128)S(1)}, u32[]{:S(2)}, u32[]{:S(2)}) collective-permute-start(f32[16,1,1,128,128]{4,3,0,2,1:T(8,128)S(1)} %bitcast.28), channel_id=1, source_target_pairs={{0,1},{1,0},{2,3},{3,2},{4,5},{5,4},{6,7},{7,6},{8,9},{9,8},{10,11... | collective-permute-start | bytes 3145736 | tf_op jit(solution)/shard_map/ppermute | solution.py:539
  2.0 4.9 %collective-permute-start.15 = (f32[16,1,1,128,128]{4,3,0,2,1:T(8,128)}, f32[16,1,1,128,128]{4,3,0,2,1:T(8,128)}, u32[]{:S(2)}, u32[]{:S(2)}) collective-permute-start(f32[16,1,1,128,128]{4,3,0,2,1:T(8,128)} %bitcast.12), channel_id=1, source_target_pairs={{0,1},{1,0},{2,3},{3,2},{4,5},{5,4},{6,7},{7,6},{8,9},{9,8},{10,11... | collective-permute-start | bytes 3145736 | tf_op jit(solution)/shard_map/ppermute | solution.py:539
  2.2 4.5 %collective-permute-start.13 = (f32[424,128]{1,0:T(8,128)S(1)}, f32[424,128]{1,0:T(8,128)S(1)}, u32[]{:S(2)}, u32[]{:S(2)}) collective-permute-start(f32[424,128]{1,0:T(8,128)S(1)} %shard_map.111.pack_hi), channel_id=1, source_target_pairs={{0,1},{1,0},{2,3},{3,2},{4,5},{5,4},{6,7},{7,6},{8,9},{9,8},{10,11... | collective-permute-start | bytes 651272 | tf_op jit(solution)/shard_map/ppermute | solution.py:539
  2.6 7.3 %collective-permute-start.12 = (f32[8,128]{1,0:T(8,128)S(1)}, f32[8,128]{1,0:T(8,128)S(1)}, u32[]{:S(2)}, u32[]{:S(2)}) collective-permute-start(f32[8,128]{1,0:T(8,128)S(1)} %shard_map.110), channel_id=1, source_target_pairs={{0,4},{4,8},{8,12},{12,16},{16,20},{20,24},{24,28},{28,0},{1,5},{5... | collective-permute-start | bytes 12296 | tf_op jit(solution)/shard_map/ppermute | solution.py:649
  10.9 29.4 %collective-permute-start.16 = (f32[32,128]{1,0:T(8,128)S(1)}, f32[32,128]{1,0:T(8,128)S(1)}, u32[]{:S(2)}, u32[]{:S(2)}) collective-permute-start(f32[32,128]{1,0:T(8,128)S(1)} %get-tuple-element.114.both_ref), channel_id=1, source_target_pairs={{0,1},{1,0},{2,3},{3,2},{4,5},{5,4},{6,7},{7,6},{8,9},{9,8},{10,11... | collective-permute-start | bytes 49160 | tf_op jit(solution)/shard_map/ppermute | solution.py:539
